TPU v7x, 32 devices: a whole 2x2x4 slice. The times are simulated.
32 devices in a mesh: dp: 4 (over x, core), ctx: 8 (over z, y).
Axes of the slice: x: 2, y: 2, z: 4, core: 2. Of those that a mesh axis runs over, the one named last changes fastest.
Arguments:
- queries: bfloat16 [4, 2048, 512], P('dp', 'ctx'), may hold values from -40 to 40
- key_rows: bfloat16 [4, 2048, 512], P('dp', 'ctx'), may hold values from -40 to 40
- value_rows: bfloat16 [4, 2048, 512], P('dp', 'ctx'), may hold values from -24 to 24
- out_weight: bfloat16 [512, 1024], P('dp'), may hold values from -0.5 to 0.5
- head_weight: bfloat16 [1024, 1024], P('dp'), may hold values from -1.1953125 to 1.1953125
- conv_weight: float32 [9, 1024], replicated, may hold values from -3 to 3
- lengths: int32 [4], P('dp'), may hold values from 1 to 2048, 2730 in all
- label_mask: int32 [4, 2048], P('dp', 'ctx'), may hold values 0 or 1
- targets: int32 [4, 2048], P('dp', 'ctx'), may hold values from 0 to 1023
Outputs:
- loss: float32 [], replicated
- d_queries: bfloat16 [4, 2048, 512], P('dp', 'ctx')
- d_keys: bfloat16 [4, 2048, 512], P('dp', 'ctx')
- d_values: bfloat16 [4, 2048, 512], P('dp', 'ctx')
- d_conv: float32 [9, 1024], replicated
Inputs may be any that keep to these rules, and one draw needn't show every extreme that they name: `lengths`: the longest recording has exactly 2048 frames.
All inputs are finite; a program needn't handle non-finite values. No bound on the sum of `lengths` or of `label_mask` on one device may be relied on, other than what follows from the above.
Results may differ from a plain program's by a relative error of at most 0.034.
Values may be sent and summed in bfloat16 or wider, within the bound.
No kernel may reach another device: no remote copies, remote signals or barrier semaphores. Data moves between devices by JAX's collectives and lax.ppermute only.
A program may use at most 64 MiB of HBM per device.

v0:
```python
import math

import jax
import jax.numpy as jnp
from jax import lax
from jax.sharding import PartitionSpec as P

HEAD_DIM = 128
WINDOW = 128
TAPS = 9
VOCAB = 1024


def padded(block, sides, width):
    for axis, dim in sides:
        count = lax.axis_size(axis)
        forward = [(i, i + 1) for i in range(count - 1)]
        backward = [(target, source) for source, target in forward]
        low = lax.ppermute(
            lax.slice_in_dim(block, block.shape[dim] - width, None, axis=dim), axis, forward
        )
        high = lax.ppermute(lax.slice_in_dim(block, 0, width, axis=dim), axis, backward)
        block = jnp.concatenate([low, block, high], axis=dim)
    return block


def passed_along(value, axis, by):
    size = lax.axis_size(axis)
    pairs = [(i, i + by) for i in range(size) if 0 <= i + by < size]
    return lax.ppermute(value, axis, pairs)


def band_scores(query_heads, key_heads, query_pos, key_pos, length, factor):
    product = (
        jnp.einsum("qhd,khd->hqk", query_heads, key_heads, preferred_element_type=jnp.float32)
        * factor
    )
    inside = (
        (jnp.abs(query_pos[:, None] - key_pos[None, :]) <= WINDOW)
        & (key_pos[None, :] >= 0)
        & (key_pos[None, :] < length)
    )
    return jnp.where(inside[None], product, -1e30)


def local(
    queries,
    key_rows,
    value_rows,
    out_weight,
    head_weight,
    conv_weight,
    lengths,
    label_mask,
    targets,
):
    tokens = queries.shape[1]
    att_width = queries.shape[2]
    head_count = att_width // HEAD_DIM
    factor = 1.0 / math.sqrt(HEAD_DIM)
    margin = (TAPS - 1) // 2
    offset = lax.axis_index("ctx") * tokens
    length = lengths[0]
    out_full, head_full = (
        lax.all_gather(out_weight, "dp", axis=0, tiled=True),
        lax.all_gather(head_weight, "dp", axis=0, tiled=True),
    )
    query_mat = queries[0]
    query_heads = query_mat.reshape(tokens, head_count, HEAD_DIM)
    paired = jnp.concatenate([key_rows[0], value_rows[0]], axis=1)
    paired_ext = padded(paired, (("ctx", 0),), WINDOW)
    key_heads = paired_ext[:, :att_width].reshape(-1, head_count, HEAD_DIM)
    value_heads = paired_ext[:, att_width:].reshape(-1, head_count, HEAD_DIM)
    query_pos = offset + jnp.arange(tokens, dtype=jnp.int32)
    key_pos = offset - WINDOW + jnp.arange(tokens + 2 * WINDOW, dtype=jnp.int32)
    scores = band_scores(query_heads, key_heads, query_pos, key_pos, length, factor)
    row_max = jnp.max(scores, axis=-1)
    log_total = row_max + jnp.log(jnp.sum(jnp.exp(scores - row_max[..., None]), axis=-1))
    probs = jnp.exp(scores - log_total[..., None])
    prob_half = probs.astype(jnp.bfloat16)
    attn = jnp.einsum(
        "hqk,khd->qhd", prob_half, value_heads, preferred_element_type=jnp.float32
    ).astype(jnp.bfloat16)
    attn = attn.reshape(tokens, att_width)
    live = query_pos < length
    hidden = jnp.dot(attn, out_full, preferred_element_type=jnp.float32)
    hidden = jnp.where(live[:, None], hidden, 0.0)
    hidden_ext = padded(hidden.astype(jnp.bfloat16), (("ctx", 0),), margin).astype(hidden.dtype)
    conv = jnp.zeros_like(hidden)
    for tap in range(TAPS):
        conv = conv + conv_weight[tap] * hidden_ext[tap : tap + tokens]
    sigma = jax.nn.sigmoid(conv)
    gated = (conv * sigma).astype(jnp.bfloat16)
    logits = jnp.dot(gated, head_full, preferred_element_type=jnp.float32)
    top = jnp.max(logits, axis=-1, keepdims=True)
    log_norm = top[:, 0] + jnp.log(jnp.sum(jnp.exp(logits - top), axis=-1))
    target_hit = targets[0][:, None] == jnp.arange(VOCAB, dtype=jnp.int32)[None, :]
    picked = jnp.sum(jnp.where(target_hit, logits, 0.0), axis=-1)
    selected = ((label_mask[0] == 1) & live).astype(jnp.float32)
    loss_local = jnp.sum(selected * (log_norm - picked))
    count_local = jnp.sum(selected)
    frame_total = lax.psum(count_local, ("dp", "ctx"))
    loss_total = lax.psum(loss_local, ("dp", "ctx"))
    soft = jnp.exp(logits - log_norm[:, None])
    dlogits = (selected[:, None] * (soft - target_hit.astype(jnp.float32))).astype(jnp.bfloat16)
    d_gated = lax.dot_general(
        dlogits, head_full, (((1,), (1,)), ((), ())), preferred_element_type=jnp.float32
    )
    d_pre = d_gated * sigma * (1.0 + conv * (1.0 - sigma))
    conv_grad = jnp.stack(
        [jnp.sum(d_pre * hidden_ext[tap : tap + tokens], axis=0) for tap in range(TAPS)]
    )
    d_pre_ext = padded(d_pre.astype(jnp.bfloat16), (("ctx", 0),), margin).astype(d_pre.dtype)
    d_hidden = jnp.zeros_like(d_pre)
    for tap in range(TAPS):
        d_hidden = (
            d_hidden + conv_weight[tap] * d_pre_ext[2 * margin - tap : 2 * margin - tap + tokens]
        )
    d_hidden = jnp.where(live[:, None], d_hidden, 0.0).astype(jnp.bfloat16)
    d_attn = lax.dot_general(
        d_hidden, out_full, (((1,), (1,)), ((), ())), preferred_element_type=jnp.float32
    ).astype(jnp.bfloat16)
    d_heads = d_attn.reshape(tokens, head_count, HEAD_DIM)
    attn_heads = attn.reshape(tokens, head_count, HEAD_DIM)
    row_delta = jnp.sum(d_heads.astype(jnp.float32) * attn_heads.astype(jnp.float32), axis=-1).T
    d_probs = jnp.einsum("qhd,khd->hqk", d_heads, value_heads, preferred_element_type=jnp.float32)
    d_scores = (probs * (d_probs - row_delta[..., None])).astype(jnp.bfloat16)
    d_query = (
        jnp.einsum("hqk,khd->qhd", d_scores, key_heads, preferred_element_type=jnp.float32) * factor
    )
    d_query = d_query.astype(jnp.bfloat16).reshape(1, tokens, att_width)
    key_part = (
        jnp.einsum("hqk,qhd->khd", d_scores, query_heads, preferred_element_type=jnp.float32)
        * factor
    )
    value_part = jnp.einsum("hqk,qhd->khd", prob_half, d_heads, preferred_element_type=jnp.float32)
    ext_grads = jnp.concatenate(
        [key_part.reshape(-1, att_width), value_part.reshape(-1, att_width)], axis=1
    )
    from_right = passed_along(ext_grads[:WINDOW].astype(jnp.bfloat16), "ctx", -1).astype(
        jnp.float32
    )
    from_left = passed_along(ext_grads[tokens + WINDOW :].astype(jnp.bfloat16), "ctx", 1).astype(
        jnp.float32
    )
    own_grads = ext_grads[WINDOW : WINDOW + tokens]
    own_grads = own_grads.at[:WINDOW].add(from_left)
    own_grads = own_grads.at[tokens - WINDOW :].add(from_right)
    d_key = own_grads[:, :att_width].astype(jnp.bfloat16).reshape(1, tokens, att_width)
    d_value = own_grads[:, att_width:].astype(jnp.bfloat16).reshape(1, tokens, att_width)
    conv_total = lax.psum(conv_grad, ("dp", "ctx"))
    loss = loss_total / frame_total
    d_conv = conv_total / jnp.sqrt(frame_total)
    return (loss, d_query, d_key, d_value, d_conv)


def solution(mesh):
    placed = (
        P("dp", "ctx", None),
        P("dp", "ctx", None),
        P("dp", "ctx", None),
        P("dp", None),
        P("dp", None),
        P(),
        P("dp"),
        P("dp", "ctx"),
        P("dp", "ctx"),
    )
    return jax.shard_map(
        local,
        mesh=mesh,
        in_specs=placed,
        out_specs=(P(), P("dp", "ctx", None), P("dp", "ctx", None), P("dp", "ctx", None), P()),
        check_vma=False,
    )
```

profile of v0, /device:TPU:0, one launch (start us, length us, event | category | flops | bytes accessed | tf_op | source)
XLA Modules:
  0.0 145.0 jit_solution(9960458524800264047)
XLA Ops:
  8.0 1.1 copy.29
  9.1 1.1 copy.30
  10.2 4.9 %collective-permute-start = (bf16[128,1024]{0,1:T(8,128)(2,1)S(1)}, bf16[128,1024]{0,1:T(8,128)(2,1)S(1)}, u32[]{:S(2)}, u32[]{:S(2)}) collective-permute-start(bf16[128,1024]{0,1:T(8,128)(2,1)S(1)} %get-tuple-element.69), channel_id=1, source_target_pairs={{0,1},{1,2},{2,3},{3,4},{4,5},{5,6},{6,7},{8,9},{9,10},{10,11},{11... | collective-permute-start | bytes 786440 | tf_op jit(solution)/shard_map/ppermute | solution.py:19
  15.1 1.3 collective-permute-start.1
  17.6 8.7 %collective-permute-done = bf16[128,1024]{0,1:T(8,128)(2,1)S(1)} collective-permute-done((bf16[128,1024]{0,1:T(8,128)(2,1)S(1)}, bf16[128,1024]{0,1:T(8,128)(2,1)S(1)}, u32[]{:S(2)}, u32[]{:S(2)}) %collective-permute-start) | collective-permute-done | bytes 262176 | tf_op jit(solution)/shard_map/ppermute | solution.py:19
  29.0 1.7 %fusion.3 = bf16[256,1024]{1,0:T(8,128)(2,1)S(1)} fusion(bf16[256,512]{0,1:T(8,128)(2,1)S(1)} %bitcast.79, bf16[512,1024]{1,0:T(8,128)(2,1)} %all-gather.3.cloned.1.call-done, pred[256]{0:T(512)(128)(4,1)S(1)} %get-tuple-element.56), kind=kOutput, calls=%fused_computation.15 | convolution fusion | flops 268959744 | bytes 1835264 | tf_op jit(solution)/shard_map/dot_general | solution.py:86
  30.8 4.1 %collective-permute-start.2 = (bf16[4,1024]{1,0:T(4,128)(2,1)S(1)}, bf16[4,1024]{1,0:T(4,128)(2,1)S(1)}, u32[]{:S(2)}, u32[]{:S(2)}) collective-permute-start(bf16[4,1024]{1,0:T(4,128)(2,1)S(1)} %get-tuple-element.67), channel_id=1, source_target_pairs={{0,1},{1,2},{2,3},{3,4},{4,5},{5,6},{6,7},{8,9},{9,10},{10,11},{11... | collective-permute-start | bytes 24584 | tf_op jit(solution)/shard_map/ppermute | solution.py:19
  34.9 1.3 collective-permute-start.3
  36.2 4.6 %collective-permute-done.3 = bf16[4,1024]{1,0:T(4,128)(2,1)S(1)} collective-permute-done((bf16[4,1024]{1,0:T(4,128)(2,1)S(1)}, bf16[4,1024]{1,0:T(4,128)(2,1)S(1)}, u32[]{:S(2)}, u32[]{:S(2)}) %collective-permute-start.3) | collective-permute-done | bytes 8224 | tf_op jit(solution)/shard_map/ppermute | solution.py:22
  41.0 2.0 %multiply_add_fusion = f32[256,1024]{1,0:T(8,128)} fusion(f32[264,1024]{1,0:T(8,128)S(1)} %maximum_convert_fusion, f32[1024]{0:T(1024)S(1)} %bitcast.94, f32[1024]{0:T(1024)S(1)} %bitcast.96, f32[1024]{0:T(1024)S(1)} %bitcast.82, f32[1024]{0:T(1024)S(1)} %bitcast.84, f32[1024]{0:T(1024)S(1)} %bitcast.86, f32[1024]{0:T(1024)S(1)} %bitcast.88, ...), kind=kLoop, calls=%fused_computation.56 | loop fusion | flops 4456448 | bytes 10522624 | tf_op jit(solution)/shard_map/add | solution.py:91
  43.0 10.2 %all-gather.5.cloned.1.call-done = bf16[1024,1024]{1,0:T(8,128)(2,1)} async-done(((bf16[256,1024]{1,0:T(8,128)(2,1)}), bf16[1024,1024]{1,0:T(8,128)(2,1)}) %all-gather.5.cloned.1.call-update) | async-done | bytes 2097168 | tf_op jit(solution)/shard_map/all_gather | solution.py:66
  53.2 2.9 %fusion.42 = (f32[256]{0:T(256)S(1)}, f32[256,1024]{1,0:T(8,128)S(1)}) fusion(bf16[1024,1024]{1,0:T(8,128)(2,1)} %all-gather.5.cloned.1.call-done, f32[256,1024]{1,0:T(8,128)} %multiply_add_fusion), kind=kOutput, calls=%fused_computation.100 | convolution fusion | flops 538443520 | bytes 4195328 | tf_op jit(solution)/shard_map/dot_general | solution.py:94
  57.2 3.2 %multiply_reduce_fusion = (f32[1024]{0:T(1024)S(1)}, f32[1024]{0:T(1024)S(1)}, f32[1024]{0:T(1024)S(1)}, f32[1024]{0:T(1024)S(1)}, f32[1024]{0:T(1024)S(1)}, /*i...) fusion(f32[264,1024]{1,0:T(8,128)S(1)} %maximum_convert_fusion,, ...), kind=kOutput, calls=%fused_computation.41 | convolution fusion | flops 545512448 | bytes 14195712 | tf_op jit(solution)/shard_map/dot_general | solution.py:106
  61.2 3.4 %collective-permute-start.4 = (bf16[4,1024]{1,0:T(4,128)(2,1)S(1)}, bf16[4,1024]{1,0:T(4,128)(2,1)S(1)}, u32[]{:S(2)}, u32[]{:S(2)}) collective-permute-start(bf16[4,1024]{1,0:T(4,128)(2,1)S(1)} %get-tuple-element.65), channel_id=1, source_target_pairs={{0,1},{1,2},{2,3},{3,4},{4,5},{5,6},{6,7},{8,9},{9,10},{10,11},{11... | collective-permute-start | bytes 24584 | tf_op jit(solution)/shard_map/ppermute | solution.py:19
  64.6 1.3 collective-permute-start.5
  65.9 42.2 %all-reduce = (f32[]{:T(128)}, f32[]{:T(128)}, f32[9,1024]{1,0:T(8,128)S(1)}) all-reduce(f32[]{:T(128)} %get-tuple-element.51, f32[]{:T(128)} %get-tuple-element.50, f32[9,1024]{1,0:T(8,128)S(1)} %stack.39), channel_id=1, replica_groups=mesh['dp'=4,'ctx'=8] {'dp','ctx'}, use_global_device_ids=true, to_apply=%region_6.7 | all-reduce | flops 9218 | bytes 73744 | tf_op jit(solution)/shard_map/psum | solution.py:103
  110.8 1.2 maximum_convert_fusion.1
  112.0 2.7 %convolution_convert_fusion = bf16[256,512]{1,0:T(8,128)(2,1)S(1)} fusion(bf16[512,1024]{1,0:T(8,128)(2,1)} %all-gather.3.cloned.1.call-done, f32[264,1024]{1,0:T(8,128)S(1)} %maximum_convert_fusion.1, f32[1024]{0:T(1024)S(1)} %bitcast.95, f32[1024]{0:T(1024)S(1)} %bitcast.97, f32[1024]{0:T(1024)S(1)} %bitcast.83, f32[1024]{0:T(1024)S(1)} %bitcast.85, ...), kind=kOutput, calls=%fused_computation.18 | convolution fusion | flops 273547264 | bytes 10785280 | tf_op jit(solution)/shard_map/dot_general | solution.py:120
  115.0 1.5 %fusion.28 = f32[4,128,512]{2,1,0:T(8,128)} fusion(bf16[256,4,128]{0,2,1:T(8,128)(2,1)S(1)} %bitcast.70, f32[4,256,512]{1,2,0:T(8,128)S(1)} %get-tuple-element.81, f32[4,256]{1,0:T(4,128)S(1)} %log_add_fusion), kind=kOutput, calls=%fused_computation.75 | convolution fusion | flops 135266304 | bytes 3411968 | tf_op jit(solution)/shard_map/hqk,qhd->khd/dot_general | solution.py:136
  120.1 4.9 %collective-permute-start.6 = (bf16[128,1024]{1,0:T(8,128)(2,1)}, bf16[128,1024]{1,0:T(8,128)(2,1)}, u32[]{:S(2)}, u32[]{:S(2)}) collective-permute-start(bf16[128,1024]{1,0:T(8,128)(2,1)} %get-tuple-element.59), channel_id=1, source_target_pairs={{0,1},{1,2},{2,3},{3,4},{4,5},{5,6},{6,7},{8,9},{9,10},{10,11},{11... | collective-permute-start | bytes 786440 | tf_op jit(solution)/shard_map/ppermute | solution.py:30
  125.3 1.3 collective-permute-start.7
  127.5 6.5 %collective-permute-done.6 = bf16[128,1024]{1,0:T(8,128)(2,1)} collective-permute-done((bf16[128,1024]{1,0:T(8,128)(2,1)}, bf16[128,1024]{1,0:T(8,128)(2,1)}, u32[]{:S(2)}, u32[]{:S(2)}) %collective-permute-start.6) | collective-permute-done | bytes 262176 | tf_op jit(solution)/shard_map/ppermute | solution.py:30
  134.0 1.0 fusion.19
  135.1 1.1 fusion.20
  (77 shorter events, 12.7 us)
Async XLA Ops:
  7.2 9.9 %copy-start.15 = (s32[1,256]{1,0:T(1,128)S(1)}, s32[1,256]{1,0:T(1,128)}, u32[]{:S(2)}) copy-start(s32[1,256]{1,0:T(1,128)} %param.20) | copy-start | bytes 3076
  7.2 10.0 %copy-start.11 = (bf16[1,256,512]{2,1,0:T(8,128)(2,1)S(1)}, bf16[1,256,512]{2,1,0:T(8,128)(2,1)}, u32[]{:S(2)}) copy-start(bf16[1,256,512]{2,1,0:T(8,128)(2,1)} %param.13) | copy-start | bytes 786436
  7.2 21.8 %all-gather.3.cloned.1.call-start = ((), (), s32[]{:S(2)}) async-start(), calls=%async_computation | async-start | bytes 1310720 | tf_op jit(solution)/shard_map/all_gather | solution.py:65
  7.9 45.3 %all-gather.5.cloned.1.call-start = ((), (), s32[]{:S(2)}) async-start(), calls=%async_computation.1 | async-start | bytes 2621440 | tf_op jit(solution)/shard_map/all_gather | solution.py:66
  10.2 16.0 %collective-permute-start = (bf16[128,1024]{0,1:T(8,128)(2,1)S(1)}, bf16[128,1024]{0,1:T(8,128)(2,1)S(1)}, u32[]{:S(2)}, u32[]{:S(2)}) collective-permute-start(bf16[128,1024]{0,1:T(8,128)(2,1)S(1)} %get-tuple-element.69), channel_id=1, source_target_pairs={{0,1},{1,2},{2,3},{3,4},{4,5},{5,6},{6,7},{8,9},{9,10},{10,11},{11... | collective-permute-start | bytes 786440 | tf_op jit(solution)/shard_map/ppermute | solution.py:19
  15.1 11.2 %collective-permute-start.1 = (bf16[128,1024]{0,1:T(8,128)(2,1)S(1)}, bf16[128,1024]{0,1:T(8,128)(2,1)S(1)}, u32[]{:S(2)}, u32[]{:S(2)}) collective-permute-start(bf16[128,1024]{0,1:T(8,128)(2,1)S(1)} %get-tuple-element.70), channel_id=1, source_target_pairs={{1,0},{2,1},{3,2},{4,3},{5,4},{6,5},{7,6},{9,8},{10,9},{11,10},{12... | collective-permute-start | bytes 786440 | tf_op jit(solution)/shard_map/ppermute | solution.py:22
  26.4 1.7 %copy-start.4 = (bf16[512,512]{0,1:T(8,128)(2,1)}, bf16[512,512]{0,1:T(8,128)(2,1)S(1)}, u32[]{:S(2)}) copy-start(bf16[512,512]{0,1:T(8,128)(2,1)S(1)} %get-tuple-element.62) | copy-start | bytes 1572868
  28.1 8.0 %copy-start.12 = (f32[9,1024]{1,0:T(8,128)S(1)}, f32[9,1024]{1,0:T(8,128)}, u32[]{:S(2)}) copy-start(f32[9,1024]{1,0:T(8,128)} %param.18) | copy-start | bytes 110596
  28.6 7.6 %copy-start.8 = (bf16[4,128,256]{2,1,0:T(8,128)(2,1)}, bf16[4,128,256]{2,1,0:T(8,128)(2,1)S(1)}, u32[]{:S(2)}) copy-start(bf16[4,128,256]{2,1,0:T(8,128)(2,1)S(1)} %convolution_convert_fusion.1) | copy-start | bytes 786436
  30.8 5.4 %collective-permute-start.2 = (bf16[4,1024]{1,0:T(4,128)(2,1)S(1)}, bf16[4,1024]{1,0:T(4,128)(2,1)S(1)}, u32[]{:S(2)}, u32[]{:S(2)}) collective-permute-start(bf16[4,1024]{1,0:T(4,128)(2,1)S(1)} %get-tuple-element.67), channel_id=1, source_target_pairs={{0,1},{1,2},{2,3},{3,4},{4,5},{5,6},{6,7},{8,9},{9,10},{10,11},{11... | collective-permute-start | bytes 24584 | tf_op jit(solution)/shard_map/ppermute | solution.py:19
  34.9 5.9 %collective-permute-start.3 = (bf16[4,1024]{1,0:T(4,128)(2,1)S(1)}, bf16[4,1024]{1,0:T(4,128)(2,1)S(1)}, u32[]{:S(2)}, u32[]{:S(2)}) collective-permute-start(bf16[4,1024]{1,0:T(4,128)(2,1)S(1)} %get-tuple-element.68), channel_id=1, source_target_pairs={{1,0},{2,1},{3,2},{4,3},{5,4},{6,5},{7,6},{9,8},{10,9},{11,10},{12... | collective-permute-start | bytes 24584 | tf_op jit(solution)/shard_map/ppermute | solution.py:22
  43.0 13.1 %copy-start.13 = (s32[1,256]{1,0:T(1,128)S(1)}, s32[1,256]{1,0:T(1,128)}, u32[]{:S(2)}) copy-start(s32[1,256]{1,0:T(1,128)} %param.21) | copy-start | bytes 3076
  53.2 4.0 %copy-start.7 = (f32[256,1024]{1,0:T(8,128)S(1)}, f32[256,1024]{1,0:T(8,128)}, u32[]{:S(2)}) copy-start(f32[256,1024]{1,0:T(8,128)} %multiply_add_fusion) | copy-start | bytes 3145732
  53.2 4.0 %copy-start.14 = (bf16[1024,1024]{1,0:T(8,128)(2,1)S(1)}, bf16[1024,1024]{1,0:T(8,128)(2,1)}, u32[]{:S(2)}) copy-start(bf16[1024,1024]{1,0:T(8,128)(2,1)} %all-gather.5.cloned.1.call-done) | copy-start | bytes 6291460
  61.2 49.6 %collective-permute-start.4 = (bf16[4,1024]{1,0:T(4,128)(2,1)S(1)}, bf16[4,1024]{1,0:T(4,128)(2,1)S(1)}, u32[]{:S(2)}, u32[]{:S(2)}) collective-permute-start(bf16[4,1024]{1,0:T(4,128)(2,1)S(1)} %get-tuple-element.65), channel_id=1, source_target_pairs={{0,1},{1,2},{2,3},{3,4},{4,5},{5,6},{6,7},{8,9},{9,10},{10,11},{11... | collective-permute-start | bytes 24584 | tf_op jit(solution)/shard_map/ppermute | solution.py:19
  64.6 46.2 %collective-permute-start.5 = (bf16[4,1024]{1,0:T(4,128)(2,1)S(1)}, bf16[4,1024]{1,0:T(4,128)(2,1)S(1)}, u32[]{:S(2)}, u32[]{:S(2)}) collective-permute-start(bf16[4,1024]{1,0:T(4,128)(2,1)S(1)} %get-tuple-element.66), channel_id=1, source_target_pairs={{1,0},{2,1},{3,2},{4,3},{5,4},{6,5},{7,6},{9,8},{10,9},{11,10},{12... | collective-permute-start | bytes 24584 | tf_op jit(solution)/shard_map/ppermute | solution.py:22
  112.0 2.9 %copy-start.9 = (bf16[4,128,256]{2,1,0:T(8,128)(2,1)S(1)}, bf16[4,128,256]{2,1,0:T(8,128)(2,1)}, u32[]{:S(2)}) copy-start(bf16[4,128,256]{2,1,0:T(8,128)(2,1)} %copy-done.8) | copy-start | bytes 786436
  114.9 1.6 %copy-start.5 = (bf16[512,512]{0,1:T(8,128)(2,1)S(1)}, bf16[512,512]{0,1:T(8,128)(2,1)}, u32[]{:S(2)}) copy-start(bf16[512,512]{0,1:T(8,128)(2,1)} %copy-done.4) | copy-start | bytes 1572868
  117.1 1.0 copy-start
  117.1 1.6 %copy-start.6 = (f32[4,128,512]{2,1,0:T(8,128)S(1)}, f32[4,128,512]{2,1,0:T(8,128)}, u32[]{:S(2)}) copy-start(f32[4,128,512]{2,1,0:T(8,128)} %fusion.28) | copy-start | bytes 3145732
  119.1 5.9 %copy-start.1 = (bf16[4,256,512]{1,2,0:T(8,128)(2,1)S(1)}, bf16[4,256,512]{1,2,0:T(8,128)(2,1)}, u32[]{:S(2)}) copy-start(bf16[4,256,512]{1,2,0:T(8,128)(2,1)} %copy-done) | copy-start | bytes 3145732
  119.1 5.9 %copy-start.3 = (bf16[512,512]{0,1:T(8,128)(2,1)S(1)}, bf16[512,512]{0,1:T(8,128)(2,1)}, u32[]{:S(2)}) copy-start(bf16[512,512]{0,1:T(8,128)(2,1)} %copy-done.2) | copy-start | bytes 1572868
  120.1 14.0 %collective-permute-start.6 = (bf16[128,1024]{1,0:T(8,128)(2,1)}, bf16[128,1024]{1,0:T(8,128)(2,1)}, u32[]{:S(2)}, u32[]{:S(2)}) collective-permute-start(bf16[128,1024]{1,0:T(8,128)(2,1)} %get-tuple-element.59), channel_id=1, source_target_pairs={{0,1},{1,2},{2,3},{3,4},{4,5},{5,6},{6,7},{8,9},{9,10},{10,11},{11... | collective-permute-start | bytes 786440 | tf_op jit(solution)/shard_map/ppermute | solution.py:30
  125.3 9.8 %collective-permute-start.7 = (bf16[128,1024]{1,0:T(8,128)(2,1)}, bf16[128,1024]{1,0:T(8,128)(2,1)}, u32[]{:S(2)}, u32[]{:S(2)}) collective-permute-start(bf16[128,1024]{1,0:T(8,128)(2,1)} %get-tuple-element.58), channel_id=1, source_target_pairs={{1,0},{2,1},{3,2},{4,3},{5,4},{6,5},{7,6},{9,8},{10,9},{11,10},{12... | collective-permute-start | bytes 786440 | tf_op jit(solution)/shard_map/ppermute | solution.py:30
  (2 other events, 1.6 us)
Sparse Core Ops, SparseCore 0:
  9.6 19.4 all-gather.2
  30.6 22.5 all-gather.4
where the time goes:
time: 146 us; the launch traced here: 145 us
  blocking collectives  42.2 us (29%)
  waiting for transfers between devices  31.1 us (21%)
  starting transfers between devices  22.5 us (15%)
  between operations  18.3 us (13%)
  matrix products  14.4 us (10%)
  other arithmetic  8.3 us (6%)
  local copies, waits for them, and re-layouts  8.19 us (6%)
    psum x1, blocking collectives, local(): loss_total = lax.psum(loss_local, ('dp', 'ctx'))  42.2 us
    ppermute x3, starting transfers between devices, padded(): lax.ppermute(lax.slice_in_dim(block, block.shape[dim] - width, None, axis...  12.4 us
    all_gather x1, waiting for transfers between devices, local(): lax.all_gather(head_weight, 'dp', axis=0, tiled=True)  10.2 us
    ppermute x3, waiting for transfers between devices, padded(): lax.ppermute(lax.slice_in_dim(block, block.shape[dim] - width, None, axis...  8.66 us
    ppermute x2, waiting for transfers between devices, passed_along(): return lax.ppermute(value, axis, pairs)  6.53 us
    ppermute x2, starting transfers between devices, passed_along(): return lax.ppermute(value, axis, pairs)  6.18 us
    unnamed x35, local copies, waits for them, and re-layouts  5.4 us
    ppermute x3, waiting for transfers between devices, padded(): lax.ppermute(lax.slice_in_dim(block, 0, width, axis=dim), axis, backward)  4.59 us
  transfers between devices with their start and end apart: 10, of which 5 were waited for; matrix products, arithmetic and copies ran while one was open for 8% of the time, Pallas kernels for 0%

commit v1 on v0

v1 whole, which is shorter than its diff:
```python
import functools
import math

import jax
import jax.numpy as jnp
from jax import lax
from jax.experimental import pallas as pl
from jax.experimental.pallas import tpu as pltpu
from jax.sharding import PartitionSpec as P

HEAD_DIM = 128
WINDOW = 128
TAPS = 9
MARGIN = (TAPS - 1) // 2
EDGE = 8
HALO = WINDOW + 2 * EDGE
LOW = -1e30
FACTOR = 1.0 / math.sqrt(HEAD_DIM)
F32 = jnp.float32
BF16 = jnp.bfloat16


def bits_of(size):
    bits = []
    while (1 << len(bits)) < size:
        bits.append(1 << len(bits))
    return bits


def swapped(value, axis, bit):
    size = lax.axis_size(axis)
    return lax.ppermute(value, axis, [(i, i ^ bit) for i in range(size)])


def exchanged(near, far, axis):
    size = lax.axis_size(axis)
    pairs = [(i, i ^ 1) for i in range(size) if (i ^ 1) < size]
    others = [(i, i - 1 + 2 * (i % 2)) for i in range(size) if 0 <= i - 1 + 2 * (i % 2) < size]
    return lax.ppermute(near, axis, pairs), lax.ppermute(far, axis, others)


def nt(left, right):
    return lax.dot_general(left, right, (((1,), (1,)), ((), ())), preferred_element_type=F32)


def tn(left, right):
    return lax.dot_general(left, right, (((0,), (0,)), ((), ())), preferred_element_type=F32)


def nn(left, right):
    return jnp.dot(left, right, preferred_element_type=F32)


def inside_band(rows, cols, row_start, col_start, offset, length):
    row_pos = row_start + lax.broadcasted_iota(jnp.int32, (rows, cols), 0)
    col_pos = col_start + lax.broadcasted_iota(jnp.int32, (rows, cols), 1)
    return (
        (jnp.abs(row_pos - col_pos) <= WINDOW)
        & (col_pos + offset >= 0)
        & (col_pos + offset < length)
    )


def pack_kernel(targets, mask, q, k, v, near, far, meta, edges, marks, sems):
    tokens, width = q.shape
    even = lax.rem(lax.axis_index("ctx"), 2) == 0
    edge = 2 * EDGE
    ends = (slice(0, edge), slice(tokens - edge, tokens))
    copies = []

    def fetch(source, target):
        copy = pltpu.make_async_copy(source, target, sems.at[len(copies)])
        copy.start()
        copies.append(copy)

    start = pl.multiple_of(jnp.where(even, tokens - HALO, 0), 16)
    other = pl.multiple_of(jnp.where(even, 0, tokens - HALO), 16)
    for message, first in ((near, start), (far, other)):
        fetch(k.at[pl.ds(first, HALO)], message.at[:, 0:width])
        fetch(v.at[pl.ds(first, HALO)], message.at[:, width : 2 * width])
    for place, end in enumerate(ends):
        fetch(q.at[end], edges.at[place])
    fetch(targets, marks.at[0])
    fetch(mask, marks.at[1])
    for copy in copies[-2:]:
        copy.wait()
    spread = (128, tokens)
    target = jnp.broadcast_to(marks[0], spread).T
    chosen = jnp.broadcast_to(marks[1], spread).T
    spot = lax.broadcasted_iota(jnp.int32, (tokens, 128), 1)
    entry = jnp.where(spot == 0, target >> 5, jnp.where(spot == 1, target & 31, chosen))
    meta[...] = entry.astype(F32)
    for copy in copies[:-2]:
        copy.wait()
    low = lax.broadcasted_iota(jnp.int32, (edge, 1), 0) < EDGE

    def patch(message, place, use, end):
        rows = slice(place, place + edge)
        held = message[rows, :].astype(F32)
        ours = jnp.concatenate(
            [edges[end].astype(F32), meta[ends[end], :], jnp.zeros((edge, width - 128), F32)],
            axis=1,
        )
        ours = jnp.concatenate([ours[EDGE:], ours[:EDGE]], axis=0)
        message[rows, :] = jnp.where(use, ours, held).astype(BF16)

    @pl.when(even)
    def _():
        patch(near, 0, low, 1)
        patch(far, HALO - edge, ~low, 0)

    @pl.when(~even)
    def _():
        patch(near, HALO - edge, ~low, 0)
        patch(far, 0, low, 1)


def stage_kernel(q, k, v, q_own, k_own, v_own):
    q_own[...] = q[...]
    k_own[...] = k[...]
    v_own[...] = v[...]


def attention_kernel(
    info, q, k, v, meta, near, far, attn, lse, k_ext, v_ext, q_ext, meta_ext
):
    tokens, width = q.shape
    length, offset = info[0], info[1]
    even = info[3] == 0
    q_ext[16 : 16 + tokens, :] = q[...]
    k_ext[HALO : HALO + tokens, :] = k[...]
    v_ext[HALO : HALO + tokens, :] = v[...]

    def place_sides(left, right):
        for ext, first in ((k_ext, 0), (v_ext, width)):
            cols = slice(first, first + width)
            ext[0:HALO, :] = left[:, cols]
            ext[HALO + tokens : 2 * HALO + tokens, :] = right[:, cols]
        q_ext[0:16, :] = left[0:16, 0:width]
        q_ext[16 + tokens :, :] = right[HALO - 16 : HALO, 0:width]
        spots = slice(width, width + 128)
        meta_ext[0:EDGE, :] = left[0:16, spots].astype(F32)[0:EDGE]
        meta_ext[EDGE + tokens :, :] = right[HALO - 16 : HALO, spots].astype(F32)[EDGE:]

    @pl.when(even)
    def _():
        place_sides(far, near)

    @pl.when(~even)
    def _():
        place_sides(near, far)

    meta_ext[EDGE : EDGE + tokens, :] = meta[...]
    lse[...] = jnp.zeros(lse.shape, F32)
    rows, span = 16 + WINDOW, 4 * WINDOW
    spot = lax.broadcasted_iota(jnp.int32, (rows, span), 0)
    blocks = [
        (0, 0, jnp.where(spot < EDGE, spot - EDGE, spot - 16)),
        (
            tokens + 32 - rows,
            tokens + 2 * HALO - span,
            jnp.where(spot < WINDOW, spot + tokens - WINDOW, spot + tokens - WINDOW - EDGE),
        ),
    ]
    for place, key_row, query_pos in blocks:
        key_pos = key_row - HALO + lax.broadcasted_iota(jnp.int32, (rows, span), 1)
        inside = (
            (jnp.abs(query_pos - key_pos) <= WINDOW)
            & (key_pos + offset >= 0)
            & (key_pos + offset < length)
        )
        keys = slice(key_row, key_row + span)
        first = max(place, 16)
        own = slice(first - place, first - place + WINDOW)
        for at in range(0, width, HEAD_DIM):
            cols = slice(at, at + HEAD_DIM)
            head = at // HEAD_DIM
            scores = nt(q_ext[place : place + rows, cols], k_ext[keys, cols]) * FACTOR
            scores = jnp.where(inside, scores, LOW)
            top = jnp.max(scores, axis=-1, keepdims=True)
            grown = jnp.exp(scores - top)
            total = jnp.sum(grown, axis=-1, keepdims=True)
            mixed = nn(grown.astype(BF16), v_ext[keys, cols]) * (1.0 / total)
            attn[place : place + rows, cols] = mixed.astype(BF16)
            level = top + jnp.log(total)
            lse[first - 16 : first - 16 + WINDOW, 4 + head : 5 + head] = level[own]


def middle_kernel(marks, info, attn, lse, meta_ext, taps, *refs):
    count = len(marks)
    out_parts, head_parts = refs[:count], refs[count : 2 * count]
    d_attn, stats, summary = refs[2 * count : 2 * count + 3]
    (
        out_full, head_full, hid, gated, slope, logits, d_logits, d_pre, d_hid, sems,
    ) = refs[2 * count + 3 :]
    length, offset, mine = info[0], info[1], info[2]
    copies = []
    for parts, full in ((out_parts, out_full), (head_parts, head_full)):
        for mark, part in zip(marks, parts):
            rows = part.shape[0]
            start = pl.multiple_of((mine ^ mark) * rows, rows)
            copy = pltpu.make_async_copy(part, full.at[pl.ds(start, rows)], sems.at[len(copies)])
            copy.start()
            copies.append(copy)
    tokens, width = d_attn.shape
    depth = out_full.shape[1]
    vocab = head_full.shape[1]
    ext = tokens + 2 * EDGE
    lanes = 128

    row_pos = offset - EDGE + lax.broadcasted_iota(jnp.int32, (ext, lanes), 0)
    live = (row_pos >= 0) & (row_pos < length)
    hid[:, 0:EDGE, :] = jnp.zeros((depth // lanes, EDGE, lanes), F32)
    hid[:, EDGE + ext :, :] = jnp.zeros((depth // lanes, EDGE, lanes), F32)
    for copy in copies[:count]:
        copy.wait()
    for at in range(0, depth, 256):
        block = nn(attn[...], out_full[:, at : at + 256])
        block = jnp.concatenate(
            [block[0:EDGE], block[16 : 16 + tokens], block[16 + tokens + EDGE :]], axis=0
        )
        for part in range(2):
            piece = block[:, part * lanes : (part + 1) * lanes]
            hid[at // lanes + part, EDGE : EDGE + ext, :] = jnp.where(live, piece, 0.0)
    for chunk in range(depth // lanes):
        cols = slice(chunk * lanes, (chunk + 1) * lanes)
        conv = jnp.zeros((ext, lanes), F32)
        for tap in range(TAPS):
            start = EDGE - MARGIN + tap
            conv = conv + taps[tap : tap + 1, cols] * hid[chunk, start : start + ext, :]
        sigma = jax.nn.sigmoid(conv)
        gated[:, cols] = (conv * sigma).astype(BF16)
        slope[chunk] = sigma * (1.0 + conv * (1.0 - sigma))
    for copy in copies[count:]:
        copy.wait()
    for at in range(0, vocab, 256):
        logits[:, at : at + 256] = nn(gated[...], head_full[:, at : at + 256])

    meta_all = meta_ext[...]
    target = (meta_all[:, 0:1] * 32.0 + meta_all[:, 1:2]).astype(jnp.int32)
    chosen = jnp.where(live & (meta_all[:, 2:3] == 1.0), 1.0, 0.0)[:, 0:1]
    loss_rows = jnp.zeros((16, 1), F32)
    count_rows = jnp.zeros((16, 1), F32)
    word = lax.broadcasted_iota(jnp.int32, (16, vocab), 1)
    row_in = lax.broadcasted_iota(jnp.int32, (16, 1), 0)
    for at in range(0, ext, 16):
        block = logits[at : at + 16, :]
        top = jnp.max(block, axis=-1, keepdims=True)
        grown = jnp.exp(block - top)
        total = jnp.sum(grown, axis=-1, keepdims=True)
        hit = target[at : at + 16] == word
        picked = jnp.sum(jnp.where(hit, block, 0.0), axis=-1, keepdims=True)
        pick = chosen[at : at + 16]
        change = grown * (pick / total) - jnp.where(hit, pick, 0.0)
        d_logits[at : at + 16, :] = change.astype(BF16)
        own = (row_in + at >= EDGE) & (row_in + at < EDGE + tokens)
        kept = jnp.where(own, pick, 0.0)
        loss_rows = loss_rows + kept * (top + jnp.log(total) - picked)
        count_rows = count_rows + kept
    summary[...] = jnp.zeros(summary.shape, F32)
    lane = lax.broadcasted_iota(jnp.int32, (1, lanes), 1)
    loss_sum = jnp.sum(loss_rows, axis=0, keepdims=True)
    count_sum = jnp.sum(count_rows, axis=0, keepdims=True)
    summary[TAPS : TAPS + 1, 0:lanes] = jnp.where(
        lane == 0, loss_sum, jnp.where(lane == 1, count_sum, 0.0)
    )
    for at in range(0, depth, 256):
        d_gated = nt(d_logits[...], head_full[at : at + 256, :])
        for part in range(2):
            chunk = at // lanes + part
            cols = slice(chunk * lanes, (chunk + 1) * lanes)
            change = d_gated[:, part * lanes : (part + 1) * lanes] * slope[chunk]
            d_pre[chunk] = change
            owned = change[EDGE : EDGE + tokens]
            for tap in range(TAPS):
                start = 2 * EDGE - MARGIN + tap
                summary[tap : tap + 1, cols] = jnp.sum(
                    owned * hid[chunk, start : start + tokens, :], axis=0, keepdims=True
                )
    for chunk in range(depth // lanes):
        cols = slice(chunk * lanes, (chunk + 1) * lanes)
        change = jnp.zeros((tokens, lanes), F32)
        for tap in range(TAPS):
            start = EDGE + MARGIN - tap
            change = change + taps[tap : tap + 1, cols] * d_pre[chunk, start : start + tokens, :]
        d_hid[:, cols] = jnp.where(live[EDGE : EDGE + tokens], change, 0.0).astype(BF16)
    stats[...] = lse[...]
    for at in range(0, width, HEAD_DIM):
        cols = slice(at, at + HEAD_DIM)
        head = at // HEAD_DIM
        block = nt(d_hid[...], out_full[cols, :]).astype(BF16)
        d_attn[:, cols] = block
        products = block.astype(F32) * attn[16 : 16 + tokens, cols].astype(F32)
        stats[:, head : head + 1] = jnp.sum(products, axis=-1, keepdims=True)


def edge_grads_kernel(info, q_ext, k_ext, v_ext, stats, d_attn, near, far):
    tokens, width = d_attn.shape
    length, offset = info[0], info[1]
    even = info[3] == 0
    for out, on_right in ((near, even), (far, ~even)):
        first = pl.multiple_of(jnp.where(on_right, tokens - WINDOW, 0), WINDOW)
        key_start = jnp.where(on_right, tokens, -WINDOW)
        rows = pl.ds(first, WINDOW)
        asked = pl.ds(pl.multiple_of(first + 16, 16), WINDOW)
        keys = pl.ds(pl.multiple_of(key_start + HALO, 16), WINDOW)
        by_row = stats[rows, :].T
        key_pos = key_start + lax.broadcasted_iota(jnp.int32, (WINDOW, WINDOW), 0)
        query_pos = first + lax.broadcasted_iota(jnp.int32, (WINDOW, WINDOW), 1)
        inside = (
            (jnp.abs(query_pos - key_pos) <= WINDOW)
            & (key_pos + offset >= 0)
            & (key_pos + offset < length)
        )
        for start in range(0, width, HEAD_DIM):
            cols = slice(start, start + HEAD_DIM)
            head = start // HEAD_DIM
            query, change = q_ext[asked, cols], d_attn[rows, cols]
            scores = jnp.where(inside, nt(k_ext[keys, cols], query) * FACTOR, LOW)
            probs = jnp.exp(scores - by_row[4 + head : 5 + head, :])
            d_scores = probs * (nt(v_ext[keys, cols], change) - by_row[head : head + 1, :])
            out[:, cols] = (nn(d_scores.astype(BF16), query) * FACTOR).astype(BF16)
            out[:, width + start : width + start + HEAD_DIM] = nn(
                probs.astype(BF16), change
            ).astype(BF16)


def own_grads_kernel(info, q_ext, k_ext, v_ext, stats, d_attn, d_q, d_k, d_v):
    tokens, width = d_attn.shape
    length, offset = info[0], info[1]
    span = 3 * WINDOW
    d_k[...] = jnp.zeros(d_k.shape, F32)
    d_v[...] = jnp.zeros(d_v.shape, F32)
    for at in range(0, tokens, WINDOW):
        rows = slice(at, at + WINDOW)
        key_row = HALO - WINDOW + at
        inside = inside_band(WINDOW, span, at, at - WINDOW, offset, length)
        first = max(at - WINDOW, 0)
        last = min(at + 2 * WINDOW, tokens)
        mine = slice(first - at + WINDOW, last - at + WINDOW)
        for start in range(0, width, HEAD_DIM):
            cols = slice(start, start + HEAD_DIM)
            head = start // HEAD_DIM
            query, change = q_ext[at + 16 : at + 16 + WINDOW, cols], d_attn[rows, cols]
            keys = k_ext[key_row : key_row + span, cols]
            values = v_ext[key_row : key_row + span, cols]
            scores = jnp.where(inside, nt(query, keys) * FACTOR, LOW)
            probs = jnp.exp(scores - stats[rows, 4 + head : 5 + head])
            d_scores = probs * (nt(change, values) - stats[rows, head : head + 1])
            d_scores = d_scores.astype(BF16)
            d_q[rows, cols] = (nn(d_scores, keys) * FACTOR).astype(BF16)
            d_k[first:last, cols] += tn(d_scores[:, mine], query) * FACTOR
            d_v[first:last, cols] += tn(probs.astype(BF16)[:, mine], change)


def add_kernel(info, k_part, v_part, near, far, d_k, d_v):
    tokens, width = d_k.shape
    even = info[3] == 0
    for got, on_right in ((near, even), (far, ~even)):
        rows = pl.ds(pl.multiple_of(jnp.where(on_right, tokens - WINDOW, 0), WINDOW), WINDOW)
        for out, part, cols in (
            (d_k, k_part, slice(0, width)),
            (d_v, v_part, slice(width, 2 * width)),
        ):
            out[rows, :] = (part[rows, :] + got[0:WINDOW, cols].astype(F32)).astype(BF16)


def grouped(bits):
    pairs = [bits[at : at + 2] for at in range(0, len(bits), 2)]
    return [pair + [pair[0] ^ pair[1]] if len(pair) == 2 else pair for pair in pairs]


def packed(totals):
    rounded = lax.reduce_precision(totals[:TAPS], 8, 7)
    first = lax.reduce_precision(totals[TAPS:], 8, 7)
    second = lax.reduce_precision(totals[TAPS:] - first, 8, 7)
    third = totals[TAPS:] - first - second
    return jnp.concatenate([rounded, first, second, third], axis=0).astype(BF16)


def unpacked(sent):
    wide = sent.astype(F32)
    last = wide[TAPS : TAPS + 1] + wide[TAPS + 1 : TAPS + 2] + wide[TAPS + 2 : TAPS + 3]
    return jnp.concatenate([wide[:TAPS], last], axis=0)


def added(parts):
    sums = [unpacked(part) for part in parts]
    while len(sums) > 1:
        sums = [sums[at] + sums[at + 1] for at in range(0, len(sums), 2)]
    return sums[0]


def finish_kernel(*refs):
    parts, (d_conv, loss) = refs[:-2], refs[-2:]
    taps = [part[...].astype(F32)[0:TAPS] for part in parts]
    sums = []
    for part in parts:
        wide = part[...].astype(F32)
        sums.append(wide[TAPS : TAPS + 1] + wide[TAPS + 1 : TAPS + 2] + wide[TAPS + 2 : TAPS + 3])
    while len(taps) > 1:
        taps = [taps[at] + taps[at + 1] for at in range(0, len(taps), 2)]
        sums = [sums[at] + sums[at + 1] for at in range(0, len(sums), 2)]
    count = sums[0][:, 1:2]
    d_conv[...] = taps[0] / jnp.sqrt(count)
    loss[...] = sums[0][:, 0:1] / count


def call(kernel, operands, outs, scratch, places, flops, limit=24):
    specs = {
        "s": pl.BlockSpec(memory_space=pltpu.SMEM),
        "v": pl.BlockSpec(memory_space=pltpu.VMEM),
        "a": pl.BlockSpec(memory_space=pl.ANY),
    }
    arrays = list(operands) + list(outs)
    size = sum(math.prod(item.shape) * item.dtype.itemsize for item in arrays) if flops else 1
    return pl.pallas_call(
        kernel,
        out_shape=outs,
        in_specs=[specs[place] for place in places],
        out_specs=[specs["v"] for _ in outs],
        scratch_shapes=scratch,
        compiler_params=pltpu.CompilerParams(vmem_limit_bytes=limit * 1024 * 1024),
        cost_estimate=pl.CostEstimate(flops=max(flops, 1), bytes_accessed=size, transcendentals=0),
    )(*operands)


def local(
    queries,
    key_rows,
    value_rows,
    out_weight,
    head_weight,
    conv_weight,
    lengths,
    label_mask,
    targets,
):
    tokens, width = queries.shape[1:]
    depth = out_weight.shape[1]
    vocab = head_weight.shape[1]
    dp_size = lax.axis_size("dp")
    place = lax.axis_index("ctx")
    q, k, v = queries[0], key_rows[0], value_rows[0]
    info = jnp.stack([lengths[0], place * tokens, lax.axis_index("dp"), place % 2])
    info = info.astype(jnp.int32)

    shape = jax.ShapeDtypeStruct
    halo = shape((HALO, 2 * width), BF16)
    block = shape((tokens, width), BF16)
    near, far, meta = call(
        pack_kernel,
        (targets, label_mask, q, k, v),
        (halo, halo, shape((tokens, 128), F32)),
        [
            pltpu.VMEM((2, 2 * EDGE, width), BF16),
            pltpu.VMEM((2, 1, tokens), jnp.int32),
            pltpu.SemaphoreType.DMA((8,)),
        ],
        "aaaaa",
        0,
        56,
    )
    q_own, k_own, v_own = call(stage_kernel, (q, k, v), (block, block, block), [], "vvv", 0)
    near, far = exchanged(near, far, "ctx")
    ext = tokens + 2 * EDGE
    attn, lse, k_ext, v_ext, q_ext, meta_ext = call(
        attention_kernel,
        (info, q_own, k_own, v_own, meta, near, far),
        (
            shape((tokens + 32, width), BF16),
            shape((tokens, 128), F32),
            shape((tokens + 2 * HALO, width), BF16),
            shape((tokens + 2 * HALO, width), BF16),
            shape((tokens + 32, width), BF16),
            shape((ext, 128), F32),
        ),
        [],
        "svvvvvv",
        4 * tokens * 3 * WINDOW * width,
    )
    top_bit = bits_of(dp_size)[-1]
    first_hop = [swapped(head_weight, "dp", top_bit), swapped(out_weight, "dp", top_bit)]
    attn, head_far, out_far = lax.optimization_barrier((attn, *first_hop))
    held, marks = [], []
    for weight, received in ((out_weight, out_far), (head_weight, head_far)):
        pieces = [(0, weight), (top_bit, received)]
        for bit in reversed(bits_of(dp_size)[:-1]):
            pieces += [(mark ^ bit, swapped(item, "dp", bit)) for mark, item in pieces]
        marks = [mark for mark, _ in pieces]
        held += [item for _, item in pieces]

    chunks = depth // 128
    d_attn, stats, summary = call(
        functools.partial(middle_kernel, tuple(marks)),
        (info, attn, lse, meta_ext, conv_weight, *held),
        (
            shape((tokens, width), BF16),
            shape((tokens, 128), F32),
            shape((16, depth), F32),
        ),
        [
            pltpu.VMEM((width, depth), BF16),
            pltpu.VMEM((depth, vocab), BF16),
            pltpu.VMEM((chunks, ext + 2 * EDGE, 128), F32),
            pltpu.VMEM((ext, depth), BF16),
            pltpu.VMEM((chunks, ext, 128), F32),
            pltpu.VMEM((ext, vocab), F32),
            pltpu.VMEM((ext, vocab), BF16),
            pltpu.VMEM((chunks, ext, 128), F32),
            pltpu.VMEM((tokens, depth), BF16),
            pltpu.SemaphoreType.DMA((2 * dp_size,)),
        ],
        "svvvv" + "a" * (2 * dp_size),
        4 * tokens * depth * (width + vocab),
    )

    totals = summary[: TAPS + 1]
    dp_bits, ctx_bits = bits_of(dp_size), bits_of(lax.axis_size("ctx"))
    near_part, far_part = call(
        edge_grads_kernel,
        (info, q_ext, k_ext, v_ext, stats, d_attn),
        (shape((WINDOW, 2 * width), BF16), shape((WINDOW, 2 * width), BF16)),
        [],
        "svvvvv",
        16 * WINDOW * WINDOW * width,
    )
    for index, group in enumerate(grouped(dp_bits)):
        sent = packed(totals)
        got = [swapped(sent, "dp", bit) for bit in group]
        if index == 0:
            near_part, far_part, *got = lax.optimization_barrier((near_part, far_part, *got))
        totals = added([sent] + got)
    sent = packed(totals)
    near_part = jnp.concatenate([near_part, sent], axis=0)
    near_got, far_got = exchanged(near_part, far_part, "ctx")
    d_q, k_part, v_part = call(
        own_grads_kernel,
        (info, q_ext, k_ext, v_ext, stats, d_attn),
        (block, shape((tokens, width), F32), shape((tokens, width), F32)),
        [],
        "svvvvv",
        10 * tokens * 3 * WINDOW * width,
    )
    near_got, d_q, k_part, v_part = lax.optimization_barrier((near_got, d_q, k_part, v_part))
    totals = added([sent, near_got[WINDOW:]])
    groups = grouped(ctx_bits[1:])
    for index, group in enumerate(groups):
        sent = packed(totals)
        got = [swapped(sent, "ctx", bit) for bit in group]
        if index < len(groups) - 1:
            totals = added([sent] + got)
    d_k, d_v = call(
        add_kernel,
        (info, k_part, v_part, near_got, far_got),
        (block, block),
        [],
        "svvvv",
        tokens * width,
    )
    d_k, d_v, *got = lax.optimization_barrier((d_k, d_v, *got))
    d_conv, loss = call(
        finish_kernel,
        (sent, *got),
        (shape((TAPS, depth), F32), shape((1, 1), F32)),
        [],
        "v" * (1 + len(got)),
        0,
    )
    return (loss[0, 0], d_q[None], d_k[None], d_v[None], d_conv)


def solution(mesh):
    placed = (
        P("dp", "ctx", None),
        P("dp", "ctx", None),
        P("dp", "ctx", None),
        P("dp", None),
        P("dp", None),
        P(),
        P("dp"),
        P("dp", "ctx"),
        P("dp", "ctx"),
    )
    return jax.shard_map(
        local,
        mesh=mesh,
        in_specs=placed,
        out_specs=(P(), P("dp", "ctx", None), P("dp", "ctx", None), P("dp", "ctx", None), P()),
        check_vma=False,
    )
```

time: 146 us -> 59.1 us (0.40)
  blocking collectives: 42.2 us -> 0 us
  Pallas kernels: 0 us -> 20.1 us
  between operations: 18.3 us -> 1.59 us
  matrix products: 14.4 us -> 0 us
  waiting for transfers between devices: 31.1 us -> 20.5 us
  local copies, waits for them, and re-layouts: 8.19 us -> 0.19 us
  other arithmetic: 8.3 us -> 0.49 us
  starting transfers between devices: 22.5 us -> 16 us
    psum x1 -> x0, blocking collectives: 42.2 us -> none  [local(): loss_total = lax.psum(loss_local, ('dp', 'ctx'))]
    pallas_call x0 -> x8, Pallas kernels: none -> 20.1 us  [call(): pl.pallas_call(kernel, out_shape=outs, in_specs=[specs[place] for place i...]
    dot_general x10 -> x0, matrix products: 14.4 us -> none  [the longest x1 3.18 us: local(): lax.dot_general(dlogits, head_full, (((1,), (1,)), ((), ())), preferred_e...]
    all_gather x2 -> x0, waiting for transfers between devices: 10.6 us -> none  [the longest x1 10.2 us: local(): lax.all_gather(head_weight, 'dp', axis=0, tiled=True)]
    ppermute x8 -> x16, starting transfers between devices: 22.4 us -> 16 us  [the longest x12 10.6 us: swapped(): return lax.ppermute(value, axis, [(i, i ^ bit) for i in range(size)])]
    unnamed x35 -> x14, local copies, waits for them, and re-layouts: 5.4 us -> 0.03 us
    scatter-add x2 -> x0, other arithmetic: 2.07 us -> none  [the longest x1 1.07 us: local(): own_grads = own_grads.at[tokens - WINDOW:].add(from_right)]
    add x4 -> x7, other arithmetic: 2.06 us -> 0.18 us  [the longest x5 0.12 us: unpacked(): wide[TAPS:TAPS + 1] + wide[TAPS + 1:TAPS + 2] + wide[TAPS + 2:TAPS + 3]]
  transfers between devices with their start and end apart: 10 -> 16, of which waited for: 5 -> 8; matrix products, arithmetic and copies ran while one was open for 8% -> 1% of each run, Pallas kernels for 0% -> 21%
where the time goes in v1:
time: 59.1 us; the launch traced here: 58.9 us
  waiting for transfers between devices  20.5 us (35%)
  Pallas kernels  20.1 us (34%)
  starting transfers between devices  16 us (27%)
  between operations  1.59 us (3%)
    pallas_call x8, Pallas kernels, call(): pl.pallas_call(kernel, out_shape=outs, in_specs=[specs[place] for place i...  20.1 us
    ppermute x4, waiting for transfers between devices, exchanged(): return (lax.ppermute(near, axis, pairs), lax.ppermute(far, axis, others))  13.5 us
    ppermute x12, starting transfers between devices, swapped(): return lax.ppermute(value, axis, [(i, i ^ bit) for i in range(size)])  10.6 us
    ppermute x12, waiting for transfers between devices, swapped(): return lax.ppermute(value, axis, [(i, i ^ bit) for i in range(size)])  6.98 us
    ppermute x4, starting transfers between devices, exchanged(): return (lax.ppermute(near, axis, pairs), lax.ppermute(far, axis, others))  5.38 us
  transfers between devices with their start and end apart: 16, of which 8 were waited for; matrix products, arithmetic and copies ran while one was open for 1% of the time, Pallas kernels for 21%

profile of v1, /device:TPU:0, one launch (start us, length us, event | category | flops | bytes accessed | tf_op | source)
XLA Modules:
  0.0 58.9 jit_solution(8793017277227391959)
XLA Ops:
  0.6 3.0 %collective-permute-start.2 = (bf16[256,1024]{1,0:T(8,128)(2,1)}, bf16[256,1024]{1,0:T(8,128)(2,1)S(1)}, u32[]{:S(2)}, u32[]{:S(2)}) collective-permute-start(bf16[256,1024]{1,0:T(8,128)(2,1)} %refs_4_.1), channel_id=1, source_target_pairs={{0,16},{8,24},{16,0},{24,8},{1,17},{9,25},{17,1},{25,9},{2,18},{10... | collective-permute-start | bytes 1572872 | tf_op jit(solution)/shard_map/ppermute | solution.py:32
  3.6 2.1 %shard_map.129 = (bf16[144,1024]{1,0:T(8,128)(2,1)}, bf16[144,1024]{1,0:T(8,128)(2,1)}, f32[256,128]{1,0:T(8,128)}) custom-call(s32[1,256]{1,0:T(1,128)} %targets.1, s32[1,256]{1,0:T(1,128)} %mask.1, bf16[256,512]{1,0:T(8,128)(2,1)} %bitcast.12, bf16[256,512]{1,0:T(8,128)(2,1)} %bitcast.14, bf16[256,512]{1,0:T(8,128)(2,1)} %bitcast.16), custom_call_target="tpu_custom_call" | custom-call | flops 1 | bytes 1 | tf_op jit(solution)/shard_map/pallas_call | solution.py:417
  5.8 1.6 %collective-permute-start = (bf16[144,1024]{1,0:T(8,128)(2,1)}, bf16[144,1024]{1,0:T(8,128)(2,1)S(1)}, u32[]{:S(2)}, u32[]{:S(2)}) collective-permute-start(bf16[144,1024]{1,0:T(8,128)(2,1)} %get-tuple-element.50), channel_id=1, source_target_pairs={{0,1},{1,0},{2,3},{3,2},{4,5},{5,4},{6,7},{7,6},{8,9},{9,8},{10,11... | collective-permute-start | bytes 884744 | tf_op jit(solution)/shard_map/ppermute | solution.py:39
  7.4 0.7 %collective-permute-start.1 = (bf16[144,1024]{1,0:T(8,128)(2,1)}, bf16[144,1024]{1,0:T(8,128)(2,1)S(1)}, u32[]{:S(2)}, u32[]{:S(2)}) collective-permute-start(bf16[144,1024]{1,0:T(8,128)(2,1)} %get-tuple-element.51), channel_id=1, source_target_pairs={{1,2},{2,1},{3,4},{4,3},{5,6},{6,5},{9,10},{10,9},{11,12},{12,11},... | collective-permute-start | bytes 884744 | tf_op jit(solution)/shard_map/ppermute | solution.py:39
  8.0 0.6 %collective-permute-start.3 = (bf16[128,1024]{1,0:T(8,128)(2,1)}, bf16[128,1024]{1,0:T(8,128)(2,1)}, u32[]{:S(2)}, u32[]{:S(2)}) collective-permute-start(bf16[128,1024]{1,0:T(8,128)(2,1)} %refs_0_.1), channel_id=1, source_target_pairs={{0,16},{8,24},{16,0},{24,8},{1,17},{9,25},{17,1},{25,9},{2,18},{10... | collective-permute-start | bytes 786440 | tf_op jit(solution)/shard_map/ppermute | solution.py:32
  9.5 10.5 %collective-permute-done.near = bf16[144,1024]{1,0:T(8,128)(2,1)S(1)} collective-permute-done((bf16[144,1024]{1,0:T(8,128)(2,1)}, bf16[144,1024]{1,0:T(8,128)(2,1)S(1)}, u32[]{:S(2)}, u32[]{:S(2)}) %collective-permute-start) | collective-permute-done | bytes 294944 | tf_op jit(solution)/shard_map/ppermute | solution.py:39
  20.0 3.0 %shard_map.130 = (bf16[288,512]{1,0:T(8,128)(2,1)S(1)}, f32[256,128]{1,0:T(8,128)S(1)}, bf16[544,512]{1,0:T(8,128)(2,1)S(1)}, bf16[544,512]{1,0:T(8,128)(2,1)S(1...) custom-call(s32[4]{0:T(128)S(1)} %pad_add_fusion.info, bf16[256,512]{1,0:T(8,128)(2,1)S(1)} %get-tuple-element.46.q, ...), custom_call_target="tpu_custom_call" | custom-call | flops 201326592 | bytes 3481616 | tf_op jit(solution)/shard_map/pallas_call | solution.py:417
  23.1 0.5 collective-permute-start.4
  23.7 2.1 %collective-permute-done.4.refs_2_ = bf16[128,1024]{1,0:T(8,128)(2,1)S(1)} collective-permute-done((bf16[128,1024]{1,0:T(8,128)(2,1)S(1)}, bf16[128,1024]{1,0:T(8,128)(2,1)S(1)}, u32[]{:S(2)}, u32[]{:S(2)}) %collective-permute-start.4) | collective-permute-done | bytes 262176 | tf_op jit(solution)/shard_map/ppermute | solution.py:32
  26.0 7.1 %shard_map.131 = (bf16[256,512]{1,0:T(8,128)(2,1)S(1)}, f32[256,128]{1,0:T(8,128)S(1)}, f32[16,1024]{1,0:T(8,128)S(1)}) custom-call(s32[4]{0:T(128)S(1)} %pad_add_fusion.info, bf16[288,512]{1,0:T(8,128)(2,1)S(1)} %get-tuple-element.53.attn, f32[256,128]{1,0:T(8,128)S(1)} %get-tuple-element.54.lse, f32[272,128]{1,0:T(8,128)S(1)} %get-tuple-element.55.meta_ext, ...), custom_call_target="tpu_custom_call" | custom-call | flops 1610612736 | bytes 4206608 | tf_op jit(solution)/shard_map/pallas_call | solution.py:417
  33.4 0.5 collective-permute-start.9
  33.9 1.2 %collective-permute-start.10 = (bf16[12,1024]{1,0:T(8,128)(2,1)S(1)}, bf16[12,1024]{1,0:T(8,128)(2,1)S(1)}, u32[]{:S(2)}, u32[]{:S(2)}) collective-permute-start(bf16[12,1024]{1,0:T(8,128)(2,1)S(1)} %get-tuple-element.92), channel_id=1, source_target_pairs={{0,24},{8,16},{16,8},{24,0},{1,25},{9,17},{17,9},{25,1},{2,26},{10... | collective-permute-start | bytes 73736 | tf_op jit(solution)/shard_map/ppermute | solution.py:32
  35.1 2.1 %shard_map.132 = (bf16[128,1024]{1,0:T(8,128)(2,1)S(1)}, bf16[128,1024]{1,0:T(8,128)(2,1)S(1)}) custom-call(s32[4]{0:T(128)S(1)} %pad_add_fusion.info, bf16[288,512]{1,0:T(8,128)(2,1)S(1)} %get-tuple-element.59.q_ext, bf16[544,512]{1,0:T(8,128)(2,1)S(1)} %get-tuple-element.60.k_ext, bf16[544,512]{1,0:T(8,128)(2,1)S(1)} %get-tuple-element.61.v_ext, ...), custom_call_target="tpu_custom_call" | custom-call | flops 134217728 | bytes 2326544 | tf_op jit(solution)/shard_map/pallas_call | solution.py:417
  38.0 2.5 %collective-permute-start.11 = (bf16[140,1024]{1,0:T(8,128)(2,1)S(1)}, bf16[140,1024]{1,0:T(8,128)(2,1)S(1)}, u32[]{:S(2)}, u32[]{:S(2)}) collective-permute-start(bf16[140,1024]{1,0:T(8,128)(2,1)S(1)} %concatenate.41), channel_id=1, source_target_pairs={{0,1},{1,0},{2,3},{3,2},{4,5},{5,4},{6,7},{7,6},{8,9},{9,8},{10,11... | collective-permute-start | bytes 860168 | tf_op jit(solution)/shard_map/ppermute | solution.py:39
  40.5 3.6 %shard_map.133 = (bf16[256,512]{1,0:T(8,128)(2,1)}, f32[256,512]{1,0:T(8,128)S(1)}, f32[256,512]{1,0:T(8,128)S(1)}) custom-call(s32[4]{0:T(128)S(1)} %pad_add_fusion.info, bf16[288,512]{1,0:T(8,128)(2,1)S(1)} %get-tuple-element.59.q_ext, bf16[544,512]{1,0:T(8,128)(2,1)S(1)} %get-tuple-element.60.k_ext, bf16[544,512]{1,0:T(8,128)(2,1)S(1)} %get-tuple-element.61.v_ext, ...), custom_call_target="tpu_custom_call" | custom-call | flops 503316480 | bytes 3112976 | tf_op jit(solution)/shard_map/pallas_call | solution.py:417
  44.0 0.7 %collective-permute-start.12 = (bf16[128,1024]{1,0:T(8,128)(2,1)S(1)}, bf16[128,1024]{1,0:T(8,128)(2,1)S(1)}, u32[]{:S(2)}, u32[]{:S(2)}) collective-permute-start(bf16[128,1024]{1,0:T(8,128)(2,1)S(1)} %get-tuple-element.76), channel_id=1, source_target_pairs={{1,2},{2,1},{3,4},{4,3},{5,6},{6,5},{9,10},{10,9},{11,12},{12,11},... | collective-permute-start | bytes 786440 | tf_op jit(solution)/shard_map/ppermute | solution.py:39
  44.8 3.0 %collective-permute-done.11.near = bf16[140,1024]{1,0:T(8,128)(2,1)S(1)} collective-permute-done((bf16[140,1024]{1,0:T(8,128)(2,1)S(1)}, bf16[140,1024]{1,0:T(8,128)(2,1)S(1)}, u32[]{:S(2)}, u32[]{:S(2)}) %collective-permute-start.11) | collective-permute-done | bytes 286752 | tf_op jit(solution)/shard_map/ppermute | solution.py:39
  47.9 1.9 %collective-permute-start.13 = (bf16[12,1024]{1,0:T(8,128)(2,1)S(1)}, bf16[12,1024]{1,0:T(8,128)(2,1)S(1)}, u32[]{:S(2)}, u32[]{:S(2)}) collective-permute-start(bf16[12,1024]{1,0:T(8,128)(2,1)S(1)} %pad_maximum_fusion.1.refs_0_), channel_id=1, source_target_pairs={{0,2},{1,3},{2,0},{3,1},{4,6},{5,7},{6,4},{7,5},{8,10},{9,11},{10,... | collective-permute-start | bytes 73736 | tf_op jit(solution)/shard_map/ppermute | solution.py:32
  49.8 2.6 %collective-permute-start.14 = (bf16[12,1024]{1,0:T(8,128)(2,1)S(1)}, bf16[12,1024]{1,0:T(8,128)(2,1)S(1)}, u32[]{:S(2)}, u32[]{:S(2)}) collective-permute-start(bf16[12,1024]{1,0:T(8,128)(2,1)S(1)} %pad_maximum_fusion.1.refs_0_), channel_id=1, source_target_pairs={{0,4},{1,5},{2,6},{3,7},{4,0},{5,1},{6,2},{7,3},{8,12},{9,13},{10,... | collective-permute-start | bytes 73736 | tf_op jit(solution)/shard_map/ppermute | solution.py:32
  52.4 1.4 %shard_map.134 = (bf16[256,512]{1,0:T(8,128)(2,1)}, bf16[256,512]{1,0:T(8,128)(2,1)}) custom-call(s32[4]{0:T(128)S(1)} %pad_add_fusion.info, f32[256,512]{1,0:T(8,128)S(1)} %get-tuple-element.74.k_part, f32[256,512]{1,0:T(8,128)S(1)} %get-tuple-element.75.v_part, bf16[140,1024]{1,0:T(8,128)(2,1)S(1)} %collective-permute-done.11.near, ...), custom_call_target="tpu_custom_call" | custom-call | flops 131072 | bytes 2121744 | tf_op jit(solution)/shard_map/pallas_call | solution.py:417
  53.8 1.1 %collective-permute-done.13.refs_1_ = bf16[12,1024]{1,0:T(8,128)(2,1)S(1)} collective-permute-done((bf16[12,1024]{1,0:T(8,128)(2,1)S(1)}, bf16[12,1024]{1,0:T(8,128)(2,1)S(1)}, u32[]{:S(2)}, u32[]{:S(2)}) %collective-permute-start.13) | collective-permute-done | bytes 24608 | tf_op jit(solution)/shard_map/ppermute | solution.py:32
  54.9 1.5 %collective-permute-done.14.refs_2_ = bf16[12,1024]{1,0:T(8,128)(2,1)S(1)} collective-permute-done((bf16[12,1024]{1,0:T(8,128)(2,1)S(1)}, bf16[12,1024]{1,0:T(8,128)(2,1)S(1)}, u32[]{:S(2)}, u32[]{:S(2)}) %collective-permute-start.14) | collective-permute-done | bytes 24608 | tf_op jit(solution)/shard_map/ppermute | solution.py:32
  56.4 1.7 %collective-permute-done.15.refs_3_ = bf16[12,1024]{1,0:T(8,128)(2,1)S(1)} collective-permute-done((bf16[12,1024]{1,0:T(8,128)(2,1)S(1)}, bf16[12,1024]{1,0:T(8,128)(2,1)S(1)}, u32[]{:S(2)}, u32[]{:S(2)}) %collective-permute-start.15) | collective-permute-done | bytes 24608 | tf_op jit(solution)/shard_map/ppermute | solution.py:32
  58.1 0.8 %shard_map.135 = (f32[9,1024]{1,0:T(8,128)}, f32[1,1]{1,0:T(1,128)}) custom-call(bf16[12,1024]{1,0:T(8,128)(2,1)S(1)} %pad_maximum_fusion.1.refs_0_, bf16[12,1024]{1,0:T(8,128)(2,1)S(1)} %collective-permute-done.13.refs_1_, bf16[12,1024]{1,0:T(8,128)(2,1)S(1)} %collective-permute-done.14.refs_2_, bf16[12,1024]{1,0:T(8,128)(2,1)S(1)} %collective-permute-done.15.refs_3_), custom_call_target="tpu_custom_call" | custom-call | flops 1 | bytes 1 | tf_op jit(solution)/shard_map/pallas_call | solution.py:417
  (58 shorter events, 1.7 us)
Async XLA Ops:
  0.6 22.4 %collective-permute-start.2 = (bf16[256,1024]{1,0:T(8,128)(2,1)}, bf16[256,1024]{1,0:T(8,128)(2,1)S(1)}, u32[]{:S(2)}, u32[]{:S(2)}) collective-permute-start(bf16[256,1024]{1,0:T(8,128)(2,1)} %refs_4_.1), channel_id=1, source_target_pairs={{0,16},{8,24},{16,0},{24,8},{1,17},{9,25},{17,1},{25,9},{2,18},{10... | collective-permute-start | bytes 1572872 | tf_op jit(solution)/shard_map/ppermute | solution.py:32
  3.6 5.0 %copy-start = (bf16[1,256,512]{2,1,0:T(8,128)(2,1)S(1)}, bf16[1,256,512]{2,1,0:T(8,128)(2,1)}, u32[]{:S(2)}) copy-start(bf16[1,256,512]{2,1,0:T(8,128)(2,1)} %param.9) | copy-start | bytes 786436
  3.6 5.0 %copy-start.1 = (bf16[1,256,512]{2,1,0:T(8,128)(2,1)S(1)}, bf16[1,256,512]{2,1,0:T(8,128)(2,1)}, u32[]{:S(2)}) copy-start(bf16[1,256,512]{2,1,0:T(8,128)(2,1)} %param.10) | copy-start | bytes 786436
  3.6 5.0 %copy-start.2 = (bf16[1,256,512]{2,1,0:T(8,128)(2,1)S(1)}, bf16[1,256,512]{2,1,0:T(8,128)(2,1)}, u32[]{:S(2)}) copy-start(bf16[1,256,512]{2,1,0:T(8,128)(2,1)} %param.11) | copy-start | bytes 786436
  5.8 14.2 %collective-permute-start = (bf16[144,1024]{1,0:T(8,128)(2,1)}, bf16[144,1024]{1,0:T(8,128)(2,1)S(1)}, u32[]{:S(2)}, u32[]{:S(2)}) collective-permute-start(bf16[144,1024]{1,0:T(8,128)(2,1)} %get-tuple-element.50), channel_id=1, source_target_pairs={{0,1},{1,0},{2,3},{3,2},{4,5},{5,4},{6,7},{7,6},{8,9},{9,8},{10,11... | collective-permute-start | bytes 884744 | tf_op jit(solution)/shard_map/ppermute | solution.py:39
  7.4 12.6 %collective-permute-start.1 = (bf16[144,1024]{1,0:T(8,128)(2,1)}, bf16[144,1024]{1,0:T(8,128)(2,1)S(1)}, u32[]{:S(2)}, u32[]{:S(2)}) collective-permute-start(bf16[144,1024]{1,0:T(8,128)(2,1)} %get-tuple-element.51), channel_id=1, source_target_pairs={{1,2},{2,1},{3,4},{4,3},{5,6},{6,5},{9,10},{10,9},{11,12},{12,11},... | collective-permute-start | bytes 884744 | tf_op jit(solution)/shard_map/ppermute | solution.py:39
  8.0 15.0 %collective-permute-start.3 = (bf16[128,1024]{1,0:T(8,128)(2,1)}, bf16[128,1024]{1,0:T(8,128)(2,1)}, u32[]{:S(2)}, u32[]{:S(2)}) collective-permute-start(bf16[128,1024]{1,0:T(8,128)(2,1)} %refs_0_.1), channel_id=1, source_target_pairs={{0,16},{8,24},{16,0},{24,8},{1,17},{9,25},{17,1},{25,9},{2,18},{10... | collective-permute-start | bytes 786440 | tf_op jit(solution)/shard_map/ppermute | solution.py:32
  8.6 17.1 %collective-permute-start.6 = (bf16[256,1024]{1,0:T(8,128)(2,1)}, bf16[256,1024]{1,0:T(8,128)(2,1)}, u32[]{:S(2)}, u32[]{:S(2)}) collective-permute-start(bf16[256,1024]{1,0:T(8,128)(2,1)} %refs_4_.1), channel_id=1, source_target_pairs={{0,8},{8,0},{16,24},{24,16},{1,9},{9,1},{17,25},{25,17},{2,10},{10... | collective-permute-start | bytes 1572872 | tf_op jit(solution)/shard_map/ppermute | solution.py:32
  8.7 11.3 %copy-start.3 = (f32[256,128]{1,0:T(8,128)S(1)}, f32[256,128]{1,0:T(8,128)}, u32[]{:S(2)}) copy-start(f32[256,128]{1,0:T(8,128)} %get-tuple-element.49.meta) | copy-start | bytes 393220
  20.0 3.1 %copy-start.5 = (bf16[128,1024]{1,0:T(8,128)(2,1)S(1)}, bf16[128,1024]{1,0:T(8,128)(2,1)}, u32[]{:S(2)}) copy-start(bf16[128,1024]{1,0:T(8,128)(2,1)} %refs_0_.1) | copy-start | bytes 786436
  20.0 6.0 %copy-start.4 = (bf16[256,1024]{1,0:T(8,128)(2,1)S(1)}, bf16[256,1024]{1,0:T(8,128)(2,1)}, u32[]{:S(2)}) copy-start(bf16[256,1024]{1,0:T(8,128)(2,1)} %refs_4_.1) | copy-start | bytes 1572868
  20.0 6.0 %copy-start.6 = (f32[9,1024]{1,0:T(8,128)S(1)}, f32[9,1024]{1,0:T(8,128)}, u32[]{:S(2)}) copy-start(f32[9,1024]{1,0:T(8,128)} %taps.1) | copy-start | bytes 110596
  23.0 2.9 %collective-permute-start.7 = (bf16[256,1024]{1,0:T(8,128)(2,1)S(1)}, bf16[256,1024]{1,0:T(8,128)(2,1)S(1)}, u32[]{:S(2)}, u32[]{:S(2)}) collective-permute-start(bf16[256,1024]{1,0:T(8,128)(2,1)S(1)} %collective-permute-done.2.refs_5_), channel_id=1, source_target_pairs={{0,8},{8,0},{16,24},{24,16},{1,9},{9,1},{17,25},{25,17},{2,10},{10... | collective-permute-start | bytes 1572872 | tf_op jit(solution)/shard_map/ppermute | solution.py:32
  23.1 2.6 %collective-permute-start.4 = (bf16[128,1024]{1,0:T(8,128)(2,1)S(1)}, bf16[128,1024]{1,0:T(8,128)(2,1)S(1)}, u32[]{:S(2)}, u32[]{:S(2)}) collective-permute-start(bf16[128,1024]{1,0:T(8,128)(2,1)S(1)} %copy-done.5), channel_id=1, source_target_pairs={{0,8},{8,0},{16,24},{24,16},{1,9},{9,1},{17,25},{25,17},{2,10},{10... | collective-permute-start | bytes 786440 | tf_op jit(solution)/shard_map/ppermute | solution.py:32
  23.6 2.4 %collective-permute-start.5 = (bf16[128,1024]{1,0:T(8,128)(2,1)}, bf16[128,1024]{1,0:T(8,128)(2,1)S(1)}, u32[]{:S(2)}, u32[]{:S(2)}) collective-permute-start(bf16[128,1024]{1,0:T(8,128)(2,1)} %collective-permute-done.3.refs_1_), channel_id=1, source_target_pairs={{0,8},{8,0},{16,24},{24,16},{1,9},{9,1},{17,25},{25,17},{2,10},{10... | collective-permute-start | bytes 786440 | tf_op jit(solution)/shard_map/ppermute | solution.py:32
  33.2 4.0 %collective-permute-start.8 = (bf16[12,1024]{1,0:T(8,128)(2,1)S(1)}, bf16[12,1024]{1,0:T(8,128)(2,1)S(1)}, u32[]{:S(2)}, u32[]{:S(2)}) collective-permute-start(bf16[12,1024]{1,0:T(8,128)(2,1)S(1)} %get-tuple-element.92), channel_id=1, source_target_pairs={{0,8},{8,0},{16,24},{24,16},{1,9},{9,1},{17,25},{25,17},{2,10},{10... | collective-permute-start | bytes 73736 | tf_op jit(solution)/shard_map/ppermute | solution.py:32
  33.4 4.2 %collective-permute-start.9 = (bf16[12,1024]{1,0:T(8,128)(2,1)S(1)}, bf16[12,1024]{1,0:T(8,128)(2,1)S(1)}, u32[]{:S(2)}, u32[]{:S(2)}) collective-permute-start(bf16[12,1024]{1,0:T(8,128)(2,1)S(1)} %get-tuple-element.92), channel_id=1, source_target_pairs={{0,16},{8,24},{16,0},{24,8},{1,17},{9,25},{17,1},{25,9},{2,18},{10... | collective-permute-start | bytes 73736 | tf_op jit(solution)/shard_map/ppermute | solution.py:32
  33.9 3.7 %collective-permute-start.10 = (bf16[12,1024]{1,0:T(8,128)(2,1)S(1)}, bf16[12,1024]{1,0:T(8,128)(2,1)S(1)}, u32[]{:S(2)}, u32[]{:S(2)}) collective-permute-start(bf16[12,1024]{1,0:T(8,128)(2,1)S(1)} %get-tuple-element.92), channel_id=1, source_target_pairs={{0,24},{8,16},{16,8},{24,0},{1,25},{9,17},{17,9},{25,1},{2,26},{10... | collective-permute-start | bytes 73736 | tf_op jit(solution)/shard_map/ppermute | solution.py:32
  38.0 9.8 %collective-permute-start.11 = (bf16[140,1024]{1,0:T(8,128)(2,1)S(1)}, bf16[140,1024]{1,0:T(8,128)(2,1)S(1)}, u32[]{:S(2)}, u32[]{:S(2)}) collective-permute-start(bf16[140,1024]{1,0:T(8,128)(2,1)S(1)} %concatenate.41), channel_id=1, source_target_pairs={{0,1},{1,0},{2,3},{3,2},{4,5},{5,4},{6,7},{7,6},{8,9},{9,8},{10,11... | collective-permute-start | bytes 860168 | tf_op jit(solution)/shard_map/ppermute | solution.py:39
  44.0 8.4 %collective-permute-start.12 = (bf16[128,1024]{1,0:T(8,128)(2,1)S(1)}, bf16[128,1024]{1,0:T(8,128)(2,1)S(1)}, u32[]{:S(2)}, u32[]{:S(2)}) collective-permute-start(bf16[128,1024]{1,0:T(8,128)(2,1)S(1)} %get-tuple-element.76), channel_id=1, source_target_pairs={{1,2},{2,1},{3,4},{4,3},{5,6},{6,5},{9,10},{10,9},{11,12},{12,11},... | collective-permute-start | bytes 786440 | tf_op jit(solution)/shard_map/ppermute | solution.py:39
  47.9 7.0 %collective-permute-start.13 = (bf16[12,1024]{1,0:T(8,128)(2,1)S(1)}, bf16[12,1024]{1,0:T(8,128)(2,1)S(1)}, u32[]{:S(2)}, u32[]{:S(2)}) collective-permute-start(bf16[12,1024]{1,0:T(8,128)(2,1)S(1)} %pad_maximum_fusion.1.refs_0_), channel_id=1, source_target_pairs={{0,2},{1,3},{2,0},{3,1},{4,6},{5,7},{6,4},{7,5},{8,10},{9,11},{10,... | collective-permute-start | bytes 73736 | tf_op jit(solution)/shard_map/ppermute | solution.py:32
  49.8 6.6 %collective-permute-start.14 = (bf16[12,1024]{1,0:T(8,128)(2,1)S(1)}, bf16[12,1024]{1,0:T(8,128)(2,1)S(1)}, u32[]{:S(2)}, u32[]{:S(2)}) collective-permute-start(bf16[12,1024]{1,0:T(8,128)(2,1)S(1)} %pad_maximum_fusion.1.refs_0_), channel_id=1, source_target_pairs={{0,4},{1,5},{2,6},{3,7},{4,0},{5,1},{6,2},{7,3},{8,12},{9,13},{10,... | collective-permute-start | bytes 73736 | tf_op jit(solution)/shard_map/ppermute | solution.py:32
  52.4 5.7 %collective-permute-start.15 = (bf16[12,1024]{1,0:T(8,128)(2,1)S(1)}, bf16[12,1024]{1,0:T(8,128)(2,1)S(1)}, u32[]{:S(2)}, u32[]{:S(2)}) collective-permute-start(bf16[12,1024]{1,0:T(8,128)(2,1)S(1)} %pad_maximum_fusion.1.refs_0_), channel_id=1, source_target_pairs={{0,6},{1,7},{2,4},{3,5},{4,2},{5,3},{6,0},{7,1},{8,14},{9,15},{10,... | collective-permute-start | bytes 73736 | tf_op jit(solution)/shard_map/ppermute | solution.py:32

commit v2 on v1

--- a/solution.py
+++ b/solution.py
@@ -51,18 +51,17 @@
     return jnp.dot(left, right, preferred_element_type=F32)
 
 
-def inside_band(rows, cols, row_start, col_start, offset, length):
-    row_pos = row_start + lax.broadcasted_iota(jnp.int32, (rows, cols), 0)
-    col_pos = col_start + lax.broadcasted_iota(jnp.int32, (rows, cols), 1)
+def in_reach(query_pos, key_pos, offset, length):
     return (
-        (jnp.abs(row_pos - col_pos) <= WINDOW)
-        & (col_pos + offset >= 0)
-        & (col_pos + offset < length)
-    )
-
-
-def pack_kernel(targets, mask, q, k, v, near, far, meta, edges, marks, sems):
+        (jnp.abs(query_pos - key_pos) <= WINDOW)
+        & (key_pos + offset >= 0)
+        & (key_pos + offset < length)
+    )
+
+
+def pack_kernel(targets, mask, q, k, v, head, near, far, meta, piece, edges, marks, sems):
     tokens, width = q.shape
+    half = piece.shape[0]
     even = lax.rem(lax.axis_index("ctx"), 2) == 0
     edge = 2 * EDGE
     ends = (slice(0, edge), slice(tokens - edge, tokens))
@@ -80,6 +79,8 @@
         fetch(v.at[pl.ds(first, HALO)], message.at[:, width : 2 * width])
     for place, end in enumerate(ends):
         fetch(q.at[end], edges.at[place])
+    start = pl.multiple_of(lax.rem(lax.axis_index("ctx") // 2, 2) * half, half)
+    fetch(head.at[pl.ds(start, half)], piece)
     fetch(targets, marks.at[0])
     fetch(mask, marks.at[1])
     for copy in copies[-2:]:
@@ -162,44 +163,55 @@
             jnp.where(spot < WINDOW, spot + tokens - WINDOW, spot + tokens - WINDOW - EDGE),
         ),
     ]
+    work = []
     for place, key_row, query_pos in blocks:
         key_pos = key_row - HALO + lax.broadcasted_iota(jnp.int32, (rows, span), 1)
-        inside = (
-            (jnp.abs(query_pos - key_pos) <= WINDOW)
-            & (key_pos + offset >= 0)
-            & (key_pos + offset < length)
-        )
+        inside = in_reach(query_pos, key_pos, offset, length)
         keys = slice(key_row, key_row + span)
+        work += [(place, keys, inside, at) for at in range(0, width, HEAD_DIM)]
+
+    def scores_of(item):
+        place, keys, inside, at = item
+        cols = slice(at, at + HEAD_DIM)
+        product = nt(q_ext[place : place + rows, cols], k_ext[keys, cols])
+        return jnp.where(inside, product * FACTOR, LOW)
+
+    scores = scores_of(work[0])
+    for index, (place, keys, _, at) in enumerate(work):
+        later = scores_of(work[index + 1]) if index + 1 < len(work) else None
+        cols = slice(at, at + HEAD_DIM)
+        head = at // HEAD_DIM
+        top = jnp.max(scores, axis=-1, keepdims=True)
+        grown = jnp.exp(scores - top)
+        total = jnp.sum(grown, axis=-1, keepdims=True)
+        mixed = nn(grown.astype(BF16), v_ext[keys, cols]) * (1.0 / total)
+        attn[place : place + rows, cols] = mixed.astype(BF16)
+        level = top + jnp.log(total)
         first = max(place, 16)
-        own = slice(first - place, first - place + WINDOW)
-        for at in range(0, width, HEAD_DIM):
-            cols = slice(at, at + HEAD_DIM)
-            head = at // HEAD_DIM
-            scores = nt(q_ext[place : place + rows, cols], k_ext[keys, cols]) * FACTOR
-            scores = jnp.where(inside, scores, LOW)
-            top = jnp.max(scores, axis=-1, keepdims=True)
-            grown = jnp.exp(scores - top)
-            total = jnp.sum(grown, axis=-1, keepdims=True)
-            mixed = nn(grown.astype(BF16), v_ext[keys, cols]) * (1.0 / total)
-            attn[place : place + rows, cols] = mixed.astype(BF16)
-            level = top + jnp.log(total)
-            lse[first - 16 : first - 16 + WINDOW, 4 + head : 5 + head] = level[own]
+        lse[first - 16 : first - 16 + WINDOW, 4 + head : 5 + head] = level[
+            first - place : first - place + WINDOW
+        ]
+        scores = later
 
 
 def middle_kernel(marks, info, attn, lse, meta_ext, taps, *refs):
-    count = len(marks)
-    out_parts, head_parts = refs[:count], refs[count : 2 * count]
-    d_attn, stats, summary = refs[2 * count : 2 * count + 3]
+    count = sum(len(pieces) for pieces in marks)
+    held = list(refs[:count])
+    d_attn, stats, summary = refs[count : count + 3]
     (
         out_full, head_full, hid, gated, slope, logits, d_logits, d_pre, d_hid, sems,
-    ) = refs[2 * count + 3 :]
+    ) = refs[count + 3 :]
     length, offset, mine = info[0], info[1], info[2]
     copies = []
-    for parts, full in ((out_parts, out_full), (head_parts, head_full)):
-        for mark, part in zip(marks, parts):
-            rows = part.shape[0]
-            start = pl.multiple_of((mine ^ mark) * rows, rows)
-            copy = pltpu.make_async_copy(part, full.at[pl.ds(start, rows)], sems.at[len(copies)])
+    for full, pieces, halves in ((out_full, marks[0], 1), (head_full, marks[1], 1), (head_full, marks[2], 2)):
+        for mark, part in pieces:
+            source = held[len(copies)]
+            rows = source.shape[0]
+            start = (mine ^ mark) * (rows * halves)
+            if halves == 2:
+                start = start + (info[4] ^ part) * rows
+            target = full.at[pl.ds(pl.multiple_of(start, rows), rows)]
+            copy = pltpu.make_async_copy(source, target, sems.at[len(copies)])
             copy.start()
             copies.append(copy)
     tokens, width = d_attn.shape
@@ -212,7 +224,7 @@
     live = (row_pos >= 0) & (row_pos < length)
     hid[:, 0:EDGE, :] = jnp.zeros((depth // lanes, EDGE, lanes), F32)
     hid[:, EDGE + ext :, :] = jnp.zeros((depth // lanes, EDGE, lanes), F32)
-    for copy in copies[:count]:
+    for copy in copies[: len(marks[0])]:
         copy.wait()
     for at in range(0, depth, 256):
         block = nn(attn[...], out_full[:, at : at + 256])
@@ -231,7 +243,7 @@
         sigma = jax.nn.sigmoid(conv)
         gated[:, cols] = (conv * sigma).astype(BF16)
         slope[chunk] = sigma * (1.0 + conv * (1.0 - sigma))
-    for copy in copies[count:]:
+    for copy in copies[len(marks[0]) :]:
         copy.wait()
     for at in range(0, vocab, 256):
         logits[:, at : at + 256] = nn(gated[...], head_full[:, at : at + 256])
@@ -298,6 +310,7 @@
     tokens, width = d_attn.shape
     length, offset = info[0], info[1]
     even = info[3] == 0
+    work = []
     for out, on_right in ((near, even), (far, ~even)):
         first = pl.multiple_of(jnp.where(on_right, tokens - WINDOW, 0), WINDOW)
         key_start = jnp.where(on_right, tokens, -WINDOW)
@@ -307,50 +320,53 @@
         by_row = stats[rows, :].T
         key_pos = key_start + lax.broadcasted_iota(jnp.int32, (WINDOW, WINDOW), 0)
         query_pos = first + lax.broadcasted_iota(jnp.int32, (WINDOW, WINDOW), 1)
-        inside = (
-            (jnp.abs(query_pos - key_pos) <= WINDOW)
-            & (key_pos + offset >= 0)
-            & (key_pos + offset < length)
-        )
-        for start in range(0, width, HEAD_DIM):
-            cols = slice(start, start + HEAD_DIM)
-            head = start // HEAD_DIM
+        inside = in_reach(query_pos, key_pos, offset, length)
+        for head in range(width // HEAD_DIM):
+            cols = slice(head * HEAD_DIM, (head + 1) * HEAD_DIM)
             query, change = q_ext[asked, cols], d_attn[rows, cols]
             scores = jnp.where(inside, nt(k_ext[keys, cols], query) * FACTOR, LOW)
-            probs = jnp.exp(scores - by_row[4 + head : 5 + head, :])
-            d_scores = probs * (nt(v_ext[keys, cols], change) - by_row[head : head + 1, :])
-            out[:, cols] = (nn(d_scores.astype(BF16), query) * FACTOR).astype(BF16)
-            out[:, width + start : width + start + HEAD_DIM] = nn(
-                probs.astype(BF16), change
-            ).astype(BF16)
+            d_probs = nt(v_ext[keys, cols], change)
+            work.append((out, head, by_row, query, change, scores, d_probs))
+    done = []
+    for out, head, by_row, query, change, scores, d_probs in work:
+        probs = jnp.exp(scores - by_row[4 + head : 5 + head, :])
+        d_scores = probs * (d_probs - by_row[head : head + 1, :])
+        done.append((out, head, query, change, d_scores.astype(BF16), probs.astype(BF16)))
+    for out, head, query, change, d_scores, probs in done:
+        cols = slice(head * HEAD_DIM, (head + 1) * HEAD_DIM)
+        out[:, cols] = (nn(d_scores, query) * FACTOR).astype(BF16)
+        cols = slice(width + head * HEAD_DIM, width + (head + 1) * HEAD_DIM)
+        out[:, cols] = nn(probs, change).astype(BF16)
 
 
 def own_grads_kernel(info, q_ext, k_ext, v_ext, stats, d_attn, d_q, d_k, d_v):
     tokens, width = d_attn.shape
     length, offset = info[0], info[1]
-    span = 3 * WINDOW
-    d_k[...] = jnp.zeros(d_k.shape, F32)
-    d_v[...] = jnp.zeros(d_v.shape, F32)
-    for at in range(0, tokens, WINDOW):
-        rows = slice(at, at + WINDOW)
-        key_row = HALO - WINDOW + at
-        inside = inside_band(WINDOW, span, at, at - WINDOW, offset, length)
-        first = max(at - WINDOW, 0)
-        last = min(at + 2 * WINDOW, tokens)
-        mine = slice(first - at + WINDOW, last - at + WINDOW)
-        for start in range(0, width, HEAD_DIM):
-            cols = slice(start, start + HEAD_DIM)
-            head = start // HEAD_DIM
-            query, change = q_ext[at + 16 : at + 16 + WINDOW, cols], d_attn[rows, cols]
-            keys = k_ext[key_row : key_row + span, cols]
-            values = v_ext[key_row : key_row + span, cols]
-            scores = jnp.where(inside, nt(query, keys) * FACTOR, LOW)
-            probs = jnp.exp(scores - stats[rows, 4 + head : 5 + head])
-            d_scores = probs * (nt(change, values) - stats[rows, head : head + 1])
-            d_scores = d_scores.astype(BF16)
-            d_q[rows, cols] = (nn(d_scores, keys) * FACTOR).astype(BF16)
-            d_k[first:last, cols] += tn(d_scores[:, mine], query) * FACTOR
-            d_v[first:last, cols] += tn(probs.astype(BF16)[:, mine], change)
+    span = tokens + 2 * WINDOW
+    keys = slice(HALO - WINDOW, HALO + tokens + WINDOW)
+    own = slice(WINDOW, WINDOW + tokens)
+    by_row = stats[...].T
+    key_pos = lax.broadcasted_iota(jnp.int32, (span, tokens), 0) - WINDOW
+    query_pos = lax.broadcasted_iota(jnp.int32, (span, tokens), 1)
+    inside = in_reach(query_pos, key_pos, offset, length)
+
+    def products_of(head):
+        cols = slice(head * HEAD_DIM, (head + 1) * HEAD_DIM)
+        scores = nt(k_ext[keys, cols], q_ext[16 : 16 + tokens, cols])
+        return jnp.where(inside, scores * FACTOR, LOW), nt(v_ext[keys, cols], d_attn[:, cols])
+
+    heads = width // HEAD_DIM
+    products = products_of(0)
+    for head in range(heads):
+        later = products_of(head + 1) if head + 1 < heads else None
+        cols = slice(head * HEAD_DIM, (head + 1) * HEAD_DIM)
+        scores, d_probs = products
+        probs = jnp.exp(scores - by_row[4 + head : 5 + head, :])
+        d_scores = (probs * (d_probs - by_row[head : head + 1, :])).astype(BF16)
+        d_k[:, cols] = nn(d_scores[own], q_ext[16 : 16 + tokens, cols]) * FACTOR
+        d_v[:, cols] = nn(probs[own].astype(BF16), d_attn[:, cols])
+        d_q[:, cols] = (tn(k_ext[keys, cols], d_scores) * FACTOR).T.astype(BF16)
+        products = later
 
 
 def add_kernel(info, k_part, v_part, near, far, d_k, d_v):
@@ -442,27 +458,33 @@
     dp_size = lax.axis_size("dp")
     place = lax.axis_index("ctx")
     q, k, v = queries[0], key_rows[0], value_rows[0]
-    info = jnp.stack([lengths[0], place * tokens, lax.axis_index("dp"), place % 2])
+    info = jnp.stack([lengths[0], place * tokens, lax.axis_index("dp"), place % 2, (place // 2) % 2])
     info = info.astype(jnp.int32)
 
     shape = jax.ShapeDtypeStruct
     halo = shape((HALO, 2 * width), BF16)
     block = shape((tokens, width), BF16)
-    near, far, meta = call(
+    half = head_weight.shape[0] // 2
+    near, far, meta, piece = call(
         pack_kernel,
-        (targets, label_mask, q, k, v),
-        (halo, halo, shape((tokens, 128), F32)),
+        (targets, label_mask, q, k, v, head_weight),
+        (halo, halo, shape((tokens, 128), F32), shape((half, vocab), BF16)),
         [
             pltpu.VMEM((2, 2 * EDGE, width), BF16),
             pltpu.VMEM((2, 1, tokens), jnp.int32),
-            pltpu.SemaphoreType.DMA((8,)),
+            pltpu.SemaphoreType.DMA((9,)),
         ],
-        "aaaaa",
+        "aaaaaa",
         0,
         56,
     )
     q_own, k_own, v_own = call(stage_kernel, (q, k, v), (block, block, block), [], "vvv", 0)
     near, far = exchanged(near, far, "ctx")
+    top_bit = bits_of(dp_size)[-1]
+    far_piece = swapped(piece, "dp", top_bit)
+    far_out = swapped(out_weight, "dp", top_bit)
+    far_rest = swapped(far_piece, "ctx", 2)
+    near, far, far_piece, far_out = lax.optimization_barrier((near, far, far_piece, far_out))
     ext = tokens + 2 * EDGE
     attn, lse, k_ext, v_ext, q_ext, meta_ext = call(
         attention_kernel,
@@ -479,20 +501,23 @@
         "svvvvvv",
         4 * tokens * 3 * WINDOW * width,
     )
-    top_bit = bits_of(dp_size)[-1]
-    first_hop = [swapped(head_weight, "dp", top_bit), swapped(out_weight, "dp", top_bit)]
-    attn, head_far, out_far = lax.optimization_barrier((attn, *first_hop))
-    held, marks = [], []
-    for weight, received in ((out_weight, out_far), (head_weight, head_far)):
-        pieces = [(0, weight), (top_bit, received)]
-        for bit in reversed(bits_of(dp_size)[:-1]):
-            pieces += [(mark ^ bit, swapped(item, "dp", bit)) for mark, item in pieces]
-        marks = [mark for mark, _ in pieces]
-        held += [item for _, item in pieces]
+    attn, far_rest = lax.optimization_barrier((attn, far_rest))
+    spread = [
+        [(0, 0, out_weight), (top_bit, 0, far_out)],
+        [(0, 0, head_weight)],
+        [(top_bit, 0, far_piece), (top_bit, 1, far_rest)],
+    ]
+    for bit in reversed(bits_of(dp_size)[:-1]):
+        spread = [
+            pieces + [(mark ^ bit, part, swapped(item, "dp", bit)) for mark, part, item in pieces]
+            for pieces in spread
+        ]
+    marks = [[(mark, part) for mark, part, _ in pieces] for pieces in spread]
+    held = [item for pieces in spread for _, _, item in pieces]
 
     chunks = depth // 128
     d_attn, stats, summary = call(
-        functools.partial(middle_kernel, tuple(marks)),
+        functools.partial(middle_kernel, marks),
         (info, attn, lse, meta_ext, conv_weight, *held),
         (
             shape((tokens, width), BF16),
@@ -509,9 +534,9 @@
             pltpu.VMEM((ext, vocab), BF16),
             pltpu.VMEM((chunks, ext, 128), F32),
             pltpu.VMEM((tokens, depth), BF16),
-            pltpu.SemaphoreType.DMA((2 * dp_size,)),
+            pltpu.SemaphoreType.DMA((len(held),)),
         ],
-        "svvvv" + "a" * (2 * dp_size),
+        "svvvv" + "a" * len(held),
         4 * tokens * depth * (width + vocab),
     )
 
@@ -525,30 +550,28 @@
         "svvvvv",
         16 * WINDOW * WINDOW * width,
     )
-    for index, group in enumerate(grouped(dp_bits)):
+    steps = [("ctx", ctx_bits[:1])]
+    steps += [("dp", group) for group in grouped(dp_bits)]
+    steps += [("ctx", group) for group in grouped(ctx_bits[1:])]
+    for index, (axis, group) in enumerate(steps):
         sent = packed(totals)
-        got = [swapped(sent, "dp", bit) for bit in group]
+        got = [swapped(sent, axis, bit) for bit in group]
         if index == 0:
-            near_part, far_part, *got = lax.optimization_barrier((near_part, far_part, *got))
-        totals = added([sent] + got)
-    sent = packed(totals)
-    near_part = jnp.concatenate([near_part, sent], axis=0)
-    near_got, far_got = exchanged(near_part, far_part, "ctx")
-    d_q, k_part, v_part = call(
-        own_grads_kernel,
-        (info, q_ext, k_ext, v_ext, stats, d_attn),
-        (block, shape((tokens, width), F32), shape((tokens, width), F32)),
-        [],
-        "svvvvv",
-        10 * tokens * 3 * WINDOW * width,
-    )
-    near_got, d_q, k_part, v_part = lax.optimization_barrier((near_got, d_q, k_part, v_part))
-    totals = added([sent, near_got[WINDOW:]])
-    groups = grouped(ctx_bits[1:])
-    for index, group in enumerate(groups):
-        sent = packed(totals)
-        got = [swapped(sent, "ctx", bit) for bit in group]
-        if index < len(groups) - 1:
+            near_part, far_part, d_attn, *got = lax.optimization_barrier(
+                (near_part, far_part, d_attn, *got)
+            )
+            near_got, far_got = exchanged(near_part, far_part, "ctx")
+        if index == len(steps) - 1:
+            d_q, k_part, v_part = call(
+                own_grads_kernel,
+                (info, q_ext, k_ext, v_ext, stats, d_attn),
+                (block, shape((tokens, width), F32), shape((tokens, width), F32)),
+                [],
+                "svvvvv",
+                0,
+            )
+            d_q, k_part, v_part, *got = lax.optimization_barrier((d_q, k_part, v_part, *got))
+        if index < len(steps) - 1:
             totals = added([sent] + got)
     d_k, d_v = call(
         add_kernel,

time: 59.1 us -> 56 us (0.948)
  starting transfers between devices: 16 us -> 20.1 us
  waiting for transfers between devices: 20.5 us -> 16.5 us
  Pallas kernels: 20.1 us -> 17 us
    ppermute x4, waiting for transfers between devices: 13.5 us -> 2.01 us  [exchanged(): return (lax.ppermute(near, axis, pairs), lax.ppermute(far, axis, others))]
    ppermute x12 -> x15, waiting for transfers between devices: 6.98 us -> 14.5 us  [swapped(): return lax.ppermute(value, axis, [(i, i ^ bit) for i in range(size)])]
    ppermute x12 -> x15, starting transfers between devices: 10.6 us -> 15.5 us  [swapped(): return lax.ppermute(value, axis, [(i, i ^ bit) for i in range(size)])]
    pallas_call x8, Pallas kernels: 20.1 us -> 17 us  [call(): pl.pallas_call(kernel, out_shape=outs, in_specs=[specs[place] for place i...]
    ppermute x4, starting transfers between devices: 5.38 us -> 4.67 us  [exchanged(): return (lax.ppermute(near, axis, pairs), lax.ppermute(far, axis, others))]
  transfers between devices with their start and end apart: 16 -> 19, of which waited for: 8 -> 9; matrix products, arithmetic and copies ran while one was open for 1% -> 1% of each run, Pallas kernels for 21% -> 11%
where the time goes in v2:
time: 56 us; the launch traced here: 55.8 us
  starting transfers between devices  20.1 us (36%)
  Pallas kernels  17 us (30%)
  waiting for transfers between devices  16.5 us (29%)
  between operations  1.68 us (3%)
    pallas_call x8, Pallas kernels, call(): pl.pallas_call(kernel, out_shape=outs, in_specs=[specs[place] for place i...  17 us
    ppermute x15, starting transfers between devices, swapped(): return lax.ppermute(value, axis, [(i, i ^ bit) for i in range(size)])  15.5 us
    ppermute x15, waiting for transfers between devices, swapped(): return lax.ppermute(value, axis, [(i, i ^ bit) for i in range(size)])  14.5 us
    ppermute x4, starting transfers between devices, exchanged(): return (lax.ppermute(near, axis, pairs), lax.ppermute(far, axis, others))  4.67 us
    ppermute x4, waiting for transfers between devices, exchanged(): return (lax.ppermute(near, axis, pairs), lax.ppermute(far, axis, others))  2.01 us
  transfers between devices with their start and end apart: 19, of which 9 were waited for; matrix products, arithmetic and copies ran while one was open for 1% of the time, Pallas kernels for 11%

profile of v2, /device:TPU:0, one launch (start us, length us, event | category | flops | bytes accessed | tf_op | source)
XLA Modules:
  0.0 55.8 jit_solution(13209510853613970185)
XLA Ops:
  0.7 2.4 %shard_map.129 = (bf16[144,1024]{1,0:T(8,128)(2,1)}, bf16[144,1024]{1,0:T(8,128)(2,1)}, f32[256,128]{1,0:T(8,128)}, bf16[128,1024]{1,0:T(8,128)(2,1)}) custom-call(s32[1,256]{1,0:T(1,128)} %targets.1, s32[1,256]{1,0:T(1,128)} %mask.1, bf16[256,512]{1,0:T(8,128)(2,1)} %bitcast.11, bf16[256,512]{1,0:T(8,128)(2,1)} %bitcast.13, bf16[256,512]{1,0:T(8,128)(2,1)} %bitcast.15, ...), custom_call_target="tpu_custom_call" | custom-call | flops 1 | bytes 1 | tf_op jit(solution)/shard_map/pallas_call | solution.py:433
  3.1 3.0 %collective-permute-start.2 = (bf16[128,1024]{1,0:T(8,128)(2,1)}, bf16[128,1024]{1,0:T(8,128)(2,1)S(1)}, u32[]{:S(2)}, u32[]{:S(2)}) collective-permute-start(bf16[128,1024]{1,0:T(8,128)(2,1)} %get-tuple-element.57), channel_id=1, source_target_pairs={{0,16},{8,24},{16,0},{24,8},{1,17},{9,25},{17,1},{25,9},{2,18},{10... | collective-permute-start | bytes 786440 | tf_op jit(solution)/shard_map/ppermute | solution.py:32
  6.1 1.5 %collective-permute-start = (bf16[144,1024]{1,0:T(8,128)(2,1)}, bf16[144,1024]{1,0:T(8,128)(2,1)S(1)}, u32[]{:S(2)}, u32[]{:S(2)}) collective-permute-start(bf16[144,1024]{1,0:T(8,128)(2,1)} %get-tuple-element.55), channel_id=1, source_target_pairs={{0,1},{1,0},{2,3},{3,2},{4,5},{5,4},{6,7},{7,6},{8,9},{9,8},{10,11... | collective-permute-start | bytes 884744 | tf_op jit(solution)/shard_map/ppermute | solution.py:39
  7.6 0.8 %collective-permute-start.1 = (bf16[144,1024]{1,0:T(8,128)(2,1)}, bf16[144,1024]{1,0:T(8,128)(2,1)S(1)}, u32[]{:S(2)}, u32[]{:S(2)}) collective-permute-start(bf16[144,1024]{1,0:T(8,128)(2,1)} %get-tuple-element.56), channel_id=1, source_target_pairs={{1,2},{2,1},{3,4},{4,3},{5,6},{6,5},{9,10},{10,9},{11,12},{12,11},... | collective-permute-start | bytes 884744 | tf_op jit(solution)/shard_map/ppermute | solution.py:39
  9.0 4.4 %collective-permute-done.2.refs_6_ = bf16[128,1024]{1,0:T(8,128)(2,1)S(1)} collective-permute-done((bf16[128,1024]{1,0:T(8,128)(2,1)}, bf16[128,1024]{1,0:T(8,128)(2,1)S(1)}, u32[]{:S(2)}, u32[]{:S(2)}) %collective-permute-start.2) | collective-permute-done | bytes 262176 | tf_op jit(solution)/shard_map/ppermute | solution.py:32
  13.4 1.9 %collective-permute-start.4 = (bf16[128,1024]{1,0:T(8,128)(2,1)S(1)}, bf16[128,1024]{1,0:T(8,128)(2,1)}, u32[]{:S(2)}, u32[]{:S(2)}) collective-permute-start(bf16[128,1024]{1,0:T(8,128)(2,1)S(1)} %collective-permute-done.2.refs_6_), channel_id=1, source_target_pairs={{0,2},{1,3},{2,0},{3,1},{4,6},{5,7},{6,4},{7,5},{8,10},{9,11},{10,... | collective-permute-start | bytes 786440 | tf_op jit(solution)/shard_map/ppermute | solution.py:32
  16.2 2.0 %collective-permute-done.3.refs_1_ = bf16[128,1024]{1,0:T(8,128)(2,1)S(1)} collective-permute-done((bf16[128,1024]{1,0:T(8,128)(2,1)}, bf16[128,1024]{1,0:T(8,128)(2,1)S(1)}, u32[]{:S(2)}, u32[]{:S(2)}) %collective-permute-start.3) | collective-permute-done | bytes 262176 | tf_op jit(solution)/shard_map/ppermute | solution.py:32
  18.2 2.0 %collective-permute-done.near = bf16[144,1024]{1,0:T(8,128)(2,1)S(1)} collective-permute-done((bf16[144,1024]{1,0:T(8,128)(2,1)}, bf16[144,1024]{1,0:T(8,128)(2,1)S(1)}, u32[]{:S(2)}, u32[]{:S(2)}) %collective-permute-start) | collective-permute-done | bytes 294944 | tf_op jit(solution)/shard_map/ppermute | solution.py:39
  20.7 2.1 %shard_map.130 = (bf16[288,512]{1,0:T(8,128)(2,1)S(1)}, f32[256,128]{1,0:T(8,128)S(1)}, bf16[544,512]{1,0:T(8,128)(2,1)S(1)}, bf16[544,512]{1,0:T(8,128)(2,1)S(1...) custom-call(s32[5]{0:T(128)S(1)} %stack.19.info, bf16[256,512]{1,0:T(8,128)(2,1)S(1)} %get-tuple-element.51.q, ...), custom_call_target="tpu_custom_call" | custom-call | flops 201326592 | bytes 3481620 | tf_op jit(solution)/shard_map/pallas_call | solution.py:433
  22.9 0.9 %collective-permute-done.4.refs_7_ = bf16[128,1024]{1,0:T(8,128)(2,1)} collective-permute-done((bf16[128,1024]{1,0:T(8,128)(2,1)S(1)}, bf16[128,1024]{1,0:T(8,128)(2,1)}, u32[]{:S(2)}, u32[]{:S(2)}) %collective-permute-start.4) | collective-permute-done | bytes 262176 | tf_op jit(solution)/shard_map/ppermute | solution.py:32
  23.7 1.7 %collective-permute-done.9.refs_9_ = bf16[128,1024]{1,0:T(8,128)(2,1)S(1)} collective-permute-done((bf16[128,1024]{1,0:T(8,128)(2,1)}, bf16[128,1024]{1,0:T(8,128)(2,1)S(1)}, u32[]{:S(2)}, u32[]{:S(2)}) %collective-permute-start.9) | collective-permute-done | bytes 262176 | tf_op jit(solution)/shard_map/ppermute | solution.py:32
  25.5 6.4 %shard_map.131 = (bf16[256,512]{1,0:T(8,128)(2,1)S(1)}, f32[256,128]{1,0:T(8,128)S(1)}, f32[16,1024]{1,0:T(8,128)S(1)}) custom-call(s32[5]{0:T(128)S(1)} %stack.19.info, bf16[288,512]{1,0:T(8,128)(2,1)S(1)} %get-tuple-element.61.attn, f32[256,128]{1,0:T(8,128)S(1)} %get-tuple-element.62.lse, f32[272,128]{1,0:T(8,128)S(1)} %get-tuple-element.63.meta_ext, ...), custom_call_target="tpu_custom_call" | custom-call | flops 1610612736 | bytes 4206612 | tf_op jit(solution)/shard_map/pallas_call | solution.py:433
  32.0 1.7 %collective-permute-start.10 = (bf16[12,1024]{1,0:T(8,128)(2,1)S(1)}, bf16[12,1024]{1,0:T(8,128)(2,1)S(1)}, u32[]{:S(2)}, u32[]{:S(2)}) collective-permute-start(bf16[12,1024]{1,0:T(8,128)(2,1)S(1)} %get-tuple-element.104), channel_id=1, source_target_pairs={{0,1},{1,0},{2,3},{3,2},{4,5},{5,4},{6,7},{7,6},{8,9},{9,8},{10,11... | collective-permute-start | bytes 73736 | tf_op jit(solution)/shard_map/ppermute | solution.py:32
  33.7 1.2 %shard_map.132 = (bf16[128,1024]{1,0:T(8,128)(2,1)S(1)}, bf16[128,1024]{1,0:T(8,128)(2,1)S(1)}) custom-call(s32[5]{0:T(128)S(1)} %stack.19.info, bf16[288,512]{1,0:T(8,128)(2,1)S(1)} %get-tuple-element.68.q_ext, bf16[544,512]{1,0:T(8,128)(2,1)S(1)} %get-tuple-element.69.k_ext, bf16[544,512]{1,0:T(8,128)(2,1)S(1)} %get-tuple-element.70.v_ext, ...), custom_call_target="tpu_custom_call" | custom-call | flops 134217728 | bytes 2326548 | tf_op jit(solution)/shard_map/pallas_call | solution.py:433
  34.9 1.0 %collective-permute-done.10 = bf16[12,1024]{1,0:T(8,128)(2,1)S(1)} collective-permute-done((bf16[12,1024]{1,0:T(8,128)(2,1)S(1)}, bf16[12,1024]{1,0:T(8,128)(2,1)S(1)}, u32[]{:S(2)}, u32[]{:S(2)}) %collective-permute-start.10) | collective-permute-done | bytes 24608 | tf_op jit(solution)/shard_map/ppermute | solution.py:32
  36.8 1.2 %collective-permute-start.11 = (bf16[12,1024]{1,0:T(8,128)(2,1)S(1)}, bf16[12,1024]{1,0:T(8,128)(2,1)S(1)}, u32[]{:S(2)}, u32[]{:S(2)}) collective-permute-start(bf16[12,1024]{1,0:T(8,128)(2,1)S(1)} %get-tuple-element.100), channel_id=1, source_target_pairs={{0,8},{8,0},{16,24},{24,16},{1,9},{9,1},{17,25},{25,17},{2,10},{10... | collective-permute-start | bytes 73736 | tf_op jit(solution)/shard_map/ppermute | solution.py:32
  38.1 1.7 %collective-permute-start.17 = (bf16[128,1024]{1,0:T(8,128)(2,1)S(1)}, bf16[128,1024]{1,0:T(8,128)(2,1)S(1)}, u32[]{:S(2)}, u32[]{:S(2)}) collective-permute-start(bf16[128,1024]{1,0:T(8,128)(2,1)S(1)} %get-tuple-element.82), channel_id=1, source_target_pairs={{0,1},{1,0},{2,3},{3,2},{4,5},{5,4},{6,7},{7,6},{8,9},{9,8},{10,11... | collective-permute-start | bytes 786440 | tf_op jit(solution)/shard_map/ppermute | solution.py:39
  40.8 3.2 %collective-permute-start.14 = (bf16[12,1024]{1,0:T(8,128)(2,1)S(1)}, bf16[12,1024]{1,0:T(8,128)(2,1)S(1)}, u32[]{:S(2)}, u32[]{:S(2)}) collective-permute-start(bf16[12,1024]{1,0:T(8,128)(2,1)S(1)} %pad_maximum_fusion.2.refs_0_), channel_id=1, source_target_pairs={{0,2},{1,3},{2,0},{3,1},{4,6},{5,7},{6,4},{7,5},{8,10},{9,11},{10,... | collective-permute-start | bytes 73736 | tf_op jit(solution)/shard_map/ppermute | solution.py:32
  43.9 2.7 %collective-permute-start.15 = (bf16[12,1024]{1,0:T(8,128)(2,1)S(1)}, bf16[12,1024]{1,0:T(8,128)(2,1)S(1)}, u32[]{:S(2)}, u32[]{:S(2)}) collective-permute-start(bf16[12,1024]{1,0:T(8,128)(2,1)S(1)} %pad_maximum_fusion.2.refs_0_), channel_id=1, source_target_pairs={{0,4},{1,5},{2,6},{3,7},{4,0},{5,1},{6,2},{7,3},{8,12},{9,13},{10,... | collective-permute-start | bytes 73736 | tf_op jit(solution)/shard_map/ppermute | solution.py:32
  46.6 2.6 %shard_map.133 = (bf16[256,512]{1,0:T(8,128)(2,1)}, f32[256,512]{1,0:T(8,128)S(1)}, f32[256,512]{1,0:T(8,128)S(1)}) custom-call(s32[5]{0:T(128)S(1)} %stack.19.info, bf16[288,512]{1,0:T(8,128)(2,1)S(1)} %get-tuple-element.68.q_ext, bf16[544,512]{1,0:T(8,128)(2,1)S(1)} %get-tuple-element.69.k_ext, bf16[544,512]{1,0:T(8,128)(2,1)S(1)} %get-tuple-element.70.v_ext, ...), custom_call_target="tpu_custom_call" | custom-call | flops 1 | bytes 1 | tf_op jit(solution)/shard_map/pallas_call | solution.py:433
  49.2 1.3 %collective-permute-done.14.refs_1_ = bf16[12,1024]{1,0:T(8,128)(2,1)S(1)} collective-permute-done((bf16[12,1024]{1,0:T(8,128)(2,1)S(1)}, bf16[12,1024]{1,0:T(8,128)(2,1)S(1)}, u32[]{:S(2)}, u32[]{:S(2)}) %collective-permute-start.14) | collective-permute-done | bytes 24608 | tf_op jit(solution)/shard_map/ppermute | solution.py:32
  50.5 1.7 %collective-permute-done.15.refs_2_ = bf16[12,1024]{1,0:T(8,128)(2,1)S(1)} collective-permute-done((bf16[12,1024]{1,0:T(8,128)(2,1)S(1)}, bf16[12,1024]{1,0:T(8,128)(2,1)S(1)}, u32[]{:S(2)}, u32[]{:S(2)}) %collective-permute-start.15) | collective-permute-done | bytes 24608 | tf_op jit(solution)/shard_map/ppermute | solution.py:32
  52.2 1.5 %collective-permute-done.16.refs_3_ = bf16[12,1024]{1,0:T(8,128)(2,1)S(1)} collective-permute-done((bf16[12,1024]{1,0:T(8,128)(2,1)S(1)}, bf16[12,1024]{1,0:T(8,128)(2,1)S(1)}, u32[]{:S(2)}, u32[]{:S(2)}) %collective-permute-start.16) | collective-permute-done | bytes 24608 | tf_op jit(solution)/shard_map/ppermute | solution.py:32
  53.7 1.4 %shard_map.134 = (bf16[256,512]{1,0:T(8,128)(2,1)}, bf16[256,512]{1,0:T(8,128)(2,1)}) custom-call(s32[5]{0:T(128)S(1)} %stack.19.info, f32[256,512]{1,0:T(8,128)S(1)} %get-tuple-element.80.k_part, f32[256,512]{1,0:T(8,128)S(1)} %get-tuple-element.81.v_part, bf16[128,1024]{1,0:T(8,128)(2,1)S(1)} %collective-permute-done.17.near, ...), custom_call_target="tpu_custom_call" | custom-call | flops 131072 | bytes 2097172 | tf_op jit(solution)/shard_map/pallas_call | solution.py:433
  (66 shorter events, 3.8 us)
Async XLA Ops:
  0.6 14.7 %copy-start.3 = (bf16[256,1024]{1,0:T(8,128)(2,1)S(1)}, bf16[256,1024]{1,0:T(8,128)(2,1)}, u32[]{:S(2)}) copy-start(bf16[256,1024]{1,0:T(8,128)(2,1)} %refs_4_.1) | copy-start | bytes 1572868
  0.6 14.7 %copy-start = (bf16[1,256,512]{2,1,0:T(8,128)(2,1)S(1)}, bf16[1,256,512]{2,1,0:T(8,128)(2,1)}, u32[]{:S(2)}) copy-start(bf16[1,256,512]{2,1,0:T(8,128)(2,1)} %param.9) | copy-start | bytes 786436
  0.7 14.6 %copy-start.1 = (bf16[1,256,512]{2,1,0:T(8,128)(2,1)S(1)}, bf16[1,256,512]{2,1,0:T(8,128)(2,1)}, u32[]{:S(2)}) copy-start(bf16[1,256,512]{2,1,0:T(8,128)(2,1)} %param.10) | copy-start | bytes 786436
  0.7 14.6 %copy-start.2 = (bf16[1,256,512]{2,1,0:T(8,128)(2,1)S(1)}, bf16[1,256,512]{2,1,0:T(8,128)(2,1)}, u32[]{:S(2)}) copy-start(bf16[1,256,512]{2,1,0:T(8,128)(2,1)} %param.11) | copy-start | bytes 786436
  3.1 10.3 %collective-permute-start.2 = (bf16[128,1024]{1,0:T(8,128)(2,1)}, bf16[128,1024]{1,0:T(8,128)(2,1)S(1)}, u32[]{:S(2)}, u32[]{:S(2)}) collective-permute-start(bf16[128,1024]{1,0:T(8,128)(2,1)} %get-tuple-element.57), channel_id=1, source_target_pairs={{0,16},{8,24},{16,0},{24,8},{1,17},{9,25},{17,1},{25,9},{2,18},{10... | collective-permute-start | bytes 786440 | tf_op jit(solution)/shard_map/ppermute | solution.py:32
  6.1 14.1 %collective-permute-start = (bf16[144,1024]{1,0:T(8,128)(2,1)}, bf16[144,1024]{1,0:T(8,128)(2,1)S(1)}, u32[]{:S(2)}, u32[]{:S(2)}) collective-permute-start(bf16[144,1024]{1,0:T(8,128)(2,1)} %get-tuple-element.55), channel_id=1, source_target_pairs={{0,1},{1,0},{2,3},{3,2},{4,5},{5,4},{6,7},{7,6},{8,9},{9,8},{10,11... | collective-permute-start | bytes 884744 | tf_op jit(solution)/shard_map/ppermute | solution.py:39
  7.6 10.6 %copy-start.5 = (bf16[128,1024]{1,0:T(8,128)(2,1)S(1)}, bf16[128,1024]{1,0:T(8,128)(2,1)}, u32[]{:S(2)}) copy-start(bf16[128,1024]{1,0:T(8,128)(2,1)} %refs_0_.1) | copy-start | bytes 786436
  7.6 12.6 %collective-permute-start.1 = (bf16[144,1024]{1,0:T(8,128)(2,1)}, bf16[144,1024]{1,0:T(8,128)(2,1)S(1)}, u32[]{:S(2)}, u32[]{:S(2)}) collective-permute-start(bf16[144,1024]{1,0:T(8,128)(2,1)} %get-tuple-element.56), channel_id=1, source_target_pairs={{1,2},{2,1},{3,4},{4,3},{5,6},{6,5},{9,10},{10,9},{11,12},{12,11},... | collective-permute-start | bytes 884744 | tf_op jit(solution)/shard_map/ppermute | solution.py:39
  8.4 9.8 %collective-permute-start.3 = (bf16[128,1024]{1,0:T(8,128)(2,1)}, bf16[128,1024]{1,0:T(8,128)(2,1)S(1)}, u32[]{:S(2)}, u32[]{:S(2)}) collective-permute-start(bf16[128,1024]{1,0:T(8,128)(2,1)} %refs_0_.1), channel_id=1, source_target_pairs={{0,16},{8,24},{16,0},{24,8},{1,17},{9,25},{17,1},{25,9},{2,18},{10... | collective-permute-start | bytes 786440 | tf_op jit(solution)/shard_map/ppermute | solution.py:32
  13.4 10.3 %collective-permute-start.4 = (bf16[128,1024]{1,0:T(8,128)(2,1)S(1)}, bf16[128,1024]{1,0:T(8,128)(2,1)}, u32[]{:S(2)}, u32[]{:S(2)}) collective-permute-start(bf16[128,1024]{1,0:T(8,128)(2,1)S(1)} %collective-permute-done.2.refs_6_), channel_id=1, source_target_pairs={{0,2},{1,3},{2,0},{3,1},{4,6},{5,7},{6,4},{7,5},{8,10},{9,11},{10,... | collective-permute-start | bytes 786440 | tf_op jit(solution)/shard_map/ppermute | solution.py:32
  15.3 8.4 %collective-permute-start.7 = (bf16[256,1024]{1,0:T(8,128)(2,1)S(1)}, bf16[256,1024]{1,0:T(8,128)(2,1)S(1)}, u32[]{:S(2)}, u32[]{:S(2)}) collective-permute-start(bf16[256,1024]{1,0:T(8,128)(2,1)S(1)} %copy-done.3), channel_id=1, source_target_pairs={{0,8},{8,0},{16,24},{24,16},{1,9},{9,1},{17,25},{25,17},{2,10},{10... | collective-permute-start | bytes 1572872 | tf_op jit(solution)/shard_map/ppermute | solution.py:32
  18.2 5.5 %collective-permute-start.5 = (bf16[128,1024]{1,0:T(8,128)(2,1)S(1)}, bf16[128,1024]{1,0:T(8,128)(2,1)S(1)}, u32[]{:S(2)}, u32[]{:S(2)}) collective-permute-start(bf16[128,1024]{1,0:T(8,128)(2,1)S(1)} %copy-done.5), channel_id=1, source_target_pairs={{0,8},{8,0},{16,24},{24,16},{1,9},{9,1},{17,25},{25,17},{2,10},{10... | collective-permute-start | bytes 786440 | tf_op jit(solution)/shard_map/ppermute | solution.py:32
  20.2 3.5 %collective-permute-start.6 = (bf16[128,1024]{1,0:T(8,128)(2,1)S(1)}, bf16[128,1024]{1,0:T(8,128)(2,1)S(1)}, u32[]{:S(2)}, u32[]{:S(2)}) collective-permute-start(bf16[128,1024]{1,0:T(8,128)(2,1)S(1)} %collective-permute-done.3.refs_1_), channel_id=1, source_target_pairs={{0,8},{8,0},{16,24},{24,16},{1,9},{9,1},{17,25},{25,17},{2,10},{10... | collective-permute-start | bytes 786440 | tf_op jit(solution)/shard_map/ppermute | solution.py:32
  20.2 3.5 %collective-permute-start.8 = (bf16[128,1024]{1,0:T(8,128)(2,1)S(1)}, bf16[128,1024]{1,0:T(8,128)(2,1)S(1)}, u32[]{:S(2)}, u32[]{:S(2)}) collective-permute-start(bf16[128,1024]{1,0:T(8,128)(2,1)S(1)} %collective-permute-done.2.refs_6_), channel_id=1, source_target_pairs={{0,8},{8,0},{16,24},{24,16},{1,9},{9,1},{17,25},{25,17},{2,10},{10... | collective-permute-start | bytes 786440 | tf_op jit(solution)/shard_map/ppermute | solution.py:32
  23.7 1.7 %collective-permute-start.9 = (bf16[128,1024]{1,0:T(8,128)(2,1)}, bf16[128,1024]{1,0:T(8,128)(2,1)S(1)}, u32[]{:S(2)}, u32[]{:S(2)}) collective-permute-start(bf16[128,1024]{1,0:T(8,128)(2,1)} %collective-permute-done.4.refs_7_), channel_id=1, source_target_pairs={{0,8},{8,0},{16,24},{24,16},{1,9},{9,1},{17,25},{25,17},{2,10},{10... | collective-permute-start | bytes 786440 | tf_op jit(solution)/shard_map/ppermute | solution.py:32
  32.0 4.0 %collective-permute-start.10 = (bf16[12,1024]{1,0:T(8,128)(2,1)S(1)}, bf16[12,1024]{1,0:T(8,128)(2,1)S(1)}, u32[]{:S(2)}, u32[]{:S(2)}) collective-permute-start(bf16[12,1024]{1,0:T(8,128)(2,1)S(1)} %get-tuple-element.104), channel_id=1, source_target_pairs={{0,1},{1,0},{2,3},{3,2},{4,5},{5,4},{6,7},{7,6},{8,9},{9,8},{10,11... | collective-permute-start | bytes 73736 | tf_op jit(solution)/shard_map/ppermute | solution.py:32
  36.1 4.3 %collective-permute-start.13 = (bf16[12,1024]{1,0:T(8,128)(2,1)S(1)}, bf16[12,1024]{1,0:T(8,128)(2,1)S(1)}, u32[]{:S(2)}, u32[]{:S(2)}) collective-permute-start(bf16[12,1024]{1,0:T(8,128)(2,1)S(1)} %get-tuple-element.100), channel_id=1, source_target_pairs={{0,24},{8,16},{16,8},{24,0},{1,25},{9,17},{17,9},{25,1},{2,26},{10... | collective-permute-start | bytes 73736 | tf_op jit(solution)/shard_map/ppermute | solution.py:32
  36.2 4.3 %collective-permute-start.12 = (bf16[12,1024]{1,0:T(8,128)(2,1)S(1)}, bf16[12,1024]{1,0:T(8,128)(2,1)S(1)}, u32[]{:S(2)}, u32[]{:S(2)}) collective-permute-start(bf16[12,1024]{1,0:T(8,128)(2,1)S(1)} %get-tuple-element.100), channel_id=1, source_target_pairs={{0,16},{8,24},{16,0},{24,8},{1,17},{9,25},{17,1},{25,9},{2,18},{10... | collective-permute-start | bytes 73736 | tf_op jit(solution)/shard_map/ppermute | solution.py:32
  36.8 3.7 %collective-permute-start.11 = (bf16[12,1024]{1,0:T(8,128)(2,1)S(1)}, bf16[12,1024]{1,0:T(8,128)(2,1)S(1)}, u32[]{:S(2)}, u32[]{:S(2)}) collective-permute-start(bf16[12,1024]{1,0:T(8,128)(2,1)S(1)} %get-tuple-element.100), channel_id=1, source_target_pairs={{0,8},{8,0},{16,24},{24,16},{1,9},{9,1},{17,25},{25,17},{2,10},{10... | collective-permute-start | bytes 73736 | tf_op jit(solution)/shard_map/ppermute | solution.py:32
  38.1 15.6 %collective-permute-start.17 = (bf16[128,1024]{1,0:T(8,128)(2,1)S(1)}, bf16[128,1024]{1,0:T(8,128)(2,1)S(1)}, u32[]{:S(2)}, u32[]{:S(2)}) collective-permute-start(bf16[128,1024]{1,0:T(8,128)(2,1)S(1)} %get-tuple-element.82), channel_id=1, source_target_pairs={{0,1},{1,0},{2,3},{3,2},{4,5},{5,4},{6,7},{7,6},{8,9},{9,8},{10,11... | collective-permute-start | bytes 786440 | tf_op jit(solution)/shard_map/ppermute | solution.py:39
  39.7 13.9 %collective-permute-start.18 = (bf16[128,1024]{1,0:T(8,128)(2,1)S(1)}, bf16[128,1024]{1,0:T(8,128)(2,1)S(1)}, u32[]{:S(2)}, u32[]{:S(2)}) collective-permute-start(bf16[128,1024]{1,0:T(8,128)(2,1)S(1)} %get-tuple-element.83), channel_id=1, source_target_pairs={{1,2},{2,1},{3,4},{4,3},{5,6},{6,5},{9,10},{10,9},{11,12},{12,11},... | collective-permute-start | bytes 786440 | tf_op jit(solution)/shard_map/ppermute | solution.py:39
  40.8 9.8 %collective-permute-start.14 = (bf16[12,1024]{1,0:T(8,128)(2,1)S(1)}, bf16[12,1024]{1,0:T(8,128)(2,1)S(1)}, u32[]{:S(2)}, u32[]{:S(2)}) collective-permute-start(bf16[12,1024]{1,0:T(8,128)(2,1)S(1)} %pad_maximum_fusion.2.refs_0_), channel_id=1, source_target_pairs={{0,2},{1,3},{2,0},{3,1},{4,6},{5,7},{6,4},{7,5},{8,10},{9,11},{10,... | collective-permute-start | bytes 73736 | tf_op jit(solution)/shard_map/ppermute | solution.py:32
  43.9 8.3 %collective-permute-start.15 = (bf16[12,1024]{1,0:T(8,128)(2,1)S(1)}, bf16[12,1024]{1,0:T(8,128)(2,1)S(1)}, u32[]{:S(2)}, u32[]{:S(2)}) collective-permute-start(bf16[12,1024]{1,0:T(8,128)(2,1)S(1)} %pad_maximum_fusion.2.refs_0_), channel_id=1, source_target_pairs={{0,4},{1,5},{2,6},{3,7},{4,0},{5,1},{6,2},{7,3},{8,12},{9,13},{10,... | collective-permute-start | bytes 73736 | tf_op jit(solution)/shard_map/ppermute | solution.py:32
  46.6 7.1 %collective-permute-start.16 = (bf16[12,1024]{1,0:T(8,128)(2,1)S(1)}, bf16[12,1024]{1,0:T(8,128)(2,1)S(1)}, u32[]{:S(2)}, u32[]{:S(2)}) collective-permute-start(bf16[12,1024]{1,0:T(8,128)(2,1)S(1)} %pad_maximum_fusion.2.refs_0_), channel_id=1, source_target_pairs={{0,6},{1,7},{2,4},{3,5},{4,2},{5,3},{6,0},{7,1},{8,14},{9,15},{10,... | collective-permute-start | bytes 73736 | tf_op jit(solution)/shard_map/ppermute | solution.py:32
  (2 other events, 10.1 us)

commit v3 on v2

--- a/solution.py
+++ b/solution.py
@@ -32,6 +32,12 @@
     return lax.ppermute(value, axis, [(i, i ^ bit) for i in range(size)])
 
 
+def spread(pieces, axis):
+    for bit in reversed(bits_of(lax.axis_size(axis))[:-1]):
+        pieces = pieces + [(mark ^ bit, swapped(item, axis, bit)) for mark, item in pieces]
+    return [mark for mark, _ in pieces], [item for _, item in pieces]
+
+
 def exchanged(near, far, axis):
     size = lax.axis_size(axis)
     pairs = [(i, i ^ 1) for i in range(size) if (i ^ 1) < size]
@@ -59,9 +65,8 @@
     )
 
 
-def pack_kernel(targets, mask, q, k, v, head, near, far, meta, piece, edges, marks, sems):
+def pack_kernel(targets, mask, q, k, v, near, far, meta, edges, marks, sems):
     tokens, width = q.shape
-    half = piece.shape[0]
     even = lax.rem(lax.axis_index("ctx"), 2) == 0
     edge = 2 * EDGE
     ends = (slice(0, edge), slice(tokens - edge, tokens))
@@ -79,8 +84,6 @@
         fetch(v.at[pl.ds(first, HALO)], message.at[:, width : 2 * width])
     for place, end in enumerate(ends):
         fetch(q.at[end], edges.at[place])
-    start = pl.multiple_of(lax.rem(lax.axis_index("ctx") // 2, 2) * half, half)
-    fetch(head.at[pl.ds(start, half)], piece)
     fetch(targets, marks.at[0])
     fetch(mask, marks.at[1])
     for copy in copies[-2:]:
@@ -116,7 +119,8 @@
         patch(far, 0, low, 1)
 
 
-def stage_kernel(q, k, v, q_own, k_own, v_own):
+def stage_kernel(q, k, v, meta, q_own, k_own, v_own, meta_own):
+    meta_own[...] = meta[...]
     q_own[...] = q[...]
     k_own[...] = k[...]
     v_own[...] = v[...]
@@ -194,46 +198,49 @@
         scores = later
 
 
-def middle_kernel(marks, info, attn, lse, meta_ext, taps, *refs):
-    count = sum(len(pieces) for pieces in marks)
-    held = list(refs[:count])
-    d_attn, stats, summary = refs[count : count + 3]
-    (
-        out_full, head_full, hid, gated, slope, logits, d_logits, d_pre, d_hid, sems,
-    ) = refs[count + 3 :]
-    length, offset, mine = info[0], info[1], info[2]
+def fetch_pieces(marks, mine, pieces, full, sems):
     copies = []
-    for full, pieces, halves in ((out_full, marks[0], 1), (head_full, marks[1], 1), (head_full, marks[2], 2)):
-        for mark, part in pieces:
-            source = held[len(copies)]
-            rows = source.shape[0]
-            start = (mine ^ mark) * (rows * halves)
-            if halves == 2:
-                start = start + (info[4] ^ part) * rows
-            target = full.at[pl.ds(pl.multiple_of(start, rows), rows)]
-            copy = pltpu.make_async_copy(source, target, sems.at[len(copies)])
-            copy.start()
-            copies.append(copy)
-    tokens, width = d_attn.shape
-    depth = out_full.shape[1]
-    vocab = head_full.shape[1]
-    ext = tokens + 2 * EDGE
-    lanes = 128
-
-    row_pos = offset - EDGE + lax.broadcasted_iota(jnp.int32, (ext, lanes), 0)
-    live = (row_pos >= 0) & (row_pos < length)
-    hid[:, 0:EDGE, :] = jnp.zeros((depth // lanes, EDGE, lanes), F32)
-    hid[:, EDGE + ext :, :] = jnp.zeros((depth // lanes, EDGE, lanes), F32)
-    for copy in copies[: len(marks[0])]:
+    for mark, piece in zip(marks, pieces):
+        rows = piece.shape[0]
+        target = full.at[pl.ds(pl.multiple_of((mine ^ mark) * rows, rows), rows)]
+        copies.append(pltpu.make_async_copy(piece, target, sems.at[len(copies)]))
+        copies[-1].start()
+    return copies
+
+
+def live_rows(info, rows, lanes):
+    row_pos = info[1] - EDGE + lax.broadcasted_iota(jnp.int32, (rows, lanes), 0)
+    return (row_pos >= 0) & (row_pos < info[0])
+
+
+def hidden_kernel(marks, info, attn, *refs):
+    pieces, (hid, out_full, sems) = refs[: len(marks)], refs[len(marks) :]
+    copies = fetch_pieces(marks, info[2], pieces, out_full, sems)
+    chunks, ext, lanes = hid.shape
+    ext = ext - 2 * EDGE
+    live = live_rows(info, ext, lanes)
+    hid[:, 0:EDGE, :] = jnp.zeros((chunks, EDGE, lanes), F32)
+    hid[:, EDGE + ext :, :] = jnp.zeros((chunks, EDGE, lanes), F32)
+    for copy in copies:
         copy.wait()
-    for at in range(0, depth, 256):
+    last = attn.shape[0] - 16
+    for at in range(0, chunks * lanes, 256):
         block = nn(attn[...], out_full[:, at : at + 256])
-        block = jnp.concatenate(
-            [block[0:EDGE], block[16 : 16 + tokens], block[16 + tokens + EDGE :]], axis=0
-        )
+        block = jnp.concatenate([block[0:EDGE], block[16:last], block[last + EDGE :]], axis=0)
         for part in range(2):
             piece = block[:, part * lanes : (part + 1) * lanes]
             hid[at // lanes + part, EDGE : EDGE + ext, :] = jnp.where(live, piece, 0.0)
+
+
+def middle_kernel(marks, info, attn, lse, meta_ext, taps, hid, out_full, *refs):
+    pieces, (d_attn, stats, summary) = refs[: len(marks)], refs[len(marks) : len(marks) + 3]
+    head_full, gated, slope, logits, d_logits, d_pre, d_hid, sems = refs[len(marks) + 3 :]
+    copies = fetch_pieces(marks, info[2], pieces, head_full, sems)
+    tokens, width = d_attn.shape
+    depth, vocab = head_full.shape
+    ext = tokens + 2 * EDGE
+    lanes = 128
+    live = live_rows(info, ext, lanes)
     for chunk in range(depth // lanes):
         cols = slice(chunk * lanes, (chunk + 1) * lanes)
         conv = jnp.zeros((ext, lanes), F32)
@@ -243,7 +250,7 @@
         sigma = jax.nn.sigmoid(conv)
         gated[:, cols] = (conv * sigma).astype(BF16)
         slope[chunk] = sigma * (1.0 + conv * (1.0 - sigma))
-    for copy in copies[len(marks[0]) :]:
+    for copy in copies:
         copy.wait()
     for at in range(0, vocab, 256):
         logits[:, at : at + 256] = nn(gated[...], head_full[:, at : at + 256])
@@ -369,7 +376,34 @@
         products = later
 
 
-def add_kernel(info, k_part, v_part, near, far, d_k, d_v):
+def grouped(bits):
+    pairs = [bits[at : at + 2] for at in range(0, len(bits), 2)]
+    return [pair + [pair[0] ^ pair[1]] if len(pair) == 2 else pair for pair in pairs]
+
+
+def packed(totals):
+    rounded = lax.reduce_precision(totals[:TAPS], 8, 7)
+    first = lax.reduce_precision(totals[TAPS:], 8, 7)
+    second = lax.reduce_precision(totals[TAPS:] - first, 8, 7)
+    third = totals[TAPS:] - first - second
+    return jnp.concatenate([rounded, first, second, third], axis=0).astype(BF16)
+
+
+def unpacked(sent):
+    wide = sent.astype(F32)
+    last = wide[TAPS : TAPS + 1] + wide[TAPS + 1 : TAPS + 2] + wide[TAPS + 2 : TAPS + 3]
+    return jnp.concatenate([wide[:TAPS], last], axis=0)
+
+
+def added(parts):
+    sums = [unpacked(part) for part in parts]
+    while len(sums) > 1:
+        sums = [sums[at] + sums[at + 1] for at in range(0, len(sums), 2)]
+    return sums[0]
+
+
+def finish_kernel(info, k_part, v_part, near, far, *refs):
+    parts, (d_k, d_v, d_conv, loss) = refs[:-4], refs[-4:]
     tokens, width = d_k.shape
     even = info[3] == 0
     for got, on_right in ((near, even), (far, ~even)):
@@ -378,37 +412,7 @@
             (d_k, k_part, slice(0, width)),
             (d_v, v_part, slice(width, 2 * width)),
         ):
-            out[rows, :] = (part[rows, :] + got[0:WINDOW, cols].astype(F32)).astype(BF16)
-
-
-def grouped(bits):
-    pairs = [bits[at : at + 2] for at in range(0, len(bits), 2)]
-    return [pair + [pair[0] ^ pair[1]] if len(pair) == 2 else pair for pair in pairs]
-
-
-def packed(totals):
-    rounded = lax.reduce_precision(totals[:TAPS], 8, 7)
-    first = lax.reduce_precision(totals[TAPS:], 8, 7)
-    second = lax.reduce_precision(totals[TAPS:] - first, 8, 7)
-    third = totals[TAPS:] - first - second
-    return jnp.concatenate([rounded, first, second, third], axis=0).astype(BF16)
-
-
-def unpacked(sent):
-    wide = sent.astype(F32)
-    last = wide[TAPS : TAPS + 1] + wide[TAPS + 1 : TAPS + 2] + wide[TAPS + 2 : TAPS + 3]
-    return jnp.concatenate([wide[:TAPS], last], axis=0)
-
-
-def added(parts):
-    sums = [unpacked(part) for part in parts]
-    while len(sums) > 1:
-        sums = [sums[at] + sums[at + 1] for at in range(0, len(sums), 2)]
-    return sums[0]
-
-
-def finish_kernel(*refs):
-    parts, (d_conv, loss) = refs[:-2], refs[-2:]
+            out[rows, :] = (part[rows, :] + got[:, cols].astype(F32)).astype(BF16)
     taps = [part[...].astype(F32)[0:TAPS] for part in parts]
     sums = []
     for part in parts:
@@ -458,33 +462,41 @@
     dp_size = lax.axis_size("dp")
     place = lax.axis_index("ctx")
     q, k, v = queries[0], key_rows[0], value_rows[0]
-    info = jnp.stack([lengths[0], place * tokens, lax.axis_index("dp"), place % 2, (place // 2) % 2])
+    info = jnp.stack([lengths[0], place * tokens, lax.axis_index("dp"), place % 2])
     info = info.astype(jnp.int32)
 
     shape = jax.ShapeDtypeStruct
     halo = shape((HALO, 2 * width), BF16)
     block = shape((tokens, width), BF16)
-    half = head_weight.shape[0] // 2
-    near, far, meta, piece = call(
+    near, far, meta = call(
         pack_kernel,
-        (targets, label_mask, q, k, v, head_weight),
-        (halo, halo, shape((tokens, 128), F32), shape((half, vocab), BF16)),
+        (targets, label_mask, q, k, v),
+        (halo, halo, shape((tokens, 128), F32)),
         [
             pltpu.VMEM((2, 2 * EDGE, width), BF16),
             pltpu.VMEM((2, 1, tokens), jnp.int32),
-            pltpu.SemaphoreType.DMA((9,)),
+            pltpu.SemaphoreType.DMA((8,)),
         ],
-        "aaaaaa",
+        "aaaaa",
         0,
         56,
     )
-    q_own, k_own, v_own = call(stage_kernel, (q, k, v), (block, block, block), [], "vvv", 0)
+    q_own, k_own, v_own, meta = call(
+        stage_kernel,
+        (q, k, v, meta),
+        (block, block, block, shape((tokens, 128), F32)),
+        [],
+        "vvvv",
+        0,
+    )
+    near, far, head_weight = lax.optimization_barrier((near, far, head_weight))
     near, far = exchanged(near, far, "ctx")
     top_bit = bits_of(dp_size)[-1]
-    far_piece = swapped(piece, "dp", top_bit)
     far_out = swapped(out_weight, "dp", top_bit)
-    far_rest = swapped(far_piece, "ctx", 2)
-    near, far, far_piece, far_out = lax.optimization_barrier((near, far, far_piece, far_out))
+    far_head = swapped(head_weight, "dp", top_bit)
+    out_marks, out_held = spread([(0, out_weight), (top_bit, far_out)], "dp")
+    near, far, *out_held = lax.optimization_barrier((near, far, *out_held))
+
     ext = tokens + 2 * EDGE
     attn, lse, k_ext, v_ext, q_ext, meta_ext = call(
         attention_kernel,
@@ -501,42 +513,37 @@
         "svvvvvv",
         4 * tokens * 3 * WINDOW * width,
     )
-    attn, far_rest = lax.optimization_barrier((attn, far_rest))
-    spread = [
-        [(0, 0, out_weight), (top_bit, 0, far_out)],
-        [(0, 0, head_weight)],
-        [(top_bit, 0, far_piece), (top_bit, 1, far_rest)],
-    ]
-    for bit in reversed(bits_of(dp_size)[:-1]):
-        spread = [
-            pieces + [(mark ^ bit, part, swapped(item, "dp", bit)) for mark, part, item in pieces]
-            for pieces in spread
-        ]
-    marks = [[(mark, part) for mark, part, _ in pieces] for pieces in spread]
-    held = [item for pieces in spread for _, _, item in pieces]
+    attn, far_head = lax.optimization_barrier((attn, far_head))
+    head_marks, head_held = spread([(0, head_weight), (top_bit, far_head)], "dp")
 
     chunks = depth // 128
+    hid, out_full = call(
+        functools.partial(hidden_kernel, out_marks),
+        (info, attn, *out_held),
+        (shape((chunks, ext + 2 * EDGE, 128), F32), shape((width, depth), BF16)),
+        [pltpu.SemaphoreType.DMA((len(out_held),))],
+        "sv" + "a" * len(out_held),
+        2 * tokens * depth * width,
+    )
     d_attn, stats, summary = call(
-        functools.partial(middle_kernel, marks),
-        (info, attn, lse, meta_ext, conv_weight, *held),
+        functools.partial(middle_kernel, head_marks),
+        (info, attn, lse, meta_ext, conv_weight, hid, out_full, *head_held),
         (
             shape((tokens, width), BF16),
             shape((tokens, 128), F32),
             shape((16, depth), F32),
         ),
         [
-            pltpu.VMEM((width, depth), BF16),
             pltpu.VMEM((depth, vocab), BF16),
-            pltpu.VMEM((chunks, ext + 2 * EDGE, 128), F32),
             pltpu.VMEM((ext, depth), BF16),
             pltpu.VMEM((chunks, ext, 128), F32),
             pltpu.VMEM((ext, vocab), F32),
             pltpu.VMEM((ext, vocab), BF16),
             pltpu.VMEM((chunks, ext, 128), F32),
             pltpu.VMEM((tokens, depth), BF16),
-            pltpu.SemaphoreType.DMA((len(held),)),
+            pltpu.SemaphoreType.DMA((len(head_held),)),
         ],
-        "svvvv" + "a" * len(held),
+        "svvvvvv" + "a" * len(head_held),
         4 * tokens * depth * (width + vocab),
     )
 
@@ -573,22 +580,13 @@
             d_q, k_part, v_part, *got = lax.optimization_barrier((d_q, k_part, v_part, *got))
         if index < len(steps) - 1:
             totals = added([sent] + got)
-    d_k, d_v = call(
-        add_kernel,
-        (info, k_part, v_part, near_got, far_got),
-        (block, block),
+    d_k, d_v, d_conv, loss = call(
+        finish_kernel,
+        (info, k_part, v_part, near_got, far_got, sent, *got),
+        (block, block, shape((TAPS, depth), F32), shape((1, 1), F32)),
         [],
-        "svvvv",
+        "svvvv" + "v" * (1 + len(got)),
         tokens * width,
-    )
-    d_k, d_v, *got = lax.optimization_barrier((d_k, d_v, *got))
-    d_conv, loss = call(
-        finish_kernel,
-        (sent, *got),
-        (shape((TAPS, depth), F32), shape((1, 1), F32)),
-        [],
-        "v" * (1 + len(got)),
-        0,
     )
     return (loss[0, 0], d_q[None], d_k[None], d_v[None], d_conv)
 

time: 56 us -> 55 us (0.982)
  waiting for transfers between devices: 16.5 us -> 12.7 us
  local copies, waits for them, and re-layouts: 0.16 us -> 3.81 us
  starting transfers between devices: 20.1 us -> 19.5 us
    ppermute x15 -> x13, waiting for transfers between devices: 14.5 us -> 8.58 us  [swapped(): return lax.ppermute(value, axis, [(i, i ^ bit) for i in range(size)])]
    unnamed x14, local copies, waits for them, and re-layouts: 0.03 us -> 3.77 us
    ppermute x4, waiting for transfers between devices: 2.01 us -> 4.07 us  [exchanged(): return (lax.ppermute(near, axis, pairs), lax.ppermute(far, axis, others))]
    ppermute x15 -> x13, starting transfers between devices: 15.5 us -> 14.1 us  [swapped(): return lax.ppermute(value, axis, [(i, i ^ bit) for i in range(size)])]
    ppermute x4, starting transfers between devices: 4.67 us -> 5.39 us  [exchanged(): return (lax.ppermute(near, axis, pairs), lax.ppermute(far, axis, others))]
  transfers between devices with their start and end apart: 19 -> 17, of which waited for: 9 -> 7; matrix products, arithmetic and copies ran while one was open for 1% -> 1% of each run, Pallas kernels for 11% -> 17%
where the time goes in v3:
time: 55 us; the launch traced here: 54.7 us
  starting transfers between devices  19.5 us (35%)
  Pallas kernels  16.6 us (30%)
  waiting for transfers between devices  12.7 us (23%)
  local copies, waits for them, and re-layouts  3.81 us (7%)
  between operations  1.65 us (3%)
    pallas_call x8, Pallas kernels, call(): pl.pallas_call(kernel, out_shape=outs, in_specs=[specs[place] for place i...  16.6 us
    ppermute x13, starting transfers between devices, swapped(): return lax.ppermute(value, axis, [(i, i ^ bit) for i in range(size)])  14.1 us
    ppermute x13, waiting for transfers between devices, swapped(): return lax.ppermute(value, axis, [(i, i ^ bit) for i in range(size)])  8.58 us
    ppermute x4, starting transfers between devices, exchanged(): return (lax.ppermute(near, axis, pairs), lax.ppermute(far, axis, others))  5.39 us
    ppermute x4, waiting for transfers between devices, exchanged(): return (lax.ppermute(near, axis, pairs), lax.ppermute(far, axis, others))  4.07 us
    unnamed x14, local copies, waits for them, and re-layouts  3.77 us
  transfers between devices with their start and end apart: 17, of which 7 were waited for; matrix products, arithmetic and copies ran while one was open for 1% of the time, Pallas kernels for 17%

profile of v3, /device:TPU:0, one launch (start us, length us, event | category | flops | bytes accessed | tf_op | source)
XLA Modules:
  0.0 54.7 jit_solution(15100062129731957643)
XLA Ops:
  0.6 3.0 %collective-permute-start.2 = (bf16[128,1024]{1,0:T(8,128)(2,1)}, bf16[128,1024]{1,0:T(8,128)(2,1)S(1)}, u32[]{:S(2)}, u32[]{:S(2)}) collective-permute-start(bf16[128,1024]{1,0:T(8,128)(2,1)} %refs_0_), channel_id=1, source_target_pairs={{0,16},{8,24},{16,0},{24,8},{1,17},{9,25},{17,1},{25,9},{2,18},{10... | collective-permute-start | bytes 786440 | tf_op jit(solution)/shard_map/ppermute | solution.py:32
  3.6 2.1 %shard_map.128 = (bf16[144,1024]{1,0:T(8,128)(2,1)}, bf16[144,1024]{1,0:T(8,128)(2,1)}, f32[256,128]{1,0:T(8,128)}) custom-call(s32[1,256]{1,0:T(1,128)} %targets.1, s32[1,256]{1,0:T(1,128)} %mask.1, bf16[256,512]{1,0:T(8,128)(2,1)} %bitcast.10, bf16[256,512]{1,0:T(8,128)(2,1)} %bitcast.12, bf16[256,512]{1,0:T(8,128)(2,1)} %bitcast.14), custom_call_target="tpu_custom_call" | custom-call | flops 1 | bytes 1 | tf_op jit(solution)/shard_map/pallas_call | solution.py:437
  5.9 2.0 %collective-permute-start = (bf16[144,1024]{1,0:T(8,128)(2,1)}, bf16[144,1024]{1,0:T(8,128)(2,1)S(1)}, u32[]{:S(2)}, u32[]{:S(2)}) collective-permute-start(bf16[144,1024]{1,0:T(8,128)(2,1)} %get-tuple-element.60), channel_id=1, source_target_pairs={{0,1},{1,0},{2,3},{3,2},{4,5},{5,4},{6,7},{7,6},{8,9},{9,8},{10,11... | collective-permute-start | bytes 884744 | tf_op jit(solution)/shard_map/ppermute | solution.py:45
  8.6 2.4 %collective-permute-done.2.refs_1_ = bf16[128,1024]{1,0:T(8,128)(2,1)S(1)} collective-permute-done((bf16[128,1024]{1,0:T(8,128)(2,1)}, bf16[128,1024]{1,0:T(8,128)(2,1)S(1)}, u32[]{:S(2)}, u32[]{:S(2)}) %collective-permute-start.2) | collective-permute-done | bytes 262176 | tf_op jit(solution)/shard_map/ppermute | solution.py:32
  11.0 0.9 %copy-done = bf16[1,256,512]{2,1,0:T(8,128)(2,1)S(1)} copy-done((bf16[1,256,512]{2,1,0:T(8,128)(2,1)S(1)}, bf16[1,256,512]{2,1,0:T(8,128)(2,1)}, u32[]{:S(2)}) %copy-start) | copy-done | bytes 262168
  12.0 0.9 %copy-done.1 = bf16[1,256,512]{2,1,0:T(8,128)(2,1)S(1)} copy-done((bf16[1,256,512]{2,1,0:T(8,128)(2,1)S(1)}, bf16[1,256,512]{2,1,0:T(8,128)(2,1)}, u32[]{:S(2)}) %copy-start.1) | copy-done | bytes 262168
  12.9 0.9 %copy-done.2 = bf16[1,256,512]{2,1,0:T(8,128)(2,1)S(1)} copy-done((bf16[1,256,512]{2,1,0:T(8,128)(2,1)S(1)}, bf16[1,256,512]{2,1,0:T(8,128)(2,1)}, u32[]{:S(2)}) %copy-start.2) | copy-done | bytes 262168
  13.9 0.9 %copy-done.4 = f32[256,128]{1,0:T(8,128)S(1)} copy-done((f32[256,128]{1,0:T(8,128)S(1)}, f32[256,128]{1,0:T(8,128)}, u32[]{:S(2)}) %copy-start.4) | copy-done | bytes 131096
  16.1 4.1 %collective-permute-done.near = bf16[144,1024]{1,0:T(8,128)(2,1)S(1)} collective-permute-done((bf16[144,1024]{1,0:T(8,128)(2,1)}, bf16[144,1024]{1,0:T(8,128)(2,1)S(1)}, u32[]{:S(2)}, u32[]{:S(2)}) %collective-permute-start) | collective-permute-done | bytes 294944 | tf_op jit(solution)/shard_map/ppermute | solution.py:45
  20.2 2.1 %shard_map.130 = (bf16[288,512]{1,0:T(8,128)(2,1)S(1)}, f32[256,128]{1,0:T(8,128)S(1)}, bf16[544,512]{1,0:T(8,128)(2,1)S(1)}, bf16[544,512]{1,0:T(8,128)(2,1)S(1...) custom-call(s32[4]{0:T(128)S(1)} %pad_add_fusion.info, bf16[256,512]{1,0:T(8,128)(2,1)S(1)} %get-tuple-element.54.q, ...), custom_call_target="tpu_custom_call" | custom-call | flops 201326592 | bytes 3481616 | tf_op jit(solution)/shard_map/pallas_call | solution.py:437
  22.5 1.2 %shard_map.131 = (f32[8,288,128]{2,1,0:T(8,128)S(1)}, bf16[512,1024]{1,0:T(8,128)(2,1)S(1)}) custom-call(s32[4]{0:T(128)S(1)} %pad_add_fusion.info, bf16[288,512]{1,0:T(8,128)(2,1)S(1)} %get-tuple-element.69.attn, bf16[128,1024]{1,0:T(8,128)(2,1)S(1)} %copy-done.3, bf16[128,1024]{1,0:T(8,128)(2,1)S(1)} %collective-permute-done.2.refs_1_, ...), custom_call_target="tpu_custom_call" | custom-call | flops 268435456 | bytes 3571728 | tf_op jit(solution)/shard_map/pallas_call | solution.py:437
  23.7 0.9 %collective-permute-done.7.refs_3_ = bf16[256,1024]{1,0:T(8,128)(2,1)S(1)} collective-permute-done((bf16[256,1024]{1,0:T(8,128)(2,1)}, bf16[256,1024]{1,0:T(8,128)(2,1)S(1)}, u32[]{:S(2)}, u32[]{:S(2)}) %collective-permute-start.7) | collective-permute-done | bytes 524320 | tf_op jit(solution)/shard_map/ppermute | solution.py:32
  24.6 5.9 %shard_map.132 = (bf16[256,512]{1,0:T(8,128)(2,1)S(1)}, f32[256,128]{1,0:T(8,128)S(1)}, f32[16,1024]{1,0:T(8,128)S(1)}) custom-call(s32[4]{0:T(128)S(1)} %pad_add_fusion.info, bf16[288,512]{1,0:T(8,128)(2,1)S(1)} %get-tuple-element.69.attn, f32[256,128]{1,0:T(8,128)S(1)} %get-tuple-element.70.lse, f32[272,128]{1,0:T(8,128)S(1)} %get-tuple-element.71.meta_ext, ...), custom_call_target="tpu_custom_call" | custom-call | flops 1610612736 | bytes 5386256 | tf_op jit(solution)/shard_map/pallas_call | solution.py:437
  30.5 2.4 %collective-permute-start.8 = (bf16[12,1024]{1,0:T(8,128)(2,1)S(1)}, bf16[12,1024]{1,0:T(8,128)(2,1)S(1)}, u32[]{:S(2)}, u32[]{:S(2)}) collective-permute-start(bf16[12,1024]{1,0:T(8,128)(2,1)S(1)} %get-tuple-element.108), channel_id=1, source_target_pairs={{0,1},{1,0},{2,3},{3,2},{4,5},{5,4},{6,7},{7,6},{8,9},{9,8},{10,11... | collective-permute-start | bytes 73736 | tf_op jit(solution)/shard_map/ppermute | solution.py:32
  33.0 1.2 %shard_map.133 = (bf16[128,1024]{1,0:T(8,128)(2,1)S(1)}, bf16[128,1024]{1,0:T(8,128)(2,1)S(1)}) custom-call(s32[4]{0:T(128)S(1)} %pad_add_fusion.info, bf16[288,512]{1,0:T(8,128)(2,1)S(1)} %get-tuple-element.64.q_ext, bf16[544,512]{1,0:T(8,128)(2,1)S(1)} %get-tuple-element.65.k_ext, bf16[544,512]{1,0:T(8,128)(2,1)S(1)} %get-tuple-element.66.v_ext, ...), custom_call_target="tpu_custom_call" | custom-call | flops 134217728 | bytes 2326544 | tf_op jit(solution)/shard_map/pallas_call | solution.py:437
  35.4 1.2 %collective-permute-start.10 = (bf16[12,1024]{1,0:T(8,128)(2,1)S(1)}, bf16[12,1024]{1,0:T(8,128)(2,1)S(1)}, u32[]{:S(2)}, u32[]{:S(2)}) collective-permute-start(bf16[12,1024]{1,0:T(8,128)(2,1)S(1)} %get-tuple-element.104), channel_id=1, source_target_pairs={{0,16},{8,24},{16,0},{24,8},{1,17},{9,25},{17,1},{25,9},{2,18},{10... | collective-permute-start | bytes 73736 | tf_op jit(solution)/shard_map/ppermute | solution.py:32
  37.0 2.1 %collective-permute-start.15 = (bf16[128,1024]{1,0:T(8,128)(2,1)S(1)}, bf16[128,1024]{1,0:T(8,128)(2,1)S(1)}, u32[]{:S(2)}, u32[]{:S(2)}) collective-permute-start(bf16[128,1024]{1,0:T(8,128)(2,1)S(1)} %get-tuple-element.91), channel_id=1, source_target_pairs={{0,1},{1,0},{2,3},{3,2},{4,5},{5,4},{6,7},{7,6},{8,9},{9,8},{10,11... | collective-permute-start | bytes 786440 | tf_op jit(solution)/shard_map/ppermute | solution.py:45
  40.1 2.9 %collective-permute-start.12 = (bf16[12,1024]{1,0:T(8,128)(2,1)S(1)}, bf16[12,1024]{1,0:T(8,128)(2,1)S(1)}, u32[]{:S(2)}, u32[]{:S(2)}) collective-permute-start(bf16[12,1024]{1,0:T(8,128)(2,1)S(1)} %pad_maximum_fusion.2.refs_0_), channel_id=1, source_target_pairs={{0,2},{1,3},{2,0},{3,1},{4,6},{5,7},{6,4},{7,5},{8,10},{9,11},{10,... | collective-permute-start | bytes 73736 | tf_op jit(solution)/shard_map/ppermute | solution.py:32
  42.9 3.0 %collective-permute-start.13 = (bf16[12,1024]{1,0:T(8,128)(2,1)S(1)}, bf16[12,1024]{1,0:T(8,128)(2,1)S(1)}, u32[]{:S(2)}, u32[]{:S(2)}) collective-permute-start(bf16[12,1024]{1,0:T(8,128)(2,1)S(1)} %pad_maximum_fusion.2.refs_0_), channel_id=1, source_target_pairs={{0,4},{1,5},{2,6},{3,7},{4,0},{5,1},{6,2},{7,3},{8,12},{9,13},{10,... | collective-permute-start | bytes 73736 | tf_op jit(solution)/shard_map/ppermute | solution.py:32
  45.9 2.6 %shard_map.134 = (bf16[256,512]{1,0:T(8,128)(2,1)}, f32[256,512]{1,0:T(8,128)S(1)}, f32[256,512]{1,0:T(8,128)S(1)}) custom-call(s32[4]{0:T(128)S(1)} %pad_add_fusion.info, bf16[288,512]{1,0:T(8,128)(2,1)S(1)} %get-tuple-element.64.q_ext, bf16[544,512]{1,0:T(8,128)(2,1)S(1)} %get-tuple-element.65.k_ext, bf16[544,512]{1,0:T(8,128)(2,1)S(1)} %get-tuple-element.66.v_ext, ...), custom_call_target="tpu_custom_call" | custom-call | flops 1 | bytes 1 | tf_op jit(solution)/shard_map/pallas_call | solution.py:437
  48.6 1.5 %collective-permute-done.12.refs_1_ = bf16[12,1024]{1,0:T(8,128)(2,1)S(1)} collective-permute-done((bf16[12,1024]{1,0:T(8,128)(2,1)S(1)}, bf16[12,1024]{1,0:T(8,128)(2,1)S(1)}, u32[]{:S(2)}, u32[]{:S(2)}) %collective-permute-start.12) | collective-permute-done | bytes 24608 | tf_op jit(solution)/shard_map/ppermute | solution.py:32
  50.0 1.4 %collective-permute-done.13.refs_2_ = bf16[12,1024]{1,0:T(8,128)(2,1)S(1)} collective-permute-done((bf16[12,1024]{1,0:T(8,128)(2,1)S(1)}, bf16[12,1024]{1,0:T(8,128)(2,1)S(1)}, u32[]{:S(2)}, u32[]{:S(2)}) %collective-permute-start.13) | collective-permute-done | bytes 24608 | tf_op jit(solution)/shard_map/ppermute | solution.py:32
  51.5 1.7 %collective-permute-done.14.refs_3_ = bf16[12,1024]{1,0:T(8,128)(2,1)S(1)} collective-permute-done((bf16[12,1024]{1,0:T(8,128)(2,1)S(1)}, bf16[12,1024]{1,0:T(8,128)(2,1)S(1)}, u32[]{:S(2)}, u32[]{:S(2)}) %collective-permute-start.14) | collective-permute-done | bytes 24608 | tf_op jit(solution)/shard_map/ppermute | solution.py:32
  53.2 1.4 %shard_map.135 = (bf16[256,512]{1,0:T(8,128)(2,1)}, bf16[256,512]{1,0:T(8,128)(2,1)}, f32[9,1024]{1,0:T(8,128)}, f32[1,1]{1,0:T(1,128)}) custom-call(s32[4]{0:T(128)S(1)} %pad_add_fusion.info, f32[256,512]{1,0:T(8,128)S(1)} %get-tuple-element.89.k_part, f32[256,512]{1,0:T(8,128)S(1)} %get-tuple-element.90.v_part, ...), custom_call_target="tpu_custom_call" | custom-call | flops 131072 | bytes 2232340 | tf_op jit(solution)/shard_map/pallas_call | solution.py:437
  (62 shorter events, 4.1 us)
Async XLA Ops:
  0.6 15.0 %copy-start.5 = (bf16[256,1024]{1,0:T(8,128)(2,1)S(1)}, bf16[256,1024]{1,0:T(8,128)(2,1)}, u32[]{:S(2)}) copy-start(bf16[256,1024]{1,0:T(8,128)(2,1)} %refs_0_.1) | copy-start | bytes 1572868
  0.6 10.4 %collective-permute-start.2 = (bf16[128,1024]{1,0:T(8,128)(2,1)}, bf16[128,1024]{1,0:T(8,128)(2,1)S(1)}, u32[]{:S(2)}, u32[]{:S(2)}) collective-permute-start(bf16[128,1024]{1,0:T(8,128)(2,1)} %refs_0_), channel_id=1, source_target_pairs={{0,16},{8,24},{16,0},{24,8},{1,17},{9,25},{17,1},{25,9},{2,18},{10... | collective-permute-start | bytes 786440 | tf_op jit(solution)/shard_map/ppermute | solution.py:32
  5.7 16.6 %collective-permute-start.5 = (bf16[256,1024]{1,0:T(8,128)(2,1)}, bf16[256,1024]{1,0:T(8,128)(2,1)}, u32[]{:S(2)}, u32[]{:S(2)}) collective-permute-start(bf16[256,1024]{1,0:T(8,128)(2,1)} %refs_0_.1), channel_id=1, source_target_pairs={{0,16},{8,24},{16,0},{24,8},{1,17},{9,25},{17,1},{25,9},{2,18},{10... | collective-permute-start | bytes 1572872 | tf_op jit(solution)/shard_map/ppermute | solution.py:32
  5.9 14.3 %collective-permute-start = (bf16[144,1024]{1,0:T(8,128)(2,1)}, bf16[144,1024]{1,0:T(8,128)(2,1)S(1)}, u32[]{:S(2)}, u32[]{:S(2)}) collective-permute-start(bf16[144,1024]{1,0:T(8,128)(2,1)} %get-tuple-element.60), channel_id=1, source_target_pairs={{0,1},{1,0},{2,3},{3,2},{4,5},{5,4},{6,7},{7,6},{8,9},{9,8},{10,11... | collective-permute-start | bytes 884744 | tf_op jit(solution)/shard_map/ppermute | solution.py:45
  7.9 12.3 %collective-permute-start.1 = (bf16[144,1024]{1,0:T(8,128)(2,1)}, bf16[144,1024]{1,0:T(8,128)(2,1)S(1)}, u32[]{:S(2)}, u32[]{:S(2)}) collective-permute-start(bf16[144,1024]{1,0:T(8,128)(2,1)} %get-tuple-element.61), channel_id=1, source_target_pairs={{1,2},{2,1},{3,4},{4,3},{5,6},{6,5},{9,10},{10,9},{11,12},{12,11},... | collective-permute-start | bytes 884744 | tf_op jit(solution)/shard_map/ppermute | solution.py:45
  8.5 7.0 %collective-permute-start.3 = (bf16[128,1024]{1,0:T(8,128)(2,1)}, bf16[128,1024]{1,0:T(8,128)(2,1)S(1)}, u32[]{:S(2)}, u32[]{:S(2)}) collective-permute-start(bf16[128,1024]{1,0:T(8,128)(2,1)} %refs_0_), channel_id=1, source_target_pairs={{0,8},{8,0},{16,24},{24,16},{1,9},{9,1},{17,25},{25,17},{2,10},{10... | collective-permute-start | bytes 786440 | tf_op jit(solution)/shard_map/ppermute | solution.py:32
  11.0 9.2 %collective-permute-start.4 = (bf16[128,1024]{1,0:T(8,128)(2,1)S(1)}, bf16[128,1024]{1,0:T(8,128)(2,1)S(1)}, u32[]{:S(2)}, u32[]{:S(2)}) collective-permute-start(bf16[128,1024]{1,0:T(8,128)(2,1)S(1)} %collective-permute-done.2.refs_1_), channel_id=1, source_target_pairs={{0,8},{8,0},{16,24},{24,16},{1,9},{9,1},{17,25},{25,17},{2,10},{10... | collective-permute-start | bytes 786440 | tf_op jit(solution)/shard_map/ppermute | solution.py:32
  11.0 1.0 %copy-start = (bf16[1,256,512]{2,1,0:T(8,128)(2,1)S(1)}, bf16[1,256,512]{2,1,0:T(8,128)(2,1)}, u32[]{:S(2)}) copy-start(bf16[1,256,512]{2,1,0:T(8,128)(2,1)} %param.9) | copy-start | bytes 786436
  11.9 0.9 %copy-start.1 = (bf16[1,256,512]{2,1,0:T(8,128)(2,1)S(1)}, bf16[1,256,512]{2,1,0:T(8,128)(2,1)}, u32[]{:S(2)}) copy-start(bf16[1,256,512]{2,1,0:T(8,128)(2,1)} %param.10) | copy-start | bytes 786436
  12.9 0.9 %copy-start.2 = (bf16[1,256,512]{2,1,0:T(8,128)(2,1)S(1)}, bf16[1,256,512]{2,1,0:T(8,128)(2,1)}, u32[]{:S(2)}) copy-start(bf16[1,256,512]{2,1,0:T(8,128)(2,1)} %param.11) | copy-start | bytes 786436
  13.8 0.9 %copy-start.4 = (f32[256,128]{1,0:T(8,128)S(1)}, f32[256,128]{1,0:T(8,128)}, u32[]{:S(2)}) copy-start(f32[256,128]{1,0:T(8,128)} %get-tuple-element.53.meta) | copy-start | bytes 393220
  14.8 7.7 %copy-start.3 = (bf16[128,1024]{1,0:T(8,128)(2,1)S(1)}, bf16[128,1024]{1,0:T(8,128)(2,1)}, u32[]{:S(2)}) copy-start(bf16[128,1024]{1,0:T(8,128)(2,1)} %refs_0_) | copy-start | bytes 786436
  15.6 8.1 %collective-permute-start.6 = (bf16[256,1024]{1,0:T(8,128)(2,1)S(1)}, bf16[256,1024]{1,0:T(8,128)(2,1)S(1)}, u32[]{:S(2)}, u32[]{:S(2)}) collective-permute-start(bf16[256,1024]{1,0:T(8,128)(2,1)S(1)} %copy-done.5), channel_id=1, source_target_pairs={{0,8},{8,0},{16,24},{24,16},{1,9},{9,1},{17,25},{25,17},{2,10},{10... | collective-permute-start | bytes 1572872 | tf_op jit(solution)/shard_map/ppermute | solution.py:32
  20.2 4.4 %copy-start.6 = (f32[9,1024]{1,0:T(8,128)S(1)}, f32[9,1024]{1,0:T(8,128)}, u32[]{:S(2)}) copy-start(f32[9,1024]{1,0:T(8,128)} %taps.1) | copy-start | bytes 110596
  22.4 2.2 %collective-permute-start.7 = (bf16[256,1024]{1,0:T(8,128)(2,1)}, bf16[256,1024]{1,0:T(8,128)(2,1)S(1)}, u32[]{:S(2)}, u32[]{:S(2)}) collective-permute-start(bf16[256,1024]{1,0:T(8,128)(2,1)} %collective-permute-done.5.refs_1_), channel_id=1, source_target_pairs={{0,8},{8,0},{16,24},{24,16},{1,9},{9,1},{17,25},{25,17},{2,10},{10... | collective-permute-start | bytes 1572872 | tf_op jit(solution)/shard_map/ppermute | solution.py:32
  30.5 4.3 %collective-permute-start.8 = (bf16[12,1024]{1,0:T(8,128)(2,1)S(1)}, bf16[12,1024]{1,0:T(8,128)(2,1)S(1)}, u32[]{:S(2)}, u32[]{:S(2)}) collective-permute-start(bf16[12,1024]{1,0:T(8,128)(2,1)S(1)} %get-tuple-element.108), channel_id=1, source_target_pairs={{0,1},{1,0},{2,3},{3,2},{4,5},{5,4},{6,7},{7,6},{8,9},{9,8},{10,11... | collective-permute-start | bytes 73736 | tf_op jit(solution)/shard_map/ppermute | solution.py:32
  35.0 4.7 %collective-permute-start.11 = (bf16[12,1024]{1,0:T(8,128)(2,1)S(1)}, bf16[12,1024]{1,0:T(8,128)(2,1)S(1)}, u32[]{:S(2)}, u32[]{:S(2)}) collective-permute-start(bf16[12,1024]{1,0:T(8,128)(2,1)S(1)} %get-tuple-element.104), channel_id=1, source_target_pairs={{0,24},{8,16},{16,8},{24,0},{1,25},{9,17},{17,9},{25,1},{2,26},{10... | collective-permute-start | bytes 73736 | tf_op jit(solution)/shard_map/ppermute | solution.py:32
  35.4 4.3 %collective-permute-start.10 = (bf16[12,1024]{1,0:T(8,128)(2,1)S(1)}, bf16[12,1024]{1,0:T(8,128)(2,1)S(1)}, u32[]{:S(2)}, u32[]{:S(2)}) collective-permute-start(bf16[12,1024]{1,0:T(8,128)(2,1)S(1)} %get-tuple-element.104), channel_id=1, source_target_pairs={{0,16},{8,24},{16,0},{24,8},{1,17},{9,25},{17,1},{25,9},{2,18},{10... | collective-permute-start | bytes 73736 | tf_op jit(solution)/shard_map/ppermute | solution.py:32
  36.7 3.2 %collective-permute-start.9 = (bf16[12,1024]{1,0:T(8,128)(2,1)S(1)}, bf16[12,1024]{1,0:T(8,128)(2,1)S(1)}, u32[]{:S(2)}, u32[]{:S(2)}) collective-permute-start(bf16[12,1024]{1,0:T(8,128)(2,1)S(1)} %get-tuple-element.104), channel_id=1, source_target_pairs={{0,8},{8,0},{16,24},{24,16},{1,9},{9,1},{17,25},{25,17},{2,10},{10... | collective-permute-start | bytes 73736 | tf_op jit(solution)/shard_map/ppermute | solution.py:32
  37.0 16.2 %collective-permute-start.15 = (bf16[128,1024]{1,0:T(8,128)(2,1)S(1)}, bf16[128,1024]{1,0:T(8,128)(2,1)S(1)}, u32[]{:S(2)}, u32[]{:S(2)}) collective-permute-start(bf16[128,1024]{1,0:T(8,128)(2,1)S(1)} %get-tuple-element.91), channel_id=1, source_target_pairs={{0,1},{1,0},{2,3},{3,2},{4,5},{5,4},{6,7},{7,6},{8,9},{9,8},{10,11... | collective-permute-start | bytes 786440 | tf_op jit(solution)/shard_map/ppermute | solution.py:45
  39.1 14.2 %collective-permute-start.16 = (bf16[128,1024]{1,0:T(8,128)(2,1)S(1)}, bf16[128,1024]{1,0:T(8,128)(2,1)S(1)}, u32[]{:S(2)}, u32[]{:S(2)}) collective-permute-start(bf16[128,1024]{1,0:T(8,128)(2,1)S(1)} %get-tuple-element.92), channel_id=1, source_target_pairs={{1,2},{2,1},{3,4},{4,3},{5,6},{6,5},{9,10},{10,9},{11,12},{12,11},... | collective-permute-start | bytes 786440 | tf_op jit(solution)/shard_map/ppermute | solution.py:45
  40.1 10.0 %collective-permute-start.12 = (bf16[12,1024]{1,0:T(8,128)(2,1)S(1)}, bf16[12,1024]{1,0:T(8,128)(2,1)S(1)}, u32[]{:S(2)}, u32[]{:S(2)}) collective-permute-start(bf16[12,1024]{1,0:T(8,128)(2,1)S(1)} %pad_maximum_fusion.2.refs_0_), channel_id=1, source_target_pairs={{0,2},{1,3},{2,0},{3,1},{4,6},{5,7},{6,4},{7,5},{8,10},{9,11},{10,... | collective-permute-start | bytes 73736 | tf_op jit(solution)/shard_map/ppermute | solution.py:32
  42.9 8.5 %collective-permute-start.13 = (bf16[12,1024]{1,0:T(8,128)(2,1)S(1)}, bf16[12,1024]{1,0:T(8,128)(2,1)S(1)}, u32[]{:S(2)}, u32[]{:S(2)}) collective-permute-start(bf16[12,1024]{1,0:T(8,128)(2,1)S(1)} %pad_maximum_fusion.2.refs_0_), channel_id=1, source_target_pairs={{0,4},{1,5},{2,6},{3,7},{4,0},{5,1},{6,2},{7,3},{8,12},{9,13},{10,... | collective-permute-start | bytes 73736 | tf_op jit(solution)/shard_map/ppermute | solution.py:32
  45.9 7.3 %collective-permute-start.14 = (bf16[12,1024]{1,0:T(8,128)(2,1)S(1)}, bf16[12,1024]{1,0:T(8,128)(2,1)S(1)}, u32[]{:S(2)}, u32[]{:S(2)}) collective-permute-start(bf16[12,1024]{1,0:T(8,128)(2,1)S(1)} %pad_maximum_fusion.2.refs_0_), channel_id=1, source_target_pairs={{0,6},{1,7},{2,4},{3,5},{4,2},{5,3},{6,0},{7,1},{8,14},{9,15},{10,... | collective-permute-start | bytes 73736 | tf_op jit(solution)/shard_map/ppermute | solution.py:32

commit v4 on v3

--- a/solution.py
+++ b/solution.py
@@ -119,15 +119,14 @@
         patch(far, 0, low, 1)
 
 
-def stage_kernel(q, k, v, meta, q_own, k_own, v_own, meta_own):
-    meta_own[...] = meta[...]
+def stage_kernel(q, k, v, q_own, k_own, v_own):
     q_own[...] = q[...]
     k_own[...] = k[...]
     v_own[...] = v[...]
 
 
 def attention_kernel(
-    info, q, k, v, meta, near, far, attn, lse, k_ext, v_ext, q_ext, meta_ext
+    info, q, k, v, near, far, attn, lse, k_ext, v_ext, q_ext, meta_edges
 ):
     tokens, width = q.shape
     length, offset = info[0], info[1]
@@ -144,8 +143,8 @@
         q_ext[0:16, :] = left[0:16, 0:width]
         q_ext[16 + tokens :, :] = right[HALO - 16 : HALO, 0:width]
         spots = slice(width, width + 128)
-        meta_ext[0:EDGE, :] = left[0:16, spots].astype(F32)[0:EDGE]
-        meta_ext[EDGE + tokens :, :] = right[HALO - 16 : HALO, spots].astype(F32)[EDGE:]
+        meta_edges[0:EDGE, :] = left[0:16, spots].astype(F32)[0:EDGE]
+        meta_edges[EDGE:, :] = right[HALO - 16 : HALO, spots].astype(F32)[EDGE:]
 
     @pl.when(even)
     def _():
@@ -155,7 +154,6 @@
     def _():
         place_sides(near, far)
 
-    meta_ext[EDGE : EDGE + tokens, :] = meta[...]
     lse[...] = jnp.zeros(lse.shape, F32)
     rows, span = 16 + WINDOW, 4 * WINDOW
     spot = lax.broadcasted_iota(jnp.int32, (rows, span), 0)
@@ -198,12 +196,14 @@
         scores = later
 
 
-def fetch_pieces(marks, mine, pieces, full, sems):
+def fetch_pieces(marks, mine, pieces, full, sems, first=0):
     copies = []
+    held = full.shape[0] // pieces[0].shape[0]
     for mark, piece in zip(marks, pieces):
         rows = piece.shape[0]
-        target = full.at[pl.ds(pl.multiple_of((mine ^ mark) * rows, rows), rows)]
-        copies.append(pltpu.make_async_copy(piece, target, sems.at[len(copies)]))
+        start = ((mine ^ mark) & (held - 1)) * rows
+        target = full.at[pl.ds(pl.multiple_of(start, rows), rows)]
+        copies.append(pltpu.make_async_copy(piece, target, sems.at[first + len(copies)]))
         copies[-1].start()
     return copies
 
@@ -213,10 +213,11 @@
     return (row_pos >= 0) & (row_pos < info[0])
 
 
-def hidden_kernel(marks, info, attn, *refs):
-    pieces, (hid, out_full, sems) = refs[: len(marks)], refs[len(marks) :]
+def hidden_kernel(marks, info, attn, taps, *refs):
+    pieces, (hid, out_full, gated, slope, sems) = refs[: len(marks)], refs[len(marks) :]
     copies = fetch_pieces(marks, info[2], pieces, out_full, sems)
     chunks, ext, lanes = hid.shape
+    depth = chunks * lanes
     ext = ext - 2 * EDGE
     live = live_rows(info, ext, lanes)
     hid[:, 0:EDGE, :] = jnp.zeros((chunks, EDGE, lanes), F32)
@@ -230,17 +231,6 @@
         for part in range(2):
             piece = block[:, part * lanes : (part + 1) * lanes]
             hid[at // lanes + part, EDGE : EDGE + ext, :] = jnp.where(live, piece, 0.0)
-
-
-def middle_kernel(marks, info, attn, lse, meta_ext, taps, hid, out_full, *refs):
-    pieces, (d_attn, stats, summary) = refs[: len(marks)], refs[len(marks) : len(marks) + 3]
-    head_full, gated, slope, logits, d_logits, d_pre, d_hid, sems = refs[len(marks) + 3 :]
-    copies = fetch_pieces(marks, info[2], pieces, head_full, sems)
-    tokens, width = d_attn.shape
-    depth, vocab = head_full.shape
-    ext = tokens + 2 * EDGE
-    lanes = 128
-    live = live_rows(info, ext, lanes)
     for chunk in range(depth // lanes):
         cols = slice(chunk * lanes, (chunk + 1) * lanes)
         conv = jnp.zeros((ext, lanes), F32)
@@ -250,12 +240,36 @@
         sigma = jax.nn.sigmoid(conv)
         gated[:, cols] = (conv * sigma).astype(BF16)
         slope[chunk] = sigma * (1.0 + conv * (1.0 - sigma))
+
+
+def middle_kernel(
+    marks, info, attn, lse, meta, meta_edges, taps, hid, out_full, gated, slope, *refs
+):
+    pieces, (d_attn, stats, summary) = refs[: len(marks)], refs[len(marks) : len(marks) + 3]
+    head_own, head_far, logits, d_logits, d_pre, d_hid, sems = refs[len(marks) + 3 :]
+    count = len(marks) // 2
+    others = fetch_pieces(marks[:count], info[2], pieces[:count], head_own, sems)
+    copies = fetch_pieces(marks[count:], info[2], pieces[count:], head_far, sems, count)
+    tokens, width = d_attn.shape
+    half, vocab = head_far.shape
+    depth = 2 * half
+    on_top = (info[2] & count) != 0
+    own_start = pl.multiple_of(jnp.where(on_top, half, 0), half)
+    far_start = pl.multiple_of(jnp.where(on_top, 0, half), half)
+    ext = tokens + 2 * EDGE
+    lanes = 128
+    live = live_rows(info, ext, lanes)
+    for copy in others:
+        copy.wait()
+    for at in range(0, vocab, 256):
+        cols = slice(at, at + 256)
+        logits[:, cols] = nn(gated[:, pl.ds(own_start, half)], head_own[:, cols])
     for copy in copies:
         copy.wait()
     for at in range(0, vocab, 256):
-        logits[:, at : at + 256] = nn(gated[...], head_full[:, at : at + 256])
-
-    meta_all = meta_ext[...]
+        cols = slice(at, at + 256)
+        logits[:, cols] += nn(gated[:, pl.ds(far_start, half)], head_far[:, cols])
+    meta_all = jnp.concatenate([meta_edges[0:EDGE], meta[...], meta_edges[EDGE:]], axis=0)
     target = (meta_all[:, 0:1] * 32.0 + meta_all[:, 1:2]).astype(jnp.int32)
     chosen = jnp.where(live & (meta_all[:, 2:3] == 1.0), 1.0, 0.0)[:, 0:1]
     loss_rows = jnp.zeros((16, 1), F32)
@@ -283,19 +297,29 @@
     summary[TAPS : TAPS + 1, 0:lanes] = jnp.where(
         lane == 0, loss_sum, jnp.where(lane == 1, count_sum, 0.0)
     )
-    for at in range(0, depth, 256):
-        d_gated = nt(d_logits[...], head_full[at : at + 256, :])
+    turns = [
+        (held, start, at)
+        for held, start in ((head_own, own_start), (head_far, far_start))
+        for at in range(0, half, 256)
+    ]
+    d_gated = nt(d_logits[...], head_own[0:256, :])
+    for turn, (_, start, at) in enumerate(turns):
+        later = None
+        if turn + 1 < len(turns):
+            held, _, following = turns[turn + 1]
+            later = nt(d_logits[...], held[following : following + 256, :])
         for part in range(2):
-            chunk = at // lanes + part
-            cols = slice(chunk * lanes, (chunk + 1) * lanes)
+            chunk = start // lanes + at // lanes + part
+            cols = pl.ds(pl.multiple_of(start + at + part * lanes, lanes), lanes)
             change = d_gated[:, part * lanes : (part + 1) * lanes] * slope[chunk]
             d_pre[chunk] = change
             owned = change[EDGE : EDGE + tokens]
             for tap in range(TAPS):
-                start = 2 * EDGE - MARGIN + tap
+                row = 2 * EDGE - MARGIN + tap
                 summary[tap : tap + 1, cols] = jnp.sum(
-                    owned * hid[chunk, start : start + tokens, :], axis=0, keepdims=True
+                    owned * hid[chunk, row : row + tokens, :], axis=0, keepdims=True
                 )
+        d_gated = later
     for chunk in range(depth // lanes):
         cols = slice(chunk * lanes, (chunk + 1) * lanes)
         change = jnp.zeros((tokens, lanes), F32)
@@ -304,13 +328,18 @@
             change = change + taps[tap : tap + 1, cols] * d_pre[chunk, start : start + tokens, :]
         d_hid[:, cols] = jnp.where(live[EDGE : EDGE + tokens], change, 0.0).astype(BF16)
     stats[...] = lse[...]
-    for at in range(0, width, HEAD_DIM):
-        cols = slice(at, at + HEAD_DIM)
-        head = at // HEAD_DIM
-        block = nt(d_hid[...], out_full[cols, :]).astype(BF16)
-        d_attn[:, cols] = block
-        products = block.astype(F32) * attn[16 : 16 + tokens, cols].astype(F32)
-        stats[:, head : head + 1] = jnp.sum(products, axis=-1, keepdims=True)
+    blocks = [
+        nt(d_hid[...], out_full[at : at + 2 * HEAD_DIM, :]).astype(BF16)
+        for at in range(0, width, 2 * HEAD_DIM)
+    ]
+    for place, pair in enumerate(blocks):
+        for part in range(2):
+            head = 2 * place + part
+            cols = slice(head * HEAD_DIM, (head + 1) * HEAD_DIM)
+            block = pair[:, part * HEAD_DIM : (part + 1) * HEAD_DIM]
+            d_attn[:, cols] = block
+            products = block.astype(F32) * attn[16 : 16 + tokens, cols].astype(F32)
+            stats[:, head : head + 1] = jnp.sum(products, axis=-1, keepdims=True)
 
 
 def edge_grads_kernel(info, q_ext, k_ext, v_ext, stats, d_attn, near, far):
@@ -481,14 +510,7 @@
         0,
         56,
     )
-    q_own, k_own, v_own, meta = call(
-        stage_kernel,
-        (q, k, v, meta),
-        (block, block, block, shape((tokens, 128), F32)),
-        [],
-        "vvvv",
-        0,
-    )
+    q_own, k_own, v_own = call(stage_kernel, (q, k, v), (block, block, block), [], "vvv", 0)
     near, far, head_weight = lax.optimization_barrier((near, far, head_weight))
     near, far = exchanged(near, far, "ctx")
     top_bit = bits_of(dp_size)[-1]
@@ -498,52 +520,58 @@
     near, far, *out_held = lax.optimization_barrier((near, far, *out_held))
 
     ext = tokens + 2 * EDGE
-    attn, lse, k_ext, v_ext, q_ext, meta_ext = call(
+    attn, lse, k_ext, v_ext, q_ext, meta_edges = call(
         attention_kernel,
-        (info, q_own, k_own, v_own, meta, near, far),
+        (info, q_own, k_own, v_own, near, far),
         (
             shape((tokens + 32, width), BF16),
             shape((tokens, 128), F32),
             shape((tokens + 2 * HALO, width), BF16),
             shape((tokens + 2 * HALO, width), BF16),
             shape((tokens + 32, width), BF16),
-            shape((ext, 128), F32),
+            shape((2 * EDGE, 128), F32),
         ),
         [],
-        "svvvvvv",
+        "svvvvv",
         4 * tokens * 3 * WINDOW * width,
     )
     attn, far_head = lax.optimization_barrier((attn, far_head))
-    head_marks, head_held = spread([(0, head_weight), (top_bit, far_head)], "dp")
+    own_marks, own_held = spread([(0, head_weight)], "dp")
+    far_marks, far_held = spread([(top_bit, far_head)], "dp")
+    head_marks, head_held = own_marks + far_marks, own_held + far_held
 
     chunks = depth // 128
-    hid, out_full = call(
+    hid, out_full, gated, slope = call(
         functools.partial(hidden_kernel, out_marks),
-        (info, attn, *out_held),
-        (shape((chunks, ext + 2 * EDGE, 128), F32), shape((width, depth), BF16)),
+        (info, attn, conv_weight, *out_held),
+        (
+            shape((chunks, ext + 2 * EDGE, 128), F32),
+            shape((width, depth), BF16),
+            shape((ext, depth), BF16),
+            shape((chunks, ext, 128), F32),
+        ),
         [pltpu.SemaphoreType.DMA((len(out_held),))],
-        "sv" + "a" * len(out_held),
+        "svv" + "a" * len(out_held),
         2 * tokens * depth * width,
     )
     d_attn, stats, summary = call(
         functools.partial(middle_kernel, head_marks),
-        (info, attn, lse, meta_ext, conv_weight, hid, out_full, *head_held),
+        (info, attn, lse, meta, meta_edges, conv_weight, hid, out_full, gated, slope, *head_held),
         (
             shape((tokens, width), BF16),
             shape((tokens, 128), F32),
             shape((16, depth), F32),
         ),
         [
-            pltpu.VMEM((depth, vocab), BF16),
-            pltpu.VMEM((ext, depth), BF16),
-            pltpu.VMEM((chunks, ext, 128), F32),
+            pltpu.VMEM((depth // 2, vocab), BF16),
+            pltpu.VMEM((depth // 2, vocab), BF16),
             pltpu.VMEM((ext, vocab), F32),
             pltpu.VMEM((ext, vocab), BF16),
             pltpu.VMEM((chunks, ext, 128), F32),
             pltpu.VMEM((tokens, depth), BF16),
             pltpu.SemaphoreType.DMA((len(head_held),)),
         ],
-        "svvvvvv" + "a" * len(head_held),
+        "svvvvvvvvv" + "a" * len(head_held),
         4 * tokens * depth * (width + vocab),
     )
 

time: 55 us -> 54.2 us (0.985)
  local copies, waits for them, and re-layouts: 3.81 us -> 2.91 us
    ppermute x4, waiting for transfers between devices: 4.07 us -> 5 us  [exchanged(): return (lax.ppermute(near, axis, pairs), lax.ppermute(far, axis, others))]
    unnamed x14, local copies, waits for them, and re-layouts: 3.77 us -> 2.87 us
  transfers between devices with their start and end apart: 17 -> 17, of which waited for: 7 -> 7; matrix products, arithmetic and copies ran while one was open for 1% -> 1% of each run, Pallas kernels for 17% -> 19%
where the time goes in v4:
time: 54.2 us; the launch traced here: 53.9 us
  starting transfers between devices  19 us (35%)
  Pallas kernels  16.7 us (31%)
  waiting for transfers between devices  13.2 us (24%)
  local copies, waits for them, and re-layouts  2.91 us (5%)
  between operations  1.66 us (3%)
    pallas_call x8, Pallas kernels, call(): pl.pallas_call(kernel, out_shape=outs, in_specs=[specs[place] for place i...  16.7 us
    ppermute x13, starting transfers between devices, swapped(): return lax.ppermute(value, axis, [(i, i ^ bit) for i in range(size)])  13.7 us
    ppermute x13, waiting for transfers between devices, swapped(): return lax.ppermute(value, axis, [(i, i ^ bit) for i in range(size)])  8.16 us
    ppermute x4, starting transfers between devices, exchanged(): return (lax.ppermute(near, axis, pairs), lax.ppermute(far, axis, others))  5.28 us
    ppermute x4, waiting for transfers between devices, exchanged(): return (lax.ppermute(near, axis, pairs), lax.ppermute(far, axis, others))  5 us
    unnamed x14, local copies, waits for them, and re-layouts  2.87 us
  transfers between devices with their start and end apart: 17, of which 7 were waited for; matrix products, arithmetic and copies ran while one was open for 1% of the time, Pallas kernels for 19%

profile of v4, /device:TPU:0, one launch (start us, length us, event | category | flops | bytes accessed | tf_op | source)
XLA Modules:
  0.0 53.9 jit_solution(3882313005981435115)
XLA Ops:
  0.6 3.0 %collective-permute-start.2 = (bf16[128,1024]{1,0:T(8,128)(2,1)}, bf16[128,1024]{1,0:T(8,128)(2,1)S(1)}, u32[]{:S(2)}, u32[]{:S(2)}) collective-permute-start(bf16[128,1024]{1,0:T(8,128)(2,1)} %refs_0_), channel_id=1, source_target_pairs={{0,16},{8,24},{16,0},{24,8},{1,17},{9,25},{17,1},{25,9},{2,18},{10... | collective-permute-start | bytes 786440 | tf_op jit(solution)/shard_map/ppermute | solution.py:32
  3.6 2.1 %shard_map.129 = (bf16[144,1024]{1,0:T(8,128)(2,1)}, bf16[144,1024]{1,0:T(8,128)(2,1)}, f32[256,128]{1,0:T(8,128)}) custom-call(s32[1,256]{1,0:T(1,128)} %targets.1, s32[1,256]{1,0:T(1,128)} %mask.1, bf16[256,512]{1,0:T(8,128)(2,1)} %bitcast.10, bf16[256,512]{1,0:T(8,128)(2,1)} %bitcast.12, bf16[256,512]{1,0:T(8,128)(2,1)} %bitcast.14), custom_call_target="tpu_custom_call" | custom-call | flops 1 | bytes 1 | tf_op jit(solution)/shard_map/pallas_call | solution.py:466
  5.9 2.0 %collective-permute-start = (bf16[144,1024]{1,0:T(8,128)(2,1)}, bf16[144,1024]{1,0:T(8,128)(2,1)S(1)}, u32[]{:S(2)}, u32[]{:S(2)}) collective-permute-start(bf16[144,1024]{1,0:T(8,128)(2,1)} %get-tuple-element.59), channel_id=1, source_target_pairs={{0,1},{1,0},{2,3},{3,2},{4,5},{5,4},{6,7},{7,6},{8,9},{9,8},{10,11... | collective-permute-start | bytes 884744 | tf_op jit(solution)/shard_map/ppermute | solution.py:45
  7.9 0.7 %collective-permute-start.1 = (bf16[144,1024]{1,0:T(8,128)(2,1)}, bf16[144,1024]{1,0:T(8,128)(2,1)S(1)}, u32[]{:S(2)}, u32[]{:S(2)}) collective-permute-start(bf16[144,1024]{1,0:T(8,128)(2,1)} %get-tuple-element.60), channel_id=1, source_target_pairs={{1,2},{2,1},{3,4},{4,3},{5,6},{6,5},{9,10},{10,9},{11,12},{12,11},... | collective-permute-start | bytes 884744 | tf_op jit(solution)/shard_map/ppermute | solution.py:45
  8.6 2.4 %collective-permute-done.2.refs_1_ = bf16[128,1024]{1,0:T(8,128)(2,1)S(1)} collective-permute-done((bf16[128,1024]{1,0:T(8,128)(2,1)}, bf16[128,1024]{1,0:T(8,128)(2,1)S(1)}, u32[]{:S(2)}, u32[]{:S(2)}) %collective-permute-start.2) | collective-permute-done | bytes 262176 | tf_op jit(solution)/shard_map/ppermute | solution.py:32
  11.0 0.9 %copy-done = bf16[1,256,512]{2,1,0:T(8,128)(2,1)S(1)} copy-done((bf16[1,256,512]{2,1,0:T(8,128)(2,1)S(1)}, bf16[1,256,512]{2,1,0:T(8,128)(2,1)}, u32[]{:S(2)}) %copy-start) | copy-done | bytes 262168
  12.0 0.9 %copy-done.1 = bf16[1,256,512]{2,1,0:T(8,128)(2,1)S(1)} copy-done((bf16[1,256,512]{2,1,0:T(8,128)(2,1)S(1)}, bf16[1,256,512]{2,1,0:T(8,128)(2,1)}, u32[]{:S(2)}) %copy-start.1) | copy-done | bytes 262168
  12.9 0.9 %copy-done.2 = bf16[1,256,512]{2,1,0:T(8,128)(2,1)S(1)} copy-done((bf16[1,256,512]{2,1,0:T(8,128)(2,1)S(1)}, bf16[1,256,512]{2,1,0:T(8,128)(2,1)}, u32[]{:S(2)}) %copy-start.2) | copy-done | bytes 262168
  15.2 5.0 %collective-permute-done.near = bf16[144,1024]{1,0:T(8,128)(2,1)S(1)} collective-permute-done((bf16[144,1024]{1,0:T(8,128)(2,1)}, bf16[144,1024]{1,0:T(8,128)(2,1)S(1)}, u32[]{:S(2)}, u32[]{:S(2)}) %collective-permute-start) | collective-permute-done | bytes 294944 | tf_op jit(solution)/shard_map/ppermute | solution.py:45
  20.2 2.1 %shard_map.130 = (bf16[288,512]{1,0:T(8,128)(2,1)S(1)}, f32[256,128]{1,0:T(8,128)S(1)}, bf16[544,512]{1,0:T(8,128)(2,1)S(1)}, bf16[544,512]{1,0:T(8,128)(2,1)S(1...) custom-call(s32[4]{0:T(128)S(1)} %pad_add_fusion.info, bf16[256,512]{1,0:T(8,128)(2,1)S(1)} %get-tuple-element.54.q, ...), custom_call_target="tpu_custom_call" | custom-call | flops 201326592 | bytes 3219472 | tf_op jit(solution)/shard_map/pallas_call | solution.py:466
  22.5 2.2 %shard_map.131 = (f32[8,288,128]{2,1,0:T(8,128)S(1)}, bf16[512,1024]{1,0:T(8,128)(2,1)S(1)}, bf16[272,1024]{1,0:T(8,128)(2,1)S(1)}, f32[8,272,128]{2,1,0:T(8,128)S(1)}) custom-call(s32[4]{0:T(128)S(1)} %pad_add_fusion.info, bf16[288,512]{1,0:T(8,128)(2,1)S(1)} %get-tuple-element.68.attn, f32[9,1024]{1,0:T(8,128)S(1)} %copy-done.4, ...), custom_call_target="tpu_custom_call" | custom-call | flops 268435456 | bytes 5279760 | tf_op jit(solution)/shard_map/pallas_call | solution.py:466
  24.8 4.9 %shard_map.132 = (bf16[256,512]{1,0:T(8,128)(2,1)S(1)}, f32[256,128]{1,0:T(8,128)S(1)}, f32[16,1024]{1,0:T(8,128)S(1)}) custom-call(s32[4]{0:T(128)S(1)} %pad_add_fusion.info, bf16[288,512]{1,0:T(8,128)(2,1)S(1)} %get-tuple-element.68.attn, f32[256,128]{1,0:T(8,128)S(1)} %get-tuple-element.69.lse, f32[256,128]{1,0:T(8,128)S(1)} %copy-done.6, ...), custom_call_target="tpu_custom_call" | custom-call | flops 1610612736 | bytes 7057424 | tf_op jit(solution)/shard_map/pallas_call | solution.py:466
  29.7 2.4 %collective-permute-start.8 = (bf16[12,1024]{1,0:T(8,128)(2,1)S(1)}, bf16[12,1024]{1,0:T(8,128)(2,1)S(1)}, u32[]{:S(2)}, u32[]{:S(2)}) collective-permute-start(bf16[12,1024]{1,0:T(8,128)(2,1)S(1)} %get-tuple-element.110), channel_id=1, source_target_pairs={{0,1},{1,0},{2,3},{3,2},{4,5},{5,4},{6,7},{7,6},{8,9},{9,8},{10,11... | collective-permute-start | bytes 73736 | tf_op jit(solution)/shard_map/ppermute | solution.py:32
  32.2 1.2 %shard_map.133 = (bf16[128,1024]{1,0:T(8,128)(2,1)S(1)}, bf16[128,1024]{1,0:T(8,128)(2,1)S(1)}) custom-call(s32[4]{0:T(128)S(1)} %pad_add_fusion.info, bf16[288,512]{1,0:T(8,128)(2,1)S(1)} %get-tuple-element.63.q_ext, bf16[544,512]{1,0:T(8,128)(2,1)S(1)} %get-tuple-element.64.k_ext, bf16[544,512]{1,0:T(8,128)(2,1)S(1)} %get-tuple-element.65.v_ext, ...), custom_call_target="tpu_custom_call" | custom-call | flops 134217728 | bytes 2326544 | tf_op jit(solution)/shard_map/pallas_call | solution.py:466
  33.4 0.8 %collective-permute-done.8 = bf16[12,1024]{1,0:T(8,128)(2,1)S(1)} collective-permute-done((bf16[12,1024]{1,0:T(8,128)(2,1)S(1)}, bf16[12,1024]{1,0:T(8,128)(2,1)S(1)}, u32[]{:S(2)}, u32[]{:S(2)}) %collective-permute-start.8) | collective-permute-done | bytes 24608 | tf_op jit(solution)/shard_map/ppermute | solution.py:32
  34.4 1.1 %collective-permute-start.11 = (bf16[12,1024]{1,0:T(8,128)(2,1)S(1)}, bf16[12,1024]{1,0:T(8,128)(2,1)S(1)}, u32[]{:S(2)}, u32[]{:S(2)}) collective-permute-start(bf16[12,1024]{1,0:T(8,128)(2,1)S(1)} %get-tuple-element.106), channel_id=1, source_target_pairs={{0,24},{8,16},{16,8},{24,0},{1,25},{9,17},{17,9},{25,1},{2,26},{10... | collective-permute-start | bytes 73736 | tf_op jit(solution)/shard_map/ppermute | solution.py:32
  36.3 1.9 %collective-permute-start.15 = (bf16[128,1024]{1,0:T(8,128)(2,1)S(1)}, bf16[128,1024]{1,0:T(8,128)(2,1)S(1)}, u32[]{:S(2)}, u32[]{:S(2)}) collective-permute-start(bf16[128,1024]{1,0:T(8,128)(2,1)S(1)} %get-tuple-element.93), channel_id=1, source_target_pairs={{0,1},{1,0},{2,3},{3,2},{4,5},{5,4},{6,7},{7,6},{8,9},{9,8},{10,11... | collective-permute-start | bytes 786440 | tf_op jit(solution)/shard_map/ppermute | solution.py:45
  39.6 2.6 %collective-permute-start.12 = (bf16[12,1024]{1,0:T(8,128)(2,1)S(1)}, bf16[12,1024]{1,0:T(8,128)(2,1)S(1)}, u32[]{:S(2)}, u32[]{:S(2)}) collective-permute-start(bf16[12,1024]{1,0:T(8,128)(2,1)S(1)} %pad_maximum_fusion.2.refs_0_), channel_id=1, source_target_pairs={{0,2},{1,3},{2,0},{3,1},{4,6},{5,7},{6,4},{7,5},{8,10},{9,11},{10,... | collective-permute-start | bytes 73736 | tf_op jit(solution)/shard_map/ppermute | solution.py:32
  42.2 3.0 %collective-permute-start.13 = (bf16[12,1024]{1,0:T(8,128)(2,1)S(1)}, bf16[12,1024]{1,0:T(8,128)(2,1)S(1)}, u32[]{:S(2)}, u32[]{:S(2)}) collective-permute-start(bf16[12,1024]{1,0:T(8,128)(2,1)S(1)} %pad_maximum_fusion.2.refs_0_), channel_id=1, source_target_pairs={{0,4},{1,5},{2,6},{3,7},{4,0},{5,1},{6,2},{7,3},{8,12},{9,13},{10,... | collective-permute-start | bytes 73736 | tf_op jit(solution)/shard_map/ppermute | solution.py:32
  45.1 2.6 %shard_map.134 = (bf16[256,512]{1,0:T(8,128)(2,1)}, f32[256,512]{1,0:T(8,128)S(1)}, f32[256,512]{1,0:T(8,128)S(1)}) custom-call(s32[4]{0:T(128)S(1)} %pad_add_fusion.info, bf16[288,512]{1,0:T(8,128)(2,1)S(1)} %get-tuple-element.63.q_ext, bf16[544,512]{1,0:T(8,128)(2,1)S(1)} %get-tuple-element.64.k_ext, bf16[544,512]{1,0:T(8,128)(2,1)S(1)} %get-tuple-element.65.v_ext, ...), custom_call_target="tpu_custom_call" | custom-call | flops 1 | bytes 1 | tf_op jit(solution)/shard_map/pallas_call | solution.py:466
  47.8 1.5 %collective-permute-done.12.refs_1_ = bf16[12,1024]{1,0:T(8,128)(2,1)S(1)} collective-permute-done((bf16[12,1024]{1,0:T(8,128)(2,1)S(1)}, bf16[12,1024]{1,0:T(8,128)(2,1)S(1)}, u32[]{:S(2)}, u32[]{:S(2)}) %collective-permute-start.12) | collective-permute-done | bytes 24608 | tf_op jit(solution)/shard_map/ppermute | solution.py:32
  49.3 1.4 %collective-permute-done.13.refs_2_ = bf16[12,1024]{1,0:T(8,128)(2,1)S(1)} collective-permute-done((bf16[12,1024]{1,0:T(8,128)(2,1)S(1)}, bf16[12,1024]{1,0:T(8,128)(2,1)S(1)}, u32[]{:S(2)}, u32[]{:S(2)}) %collective-permute-start.13) | collective-permute-done | bytes 24608 | tf_op jit(solution)/shard_map/ppermute | solution.py:32
  50.7 1.8 %collective-permute-done.14.refs_3_ = bf16[12,1024]{1,0:T(8,128)(2,1)S(1)} collective-permute-done((bf16[12,1024]{1,0:T(8,128)(2,1)S(1)}, bf16[12,1024]{1,0:T(8,128)(2,1)S(1)}, u32[]{:S(2)}, u32[]{:S(2)}) %collective-permute-start.14) | collective-permute-done | bytes 24608 | tf_op jit(solution)/shard_map/ppermute | solution.py:32
  52.4 1.4 %shard_map.135 = (bf16[256,512]{1,0:T(8,128)(2,1)}, bf16[256,512]{1,0:T(8,128)(2,1)}, f32[9,1024]{1,0:T(8,128)}, f32[1,1]{1,0:T(1,128)}) custom-call(s32[4]{0:T(128)S(1)} %pad_add_fusion.info, f32[256,512]{1,0:T(8,128)S(1)} %get-tuple-element.91.k_part, f32[256,512]{1,0:T(8,128)S(1)} %get-tuple-element.92.v_part, ...), custom_call_target="tpu_custom_call" | custom-call | flops 131072 | bytes 2232340 | tf_op jit(solution)/shard_map/pallas_call | solution.py:466
  (62 shorter events, 3.3 us)
Async XLA Ops:
  0.6 14.1 %copy-start.3 = (bf16[256,1024]{1,0:T(8,128)(2,1)S(1)}, bf16[256,1024]{1,0:T(8,128)(2,1)}, u32[]{:S(2)}) copy-start(bf16[256,1024]{1,0:T(8,128)(2,1)} %refs_0_.1) | copy-start | bytes 1572868
  0.6 10.4 %collective-permute-start.2 = (bf16[128,1024]{1,0:T(8,128)(2,1)}, bf16[128,1024]{1,0:T(8,128)(2,1)S(1)}, u32[]{:S(2)}, u32[]{:S(2)}) collective-permute-start(bf16[128,1024]{1,0:T(8,128)(2,1)} %refs_0_), channel_id=1, source_target_pairs={{0,16},{8,24},{16,0},{24,8},{1,17},{9,25},{17,1},{25,9},{2,18},{10... | collective-permute-start | bytes 786440 | tf_op jit(solution)/shard_map/ppermute | solution.py:32
  3.6 18.8 %copy-start.4 = (f32[9,1024]{1,0:T(8,128)S(1)}, f32[9,1024]{1,0:T(8,128)}, u32[]{:S(2)}) copy-start(f32[9,1024]{1,0:T(8,128)} %taps.3) | copy-start | bytes 110596
  5.8 16.6 %collective-permute-start.5 = (bf16[256,1024]{1,0:T(8,128)(2,1)}, bf16[256,1024]{1,0:T(8,128)(2,1)S(1)}, u32[]{:S(2)}, u32[]{:S(2)}) collective-permute-start(bf16[256,1024]{1,0:T(8,128)(2,1)} %refs_0_.1), channel_id=1, source_target_pairs={{0,16},{8,24},{16,0},{24,8},{1,17},{9,25},{17,1},{25,9},{2,18},{10... | collective-permute-start | bytes 1572872 | tf_op jit(solution)/shard_map/ppermute | solution.py:32
  5.9 14.3 %collective-permute-start = (bf16[144,1024]{1,0:T(8,128)(2,1)}, bf16[144,1024]{1,0:T(8,128)(2,1)S(1)}, u32[]{:S(2)}, u32[]{:S(2)}) collective-permute-start(bf16[144,1024]{1,0:T(8,128)(2,1)} %get-tuple-element.59), channel_id=1, source_target_pairs={{0,1},{1,0},{2,3},{3,2},{4,5},{5,4},{6,7},{7,6},{8,9},{9,8},{10,11... | collective-permute-start | bytes 884744 | tf_op jit(solution)/shard_map/ppermute | solution.py:45
  7.9 12.3 %collective-permute-start.1 = (bf16[144,1024]{1,0:T(8,128)(2,1)}, bf16[144,1024]{1,0:T(8,128)(2,1)S(1)}, u32[]{:S(2)}, u32[]{:S(2)}) collective-permute-start(bf16[144,1024]{1,0:T(8,128)(2,1)} %get-tuple-element.60), channel_id=1, source_target_pairs={{1,2},{2,1},{3,4},{4,3},{5,6},{6,5},{9,10},{10,9},{11,12},{12,11},... | collective-permute-start | bytes 884744 | tf_op jit(solution)/shard_map/ppermute | solution.py:45
  8.6 6.1 %collective-permute-start.3 = (bf16[128,1024]{1,0:T(8,128)(2,1)}, bf16[128,1024]{1,0:T(8,128)(2,1)S(1)}, u32[]{:S(2)}, u32[]{:S(2)}) collective-permute-start(bf16[128,1024]{1,0:T(8,128)(2,1)} %refs_0_), channel_id=1, source_target_pairs={{0,8},{8,0},{16,24},{24,16},{1,9},{9,1},{17,25},{25,17},{2,10},{10... | collective-permute-start | bytes 786440 | tf_op jit(solution)/shard_map/ppermute | solution.py:32
  11.0 9.2 %collective-permute-start.4 = (bf16[128,1024]{1,0:T(8,128)(2,1)S(1)}, bf16[128,1024]{1,0:T(8,128)(2,1)S(1)}, u32[]{:S(2)}, u32[]{:S(2)}) collective-permute-start(bf16[128,1024]{1,0:T(8,128)(2,1)S(1)} %collective-permute-done.2.refs_1_), channel_id=1, source_target_pairs={{0,8},{8,0},{16,24},{24,16},{1,9},{9,1},{17,25},{25,17},{2,10},{10... | collective-permute-start | bytes 786440 | tf_op jit(solution)/shard_map/ppermute | solution.py:32
  11.0 1.0 %copy-start = (bf16[1,256,512]{2,1,0:T(8,128)(2,1)S(1)}, bf16[1,256,512]{2,1,0:T(8,128)(2,1)}, u32[]{:S(2)}) copy-start(bf16[1,256,512]{2,1,0:T(8,128)(2,1)} %param.9) | copy-start | bytes 786436
  11.9 0.9 %copy-start.1 = (bf16[1,256,512]{2,1,0:T(8,128)(2,1)S(1)}, bf16[1,256,512]{2,1,0:T(8,128)(2,1)}, u32[]{:S(2)}) copy-start(bf16[1,256,512]{2,1,0:T(8,128)(2,1)} %param.10) | copy-start | bytes 786436
  12.9 0.9 %copy-start.2 = (bf16[1,256,512]{2,1,0:T(8,128)(2,1)S(1)}, bf16[1,256,512]{2,1,0:T(8,128)(2,1)}, u32[]{:S(2)}) copy-start(bf16[1,256,512]{2,1,0:T(8,128)(2,1)} %param.11) | copy-start | bytes 786436
  13.9 8.6 %copy-start.5 = (bf16[128,1024]{1,0:T(8,128)(2,1)S(1)}, bf16[128,1024]{1,0:T(8,128)(2,1)}, u32[]{:S(2)}) copy-start(bf16[128,1024]{1,0:T(8,128)(2,1)} %refs_0_) | copy-start | bytes 786436
  14.7 10.1 %collective-permute-start.6 = (bf16[256,1024]{1,0:T(8,128)(2,1)S(1)}, bf16[256,1024]{1,0:T(8,128)(2,1)S(1)}, u32[]{:S(2)}, u32[]{:S(2)}) collective-permute-start(bf16[256,1024]{1,0:T(8,128)(2,1)S(1)} %copy-done.3), channel_id=1, source_target_pairs={{0,8},{8,0},{16,24},{24,16},{1,9},{9,1},{17,25},{25,17},{2,10},{10... | collective-permute-start | bytes 1572872 | tf_op jit(solution)/shard_map/ppermute | solution.py:32
  20.2 4.5 %copy-start.6 = (f32[256,128]{1,0:T(8,128)S(1)}, f32[256,128]{1,0:T(8,128)}, u32[]{:S(2)}) copy-start(f32[256,128]{1,0:T(8,128)} %get-tuple-element.70.meta) | copy-start | bytes 393220
  22.4 2.4 %collective-permute-start.7 = (bf16[256,1024]{1,0:T(8,128)(2,1)S(1)}, bf16[256,1024]{1,0:T(8,128)(2,1)S(1)}, u32[]{:S(2)}, u32[]{:S(2)}) collective-permute-start(bf16[256,1024]{1,0:T(8,128)(2,1)S(1)} %collective-permute-done.5.refs_2_), channel_id=1, source_target_pairs={{0,8},{8,0},{16,24},{24,16},{1,9},{9,1},{17,25},{25,17},{2,10},{10... | collective-permute-start | bytes 1572872 | tf_op jit(solution)/shard_map/ppermute | solution.py:32
  29.7 4.5 %collective-permute-start.8 = (bf16[12,1024]{1,0:T(8,128)(2,1)S(1)}, bf16[12,1024]{1,0:T(8,128)(2,1)S(1)}, u32[]{:S(2)}, u32[]{:S(2)}) collective-permute-start(bf16[12,1024]{1,0:T(8,128)(2,1)S(1)} %get-tuple-element.110), channel_id=1, source_target_pairs={{0,1},{1,0},{2,3},{3,2},{4,5},{5,4},{6,7},{7,6},{8,9},{9,8},{10,11... | collective-permute-start | bytes 73736 | tf_op jit(solution)/shard_map/ppermute | solution.py:32
  34.4 4.6 %collective-permute-start.11 = (bf16[12,1024]{1,0:T(8,128)(2,1)S(1)}, bf16[12,1024]{1,0:T(8,128)(2,1)S(1)}, u32[]{:S(2)}, u32[]{:S(2)}) collective-permute-start(bf16[12,1024]{1,0:T(8,128)(2,1)S(1)} %get-tuple-element.106), channel_id=1, source_target_pairs={{0,24},{8,16},{16,8},{24,0},{1,25},{9,17},{17,9},{25,1},{2,26},{10... | collective-permute-start | bytes 73736 | tf_op jit(solution)/shard_map/ppermute | solution.py:32
  35.4 3.9 %collective-permute-start.10 = (bf16[12,1024]{1,0:T(8,128)(2,1)S(1)}, bf16[12,1024]{1,0:T(8,128)(2,1)S(1)}, u32[]{:S(2)}, u32[]{:S(2)}) collective-permute-start(bf16[12,1024]{1,0:T(8,128)(2,1)S(1)} %get-tuple-element.106), channel_id=1, source_target_pairs={{0,16},{8,24},{16,0},{24,8},{1,17},{9,25},{17,1},{25,9},{2,18},{10... | collective-permute-start | bytes 73736 | tf_op jit(solution)/shard_map/ppermute | solution.py:32
  36.0 3.4 %collective-permute-start.9 = (bf16[12,1024]{1,0:T(8,128)(2,1)S(1)}, bf16[12,1024]{1,0:T(8,128)(2,1)S(1)}, u32[]{:S(2)}, u32[]{:S(2)}) collective-permute-start(bf16[12,1024]{1,0:T(8,128)(2,1)S(1)} %get-tuple-element.106), channel_id=1, source_target_pairs={{0,8},{8,0},{16,24},{24,16},{1,9},{9,1},{17,25},{25,17},{2,10},{10... | collective-permute-start | bytes 73736 | tf_op jit(solution)/shard_map/ppermute | solution.py:32
  36.3 16.1 %collective-permute-start.15 = (bf16[128,1024]{1,0:T(8,128)(2,1)S(1)}, bf16[128,1024]{1,0:T(8,128)(2,1)S(1)}, u32[]{:S(2)}, u32[]{:S(2)}) collective-permute-start(bf16[128,1024]{1,0:T(8,128)(2,1)S(1)} %get-tuple-element.93), channel_id=1, source_target_pairs={{0,1},{1,0},{2,3},{3,2},{4,5},{5,4},{6,7},{7,6},{8,9},{9,8},{10,11... | collective-permute-start | bytes 786440 | tf_op jit(solution)/shard_map/ppermute | solution.py:45
  38.3 14.2 %collective-permute-start.16 = (bf16[128,1024]{1,0:T(8,128)(2,1)S(1)}, bf16[128,1024]{1,0:T(8,128)(2,1)S(1)}, u32[]{:S(2)}, u32[]{:S(2)}) collective-permute-start(bf16[128,1024]{1,0:T(8,128)(2,1)S(1)} %get-tuple-element.94), channel_id=1, source_target_pairs={{1,2},{2,1},{3,4},{4,3},{5,6},{6,5},{9,10},{10,9},{11,12},{12,11},... | collective-permute-start | bytes 786440 | tf_op jit(solution)/shard_map/ppermute | solution.py:45
  39.6 9.6 %collective-permute-start.12 = (bf16[12,1024]{1,0:T(8,128)(2,1)S(1)}, bf16[12,1024]{1,0:T(8,128)(2,1)S(1)}, u32[]{:S(2)}, u32[]{:S(2)}) collective-permute-start(bf16[12,1024]{1,0:T(8,128)(2,1)S(1)} %pad_maximum_fusion.2.refs_0_), channel_id=1, source_target_pairs={{0,2},{1,3},{2,0},{3,1},{4,6},{5,7},{6,4},{7,5},{8,10},{9,11},{10,... | collective-permute-start | bytes 73736 | tf_op jit(solution)/shard_map/ppermute | solution.py:32
  42.2 8.5 %collective-permute-start.13 = (bf16[12,1024]{1,0:T(8,128)(2,1)S(1)}, bf16[12,1024]{1,0:T(8,128)(2,1)S(1)}, u32[]{:S(2)}, u32[]{:S(2)}) collective-permute-start(bf16[12,1024]{1,0:T(8,128)(2,1)S(1)} %pad_maximum_fusion.2.refs_0_), channel_id=1, source_target_pairs={{0,4},{1,5},{2,6},{3,7},{4,0},{5,1},{6,2},{7,3},{8,12},{9,13},{10,... | collective-permute-start | bytes 73736 | tf_op jit(solution)/shard_map/ppermute | solution.py:32
  45.1 7.3 %collective-permute-start.14 = (bf16[12,1024]{1,0:T(8,128)(2,1)S(1)}, bf16[12,1024]{1,0:T(8,128)(2,1)S(1)}, u32[]{:S(2)}, u32[]{:S(2)}) collective-permute-start(bf16[12,1024]{1,0:T(8,128)(2,1)S(1)} %pad_maximum_fusion.2.refs_0_), channel_id=1, source_target_pairs={{0,6},{1,7},{2,4},{3,5},{4,2},{5,3},{6,0},{7,1},{8,14},{9,15},{10,... | collective-permute-start | bytes 73736 | tf_op jit(solution)/shard_map/ppermute | solution.py:32

commit v5 on v4

--- a/solution.py
+++ b/solution.py
@@ -592,11 +592,9 @@
         sent = packed(totals)
         got = [swapped(sent, axis, bit) for bit in group]
         if index == 0:
-            near_part, far_part, d_attn, *got = lax.optimization_barrier(
-                (near_part, far_part, d_attn, *got)
-            )
             near_got, far_got = exchanged(near_part, far_part, "ctx")
-        if index == len(steps) - 1:
+            _, _, d_attn, *got = lax.optimization_barrier((near_part, far_part, d_attn, *got))
+        if index == 1:
             d_q, k_part, v_part = call(
                 own_grads_kernel,
                 (info, q_ext, k_ext, v_ext, stats, d_attn),

time: 54.2 us -> 54.4 us (level)
    ppermute x4, starting transfers between devices: 5.28 us -> 3.42 us  [exchanged(): return (lax.ppermute(near, axis, pairs), lax.ppermute(far, axis, others))]
    ppermute x13, starting transfers between devices: 13.7 us -> 15.3 us  [swapped(): return lax.ppermute(value, axis, [(i, i ^ bit) for i in range(size)])]
    ppermute x13, waiting for transfers between devices: 8.16 us -> 8.73 us  [swapped(): return lax.ppermute(value, axis, [(i, i ^ bit) for i in range(size)])]
  transfers between devices with their start and end apart: 17 -> 17, of which waited for: 7 -> 5; matrix products, arithmetic and copies ran while one was open for 1% -> 1% of each run, Pallas kernels for 19% -> 19%
where the time goes in v5:
time: 54.4 us; the launch traced here: 54.2 us
  starting transfers between devices  18.7 us (34%)
  Pallas kernels  16.7 us (31%)
  waiting for transfers between devices  13.7 us (25%)
  local copies, waits for them, and re-layouts  2.91 us (5%)
  between operations  1.64 us (3%)
    pallas_call x8, Pallas kernels, call(): pl.pallas_call(kernel, out_shape=outs, in_specs=[specs[place] for place i...  16.7 us
    ppermute x13, starting transfers between devices, swapped(): return lax.ppermute(value, axis, [(i, i ^ bit) for i in range(size)])  15.3 us
    ppermute x13, waiting for transfers between devices, swapped(): return lax.ppermute(value, axis, [(i, i ^ bit) for i in range(size)])  8.73 us
    ppermute x4, waiting for transfers between devices, exchanged(): return (lax.ppermute(near, axis, pairs), lax.ppermute(far, axis, others))  5 us
    ppermute x4, starting transfers between devices, exchanged(): return (lax.ppermute(near, axis, pairs), lax.ppermute(far, axis, others))  3.42 us
    unnamed x14, local copies, waits for them, and re-layouts  2.87 us
  transfers between devices with their start and end apart: 17, of which 5 were waited for; matrix products, arithmetic and copies ran while one was open for 1% of the time, Pallas kernels for 19%

profile of v5, /device:TPU:0, one launch (start us, length us, event | category | flops | bytes accessed | tf_op | source)
XLA Modules:
  0.0 54.2 jit_solution(1286462765882617000)
XLA Ops:
  0.6 3.0 %collective-permute-start.2 = (bf16[128,1024]{1,0:T(8,128)(2,1)}, bf16[128,1024]{1,0:T(8,128)(2,1)S(1)}, u32[]{:S(2)}, u32[]{:S(2)}) collective-permute-start(bf16[128,1024]{1,0:T(8,128)(2,1)} %refs_0_), channel_id=1, source_target_pairs={{0,16},{8,24},{16,0},{24,8},{1,17},{9,25},{17,1},{25,9},{2,18},{10... | collective-permute-start | bytes 786440 | tf_op jit(solution)/shard_map/ppermute | solution.py:32
  3.6 2.1 %shard_map.129 = (bf16[144,1024]{1,0:T(8,128)(2,1)}, bf16[144,1024]{1,0:T(8,128)(2,1)}, f32[256,128]{1,0:T(8,128)}) custom-call(s32[1,256]{1,0:T(1,128)} %targets.1, s32[1,256]{1,0:T(1,128)} %mask.1, bf16[256,512]{1,0:T(8,128)(2,1)} %bitcast.10, bf16[256,512]{1,0:T(8,128)(2,1)} %bitcast.12, bf16[256,512]{1,0:T(8,128)(2,1)} %bitcast.14), custom_call_target="tpu_custom_call" | custom-call | flops 1 | bytes 1 | tf_op jit(solution)/shard_map/pallas_call | solution.py:466
  5.9 2.0 %collective-permute-start = (bf16[144,1024]{1,0:T(8,128)(2,1)}, bf16[144,1024]{1,0:T(8,128)(2,1)S(1)}, u32[]{:S(2)}, u32[]{:S(2)}) collective-permute-start(bf16[144,1024]{1,0:T(8,128)(2,1)} %get-tuple-element.57), channel_id=1, source_target_pairs={{0,1},{1,0},{2,3},{3,2},{4,5},{5,4},{6,7},{7,6},{8,9},{9,8},{10,11... | collective-permute-start | bytes 884744 | tf_op jit(solution)/shard_map/ppermute | solution.py:45
  7.9 0.7 %collective-permute-start.1 = (bf16[144,1024]{1,0:T(8,128)(2,1)}, bf16[144,1024]{1,0:T(8,128)(2,1)S(1)}, u32[]{:S(2)}, u32[]{:S(2)}) collective-permute-start(bf16[144,1024]{1,0:T(8,128)(2,1)} %get-tuple-element.58), channel_id=1, source_target_pairs={{1,2},{2,1},{3,4},{4,3},{5,6},{6,5},{9,10},{10,9},{11,12},{12,11},... | collective-permute-start | bytes 884744 | tf_op jit(solution)/shard_map/ppermute | solution.py:45
  8.6 2.4 %collective-permute-done.2.refs_1_ = bf16[128,1024]{1,0:T(8,128)(2,1)S(1)} collective-permute-done((bf16[128,1024]{1,0:T(8,128)(2,1)}, bf16[128,1024]{1,0:T(8,128)(2,1)S(1)}, u32[]{:S(2)}, u32[]{:S(2)}) %collective-permute-start.2) | collective-permute-done | bytes 262176 | tf_op jit(solution)/shard_map/ppermute | solution.py:32
  11.0 0.9 %copy-done = bf16[1,256,512]{2,1,0:T(8,128)(2,1)S(1)} copy-done((bf16[1,256,512]{2,1,0:T(8,128)(2,1)S(1)}, bf16[1,256,512]{2,1,0:T(8,128)(2,1)}, u32[]{:S(2)}) %copy-start) | copy-done | bytes 262168
  12.0 0.9 %copy-done.1 = bf16[1,256,512]{2,1,0:T(8,128)(2,1)S(1)} copy-done((bf16[1,256,512]{2,1,0:T(8,128)(2,1)S(1)}, bf16[1,256,512]{2,1,0:T(8,128)(2,1)}, u32[]{:S(2)}) %copy-start.1) | copy-done | bytes 262168
  12.9 0.9 %copy-done.2 = bf16[1,256,512]{2,1,0:T(8,128)(2,1)S(1)} copy-done((bf16[1,256,512]{2,1,0:T(8,128)(2,1)S(1)}, bf16[1,256,512]{2,1,0:T(8,128)(2,1)}, u32[]{:S(2)}) %copy-start.2) | copy-done | bytes 262168
  14.7 0.6 %collective-permute-start.6 = (bf16[256,1024]{1,0:T(8,128)(2,1)S(1)}, bf16[256,1024]{1,0:T(8,128)(2,1)S(1)}, u32[]{:S(2)}, u32[]{:S(2)}) collective-permute-start(bf16[256,1024]{1,0:T(8,128)(2,1)S(1)} %copy-done.3), channel_id=1, source_target_pairs={{0,8},{8,0},{16,24},{24,16},{1,9},{9,1},{17,25},{25,17},{2,10},{10... | collective-permute-start | bytes 1572872 | tf_op jit(solution)/shard_map/ppermute | solution.py:32
  15.2 5.0 %collective-permute-done.near = bf16[144,1024]{1,0:T(8,128)(2,1)S(1)} collective-permute-done((bf16[144,1024]{1,0:T(8,128)(2,1)}, bf16[144,1024]{1,0:T(8,128)(2,1)S(1)}, u32[]{:S(2)}, u32[]{:S(2)}) %collective-permute-start) | collective-permute-done | bytes 294944 | tf_op jit(solution)/shard_map/ppermute | solution.py:45
  20.2 2.1 %shard_map.130 = (bf16[288,512]{1,0:T(8,128)(2,1)S(1)}, f32[256,128]{1,0:T(8,128)S(1)}, bf16[544,512]{1,0:T(8,128)(2,1)S(1)}, bf16[544,512]{1,0:T(8,128)(2,1)S(1...) custom-call(s32[4]{0:T(128)S(1)} %pad_add_fusion.info, bf16[256,512]{1,0:T(8,128)(2,1)S(1)} %get-tuple-element.52.q, ...), custom_call_target="tpu_custom_call" | custom-call | flops 201326592 | bytes 3219472 | tf_op jit(solution)/shard_map/pallas_call | solution.py:466
  22.5 2.2 %shard_map.131 = (f32[8,288,128]{2,1,0:T(8,128)S(1)}, bf16[512,1024]{1,0:T(8,128)(2,1)S(1)}, bf16[272,1024]{1,0:T(8,128)(2,1)S(1)}, f32[8,272,128]{2,1,0:T(8,128)S(1)}) custom-call(s32[4]{0:T(128)S(1)} %pad_add_fusion.info, bf16[288,512]{1,0:T(8,128)(2,1)S(1)} %get-tuple-element.66.attn, f32[9,1024]{1,0:T(8,128)S(1)} %copy-done.4, ...), custom_call_target="tpu_custom_call" | custom-call | flops 268435456 | bytes 5279760 | tf_op jit(solution)/shard_map/pallas_call | solution.py:466
  24.8 4.9 %shard_map.132 = (bf16[256,512]{1,0:T(8,128)(2,1)S(1)}, f32[256,128]{1,0:T(8,128)S(1)}, f32[16,1024]{1,0:T(8,128)S(1)}) custom-call(s32[4]{0:T(128)S(1)} %pad_add_fusion.info, bf16[288,512]{1,0:T(8,128)(2,1)S(1)} %get-tuple-element.66.attn, f32[256,128]{1,0:T(8,128)S(1)} %get-tuple-element.67.lse, f32[256,128]{1,0:T(8,128)S(1)} %copy-done.6, ...), custom_call_target="tpu_custom_call" | custom-call | flops 1610612736 | bytes 7057424 | tf_op jit(solution)/shard_map/pallas_call | solution.py:466
  29.7 2.4 %collective-permute-start.8 = (bf16[12,1024]{1,0:T(8,128)(2,1)S(1)}, bf16[12,1024]{1,0:T(8,128)(2,1)S(1)}, u32[]{:S(2)}, u32[]{:S(2)}) collective-permute-start(bf16[12,1024]{1,0:T(8,128)(2,1)S(1)} %get-tuple-element.106), channel_id=1, source_target_pairs={{0,1},{1,0},{2,3},{3,2},{4,5},{5,4},{6,7},{7,6},{8,9},{9,8},{10,11... | collective-permute-start | bytes 73736 | tf_op jit(solution)/shard_map/ppermute | solution.py:32
  32.2 1.2 %shard_map.133 = (bf16[128,1024]{1,0:T(8,128)(2,1)S(1)}, bf16[128,1024]{1,0:T(8,128)(2,1)S(1)}) custom-call(s32[4]{0:T(128)S(1)} %pad_add_fusion.info, bf16[288,512]{1,0:T(8,128)(2,1)S(1)} %get-tuple-element.61.q_ext, bf16[544,512]{1,0:T(8,128)(2,1)S(1)} %get-tuple-element.62.k_ext, bf16[544,512]{1,0:T(8,128)(2,1)S(1)} %get-tuple-element.63.v_ext, ...), custom_call_target="tpu_custom_call" | custom-call | flops 134217728 | bytes 2326544 | tf_op jit(solution)/shard_map/pallas_call | solution.py:466
  33.5 0.7 %collective-permute-start.13 = (bf16[128,1024]{1,0:T(8,128)(2,1)S(1)}, bf16[128,1024]{1,0:T(8,128)(2,1)S(1)}, u32[]{:S(2)}, u32[]{:S(2)}) collective-permute-start(bf16[128,1024]{1,0:T(8,128)(2,1)S(1)} %get-tuple-element.82), channel_id=1, source_target_pairs={{1,2},{2,1},{3,4},{4,3},{5,6},{6,5},{9,10},{10,9},{11,12},{12,11},... | collective-permute-start | bytes 786440 | tf_op jit(solution)/shard_map/ppermute | solution.py:45
  34.6 1.5 %collective-permute-start.10 = (bf16[12,1024]{1,0:T(8,128)(2,1)S(1)}, bf16[12,1024]{1,0:T(8,128)(2,1)S(1)}, u32[]{:S(2)}, u32[]{:S(2)}) collective-permute-start(bf16[12,1024]{1,0:T(8,128)(2,1)S(1)} %get-tuple-element.102), channel_id=1, source_target_pairs={{0,16},{8,24},{16,0},{24,8},{1,17},{9,25},{17,1},{25,9},{2,18},{10... | collective-permute-start | bytes 73736 | tf_op jit(solution)/shard_map/ppermute | solution.py:32
  36.3 2.6 %shard_map.134 = (bf16[256,512]{1,0:T(8,128)(2,1)}, f32[256,512]{1,0:T(8,128)S(1)}, f32[256,512]{1,0:T(8,128)S(1)}) custom-call(s32[4]{0:T(128)S(1)} %pad_add_fusion.info, bf16[288,512]{1,0:T(8,128)(2,1)S(1)} %get-tuple-element.61.q_ext, bf16[544,512]{1,0:T(8,128)(2,1)S(1)} %get-tuple-element.62.k_ext, bf16[544,512]{1,0:T(8,128)(2,1)S(1)} %get-tuple-element.63.v_ext, ...), custom_call_target="tpu_custom_call" | custom-call | flops 1 | bytes 1 | tf_op jit(solution)/shard_map/pallas_call | solution.py:466
  39.0 0.6 %collective-permute-done.11 = bf16[12,1024]{1,0:T(8,128)(2,1)S(1)} collective-permute-done((bf16[12,1024]{1,0:T(8,128)(2,1)S(1)}, bf16[12,1024]{1,0:T(8,128)(2,1)S(1)}, u32[]{:S(2)}, u32[]{:S(2)}) %collective-permute-start.11) | collective-permute-done | bytes 24608 | tf_op jit(solution)/shard_map/ppermute | solution.py:32
  39.9 4.5 %collective-permute-start.14 = (bf16[12,1024]{1,0:T(8,128)(2,1)S(1)}, bf16[12,1024]{1,0:T(8,128)(2,1)S(1)}, u32[]{:S(2)}, u32[]{:S(2)}) collective-permute-start(bf16[12,1024]{1,0:T(8,128)(2,1)S(1)} %pad_maximum_fusion.2.refs_0_), channel_id=1, source_target_pairs={{0,2},{1,3},{2,0},{3,1},{4,6},{5,7},{6,4},{7,5},{8,10},{9,11},{10,... | collective-permute-start | bytes 73736 | tf_op jit(solution)/shard_map/ppermute | solution.py:32
  44.4 2.6 %collective-permute-start.15 = (bf16[12,1024]{1,0:T(8,128)(2,1)S(1)}, bf16[12,1024]{1,0:T(8,128)(2,1)S(1)}, u32[]{:S(2)}, u32[]{:S(2)}) collective-permute-start(bf16[12,1024]{1,0:T(8,128)(2,1)S(1)} %pad_maximum_fusion.2.refs_0_), channel_id=1, source_target_pairs={{0,4},{1,5},{2,6},{3,7},{4,0},{5,1},{6,2},{7,3},{8,12},{9,13},{10,... | collective-permute-start | bytes 73736 | tf_op jit(solution)/shard_map/ppermute | solution.py:32
  47.0 2.8 %collective-permute-done.15.refs_2_ = bf16[12,1024]{1,0:T(8,128)(2,1)S(1)} collective-permute-done((bf16[12,1024]{1,0:T(8,128)(2,1)S(1)}, bf16[12,1024]{1,0:T(8,128)(2,1)S(1)}, u32[]{:S(2)}, u32[]{:S(2)}) %collective-permute-start.15) | collective-permute-done | bytes 24608 | tf_op jit(solution)/shard_map/ppermute | solution.py:32
  49.8 2.9 %collective-permute-done.16.refs_3_ = bf16[12,1024]{1,0:T(8,128)(2,1)S(1)} collective-permute-done((bf16[12,1024]{1,0:T(8,128)(2,1)S(1)}, bf16[12,1024]{1,0:T(8,128)(2,1)S(1)}, u32[]{:S(2)}, u32[]{:S(2)}) %collective-permute-start.16) | collective-permute-done | bytes 24608 | tf_op jit(solution)/shard_map/ppermute | solution.py:32
  52.7 1.4 %shard_map.135 = (bf16[256,512]{1,0:T(8,128)(2,1)}, bf16[256,512]{1,0:T(8,128)(2,1)}, f32[9,1024]{1,0:T(8,128)}, f32[1,1]{1,0:T(1,128)}) custom-call(s32[4]{0:T(128)S(1)} %pad_add_fusion.info, f32[256,512]{1,0:T(8,128)S(1)} %get-tuple-element.89.k_part, f32[256,512]{1,0:T(8,128)S(1)} %get-tuple-element.90.v_part, ...), custom_call_target="tpu_custom_call" | custom-call | flops 131072 | bytes 2232340 | tf_op jit(solution)/shard_map/pallas_call | solution.py:466
  (61 shorter events, 1.4 us)
Async XLA Ops:
  0.6 14.1 %copy-start.3 = (bf16[256,1024]{1,0:T(8,128)(2,1)S(1)}, bf16[256,1024]{1,0:T(8,128)(2,1)}, u32[]{:S(2)}) copy-start(bf16[256,1024]{1,0:T(8,128)(2,1)} %refs_0_.1) | copy-start | bytes 1572868
  0.6 10.4 %collective-permute-start.2 = (bf16[128,1024]{1,0:T(8,128)(2,1)}, bf16[128,1024]{1,0:T(8,128)(2,1)S(1)}, u32[]{:S(2)}, u32[]{:S(2)}) collective-permute-start(bf16[128,1024]{1,0:T(8,128)(2,1)} %refs_0_), channel_id=1, source_target_pairs={{0,16},{8,24},{16,0},{24,8},{1,17},{9,25},{17,1},{25,9},{2,18},{10... | collective-permute-start | bytes 786440 | tf_op jit(solution)/shard_map/ppermute | solution.py:32
  3.6 18.8 %copy-start.4 = (f32[9,1024]{1,0:T(8,128)S(1)}, f32[9,1024]{1,0:T(8,128)}, u32[]{:S(2)}) copy-start(f32[9,1024]{1,0:T(8,128)} %taps.3) | copy-start | bytes 110596
  5.8 16.6 %collective-permute-start.5 = (bf16[256,1024]{1,0:T(8,128)(2,1)}, bf16[256,1024]{1,0:T(8,128)(2,1)S(1)}, u32[]{:S(2)}, u32[]{:S(2)}) collective-permute-start(bf16[256,1024]{1,0:T(8,128)(2,1)} %refs_0_.1), channel_id=1, source_target_pairs={{0,16},{8,24},{16,0},{24,8},{1,17},{9,25},{17,1},{25,9},{2,18},{10... | collective-permute-start | bytes 1572872 | tf_op jit(solution)/shard_map/ppermute | solution.py:32
  5.9 14.3 %collective-permute-start = (bf16[144,1024]{1,0:T(8,128)(2,1)}, bf16[144,1024]{1,0:T(8,128)(2,1)S(1)}, u32[]{:S(2)}, u32[]{:S(2)}) collective-permute-start(bf16[144,1024]{1,0:T(8,128)(2,1)} %get-tuple-element.57), channel_id=1, source_target_pairs={{0,1},{1,0},{2,3},{3,2},{4,5},{5,4},{6,7},{7,6},{8,9},{9,8},{10,11... | collective-permute-start | bytes 884744 | tf_op jit(solution)/shard_map/ppermute | solution.py:45
  7.9 12.3 %collective-permute-start.1 = (bf16[144,1024]{1,0:T(8,128)(2,1)}, bf16[144,1024]{1,0:T(8,128)(2,1)S(1)}, u32[]{:S(2)}, u32[]{:S(2)}) collective-permute-start(bf16[144,1024]{1,0:T(8,128)(2,1)} %get-tuple-element.58), channel_id=1, source_target_pairs={{1,2},{2,1},{3,4},{4,3},{5,6},{6,5},{9,10},{10,9},{11,12},{12,11},... | collective-permute-start | bytes 884744 | tf_op jit(solution)/shard_map/ppermute | solution.py:45
  8.6 6.1 %collective-permute-start.3 = (bf16[128,1024]{1,0:T(8,128)(2,1)}, bf16[128,1024]{1,0:T(8,128)(2,1)S(1)}, u32[]{:S(2)}, u32[]{:S(2)}) collective-permute-start(bf16[128,1024]{1,0:T(8,128)(2,1)} %refs_0_), channel_id=1, source_target_pairs={{0,8},{8,0},{16,24},{24,16},{1,9},{9,1},{17,25},{25,17},{2,10},{10... | collective-permute-start | bytes 786440 | tf_op jit(solution)/shard_map/ppermute | solution.py:32
  11.0 9.2 %collective-permute-start.4 = (bf16[128,1024]{1,0:T(8,128)(2,1)S(1)}, bf16[128,1024]{1,0:T(8,128)(2,1)S(1)}, u32[]{:S(2)}, u32[]{:S(2)}) collective-permute-start(bf16[128,1024]{1,0:T(8,128)(2,1)S(1)} %collective-permute-done.2.refs_1_), channel_id=1, source_target_pairs={{0,8},{8,0},{16,24},{24,16},{1,9},{9,1},{17,25},{25,17},{2,10},{10... | collective-permute-start | bytes 786440 | tf_op jit(solution)/shard_map/ppermute | solution.py:32
  11.0 1.0 %copy-start = (bf16[1,256,512]{2,1,0:T(8,128)(2,1)S(1)}, bf16[1,256,512]{2,1,0:T(8,128)(2,1)}, u32[]{:S(2)}) copy-start(bf16[1,256,512]{2,1,0:T(8,128)(2,1)} %param.9) | copy-start | bytes 786436
  11.9 0.9 %copy-start.1 = (bf16[1,256,512]{2,1,0:T(8,128)(2,1)S(1)}, bf16[1,256,512]{2,1,0:T(8,128)(2,1)}, u32[]{:S(2)}) copy-start(bf16[1,256,512]{2,1,0:T(8,128)(2,1)} %param.10) | copy-start | bytes 786436
  12.9 0.9 %copy-start.2 = (bf16[1,256,512]{2,1,0:T(8,128)(2,1)S(1)}, bf16[1,256,512]{2,1,0:T(8,128)(2,1)}, u32[]{:S(2)}) copy-start(bf16[1,256,512]{2,1,0:T(8,128)(2,1)} %param.11) | copy-start | bytes 786436
  13.9 8.6 %copy-start.5 = (bf16[128,1024]{1,0:T(8,128)(2,1)S(1)}, bf16[128,1024]{1,0:T(8,128)(2,1)}, u32[]{:S(2)}) copy-start(bf16[128,1024]{1,0:T(8,128)(2,1)} %refs_0_) | copy-start | bytes 786436
  14.7 10.1 %collective-permute-start.6 = (bf16[256,1024]{1,0:T(8,128)(2,1)S(1)}, bf16[256,1024]{1,0:T(8,128)(2,1)S(1)}, u32[]{:S(2)}, u32[]{:S(2)}) collective-permute-start(bf16[256,1024]{1,0:T(8,128)(2,1)S(1)} %copy-done.3), channel_id=1, source_target_pairs={{0,8},{8,0},{16,24},{24,16},{1,9},{9,1},{17,25},{25,17},{2,10},{10... | collective-permute-start | bytes 1572872 | tf_op jit(solution)/shard_map/ppermute | solution.py:32
  20.2 4.5 %copy-start.6 = (f32[256,128]{1,0:T(8,128)S(1)}, f32[256,128]{1,0:T(8,128)}, u32[]{:S(2)}) copy-start(f32[256,128]{1,0:T(8,128)} %get-tuple-element.68.meta) | copy-start | bytes 393220
  22.4 2.4 %collective-permute-start.7 = (bf16[256,1024]{1,0:T(8,128)(2,1)S(1)}, bf16[256,1024]{1,0:T(8,128)(2,1)S(1)}, u32[]{:S(2)}, u32[]{:S(2)}) collective-permute-start(bf16[256,1024]{1,0:T(8,128)(2,1)S(1)} %collective-permute-done.5.refs_2_), channel_id=1, source_target_pairs={{0,8},{8,0},{16,24},{24,16},{1,9},{9,1},{17,25},{25,17},{2,10},{10... | collective-permute-start | bytes 1572872 | tf_op jit(solution)/shard_map/ppermute | solution.py:32
  29.7 4.5 %collective-permute-start.8 = (bf16[12,1024]{1,0:T(8,128)(2,1)S(1)}, bf16[12,1024]{1,0:T(8,128)(2,1)S(1)}, u32[]{:S(2)}, u32[]{:S(2)}) collective-permute-start(bf16[12,1024]{1,0:T(8,128)(2,1)S(1)} %get-tuple-element.106), channel_id=1, source_target_pairs={{0,1},{1,0},{2,3},{3,2},{4,5},{5,4},{6,7},{7,6},{8,9},{9,8},{10,11... | collective-permute-start | bytes 73736 | tf_op jit(solution)/shard_map/ppermute | solution.py:32
  33.4 19.3 %collective-permute-start.12 = (bf16[128,1024]{1,0:T(8,128)(2,1)S(1)}, bf16[128,1024]{1,0:T(8,128)(2,1)S(1)}, u32[]{:S(2)}, u32[]{:S(2)}) collective-permute-start(bf16[128,1024]{1,0:T(8,128)(2,1)S(1)} %get-tuple-element.81), channel_id=1, source_target_pairs={{0,1},{1,0},{2,3},{3,2},{4,5},{5,4},{6,7},{7,6},{8,9},{9,8},{10,11... | collective-permute-start | bytes 786440 | tf_op jit(solution)/shard_map/ppermute | solution.py:45
  33.5 19.2 %collective-permute-start.13 = (bf16[128,1024]{1,0:T(8,128)(2,1)S(1)}, bf16[128,1024]{1,0:T(8,128)(2,1)S(1)}, u32[]{:S(2)}, u32[]{:S(2)}) collective-permute-start(bf16[128,1024]{1,0:T(8,128)(2,1)S(1)} %get-tuple-element.82), channel_id=1, source_target_pairs={{1,2},{2,1},{3,4},{4,3},{5,6},{6,5},{9,10},{10,9},{11,12},{12,11},... | collective-permute-start | bytes 786440 | tf_op jit(solution)/shard_map/ppermute | solution.py:45
  34.4 4.6 %collective-permute-start.9 = (bf16[12,1024]{1,0:T(8,128)(2,1)S(1)}, bf16[12,1024]{1,0:T(8,128)(2,1)S(1)}, u32[]{:S(2)}, u32[]{:S(2)}) collective-permute-start(bf16[12,1024]{1,0:T(8,128)(2,1)S(1)} %get-tuple-element.102), channel_id=1, source_target_pairs={{0,8},{8,0},{16,24},{24,16},{1,9},{9,1},{17,25},{25,17},{2,10},{10... | collective-permute-start | bytes 73736 | tf_op jit(solution)/shard_map/ppermute | solution.py:32
  34.6 4.3 %collective-permute-start.10 = (bf16[12,1024]{1,0:T(8,128)(2,1)S(1)}, bf16[12,1024]{1,0:T(8,128)(2,1)S(1)}, u32[]{:S(2)}, u32[]{:S(2)}) collective-permute-start(bf16[12,1024]{1,0:T(8,128)(2,1)S(1)} %get-tuple-element.102), channel_id=1, source_target_pairs={{0,16},{8,24},{16,0},{24,8},{1,17},{9,25},{17,1},{25,9},{2,18},{10... | collective-permute-start | bytes 73736 | tf_op jit(solution)/shard_map/ppermute | solution.py:32
  36.1 3.5 %collective-permute-start.11 = (bf16[12,1024]{1,0:T(8,128)(2,1)S(1)}, bf16[12,1024]{1,0:T(8,128)(2,1)S(1)}, u32[]{:S(2)}, u32[]{:S(2)}) collective-permute-start(bf16[12,1024]{1,0:T(8,128)(2,1)S(1)} %get-tuple-element.102), channel_id=1, source_target_pairs={{0,24},{8,16},{16,8},{24,0},{1,25},{9,17},{17,9},{25,1},{2,26},{10... | collective-permute-start | bytes 73736 | tf_op jit(solution)/shard_map/ppermute | solution.py:32
  39.9 7.1 %collective-permute-start.14 = (bf16[12,1024]{1,0:T(8,128)(2,1)S(1)}, bf16[12,1024]{1,0:T(8,128)(2,1)S(1)}, u32[]{:S(2)}, u32[]{:S(2)}) collective-permute-start(bf16[12,1024]{1,0:T(8,128)(2,1)S(1)} %pad_maximum_fusion.2.refs_0_), channel_id=1, source_target_pairs={{0,2},{1,3},{2,0},{3,1},{4,6},{5,7},{6,4},{7,5},{8,10},{9,11},{10,... | collective-permute-start | bytes 73736 | tf_op jit(solution)/shard_map/ppermute | solution.py:32
  44.4 5.4 %collective-permute-start.15 = (bf16[12,1024]{1,0:T(8,128)(2,1)S(1)}, bf16[12,1024]{1,0:T(8,128)(2,1)S(1)}, u32[]{:S(2)}, u32[]{:S(2)}) collective-permute-start(bf16[12,1024]{1,0:T(8,128)(2,1)S(1)} %pad_maximum_fusion.2.refs_0_), channel_id=1, source_target_pairs={{0,4},{1,5},{2,6},{3,7},{4,0},{5,1},{6,2},{7,3},{8,12},{9,13},{10,... | collective-permute-start | bytes 73736 | tf_op jit(solution)/shard_map/ppermute | solution.py:32
  47.0 5.7 %collective-permute-start.16 = (bf16[12,1024]{1,0:T(8,128)(2,1)S(1)}, bf16[12,1024]{1,0:T(8,128)(2,1)S(1)}, u32[]{:S(2)}, u32[]{:S(2)}) collective-permute-start(bf16[12,1024]{1,0:T(8,128)(2,1)S(1)} %pad_maximum_fusion.2.refs_0_), channel_id=1, source_target_pairs={{0,6},{1,7},{2,4},{3,5},{4,2},{5,3},{6,0},{7,1},{8,14},{9,15},{10,... | collective-permute-start | bytes 73736 | tf_op jit(solution)/shard_map/ppermute | solution.py:32
